TPU v7x, 32 devices: a whole 2x2x4 slice. The times are simulated.
32 devices in a mesh: section: 4 (over z), seq: 4 (over y, core), dp: 2 (over x).
Axes of the slice: x: 2, y: 2, z: 4, core: 2. Of those that a mesh axis runs over, the one named last changes fastest.
Arguments:
- layer_input: bfloat16 [4, 2, 512, 2048], P('section', 'dp', 'seq'), may hold values from -6 to 6
- tangent_input: bfloat16 [4, 2, 512, 2048], P('section', 'dp', 'seq'), may hold values from -6 to 6
- cotangent_input: bfloat16 [4, 2, 512, 2048], P('section', 'dp', 'seq'), may hold values from -6 to 6
- saved_normed: bfloat16 [4, 2, 512, 2048], P('section', 'dp'), may hold values from -6 to 6
- saved_inv_rms: float32 [4, 2, 512], P('section', 'dp', 'seq'), may hold values from 0.5 to 2
- saved_projections: bfloat16 [4, 2, 512, 4, 384], P('section', 'dp', None, 'seq'), may hold values from -6 to 6
- time_index: int32 [4, 2, 2], P('section', 'dp'), may hold values from 0 to 999
- input_weight: bfloat16 [4, 2048, 4, 384], P('section', None, 'seq'), may hold values from -3 to 3
- output_weight: bfloat16 [4, 4, 128, 2048], P('section'), may hold values from -0.25 to 0.25
- norm_gain: float32 [4, 2048], P('section'), may hold values from 0.5 to 1.5
- time_scale: float32 [4, 2048], P('section'), may hold values from -0.3 to 0.3
Outputs:
- next_input: bfloat16 [4, 2, 512, 2048], P('section', 'dp', 'seq')
- next_tangent: bfloat16 [4, 2, 512, 2048], P('section', 'dp', 'seq')
- prev_cotangent: bfloat16 [4, 2, 512, 2048], P('section', 'dp', 'seq')
- input_weight_gradient: float32 [4, 2048, 4, 384], P('section', 'dp', 'seq')
- output_weight_gradient: float32 [4, 4, 128, 2048], P('section', 'seq', None, 'dp')
- modulation_gradient: float32 [4, 2, 2048], P('section')
Inputs may be any that keep to these rules, and one draw needn't show every extreme that they name: `time_index`: index 0 of the last dimension is the forward micro-batch's, 1 the backward micro-batch's.
All inputs are finite; a program needn't handle non-finite values.
Results may differ from a plain program's by a relative error of at most 0.014.
Values may be sent and summed in bfloat16 or wider, within the bound.
A program may use at most 128 MiB of HBM per device.

v0:
```python
import math

import jax
import jax.numpy as jnp
from jax import lax
from jax.sharding import PartitionSpec as P

TSTEPS = 1000


EPS = 1e-06


def passed_along(value, axis, steps):
    count = lax.axis_size(axis)
    pairs = [(source, (source + steps) % count) for source in range(count)]
    return lax.ppermute(value, axis, pairs)


def timesteps(indices):
    return math.pi / 2 * (indices.astype(jnp.float32) + 0.5) / TSTEPS


def attend_tangent(queries, keys, values, tan_queries, tan_keys, tan_values):
    rows = queries.shape[0]
    block_rows = min(512, rows)
    scale = 1.0 / math.sqrt(queries.shape[1])

    def one_block(inputs):
        query_block, tangent_block = inputs
        scores = (
            jnp.einsum("qd,kd->qk", query_block, keys, preferred_element_type=jnp.float32) * scale
        )
        probs = jax.nn.softmax(scores, axis=-1)
        tan_scores = (
            jnp.einsum("qd,kd->qk", tangent_block, keys, preferred_element_type=jnp.float32)
            + jnp.einsum("qd,kd->qk", query_block, tan_keys, preferred_element_type=jnp.float32)
        ) * scale
        tan_probs = probs * (tan_scores - jnp.sum(probs * tan_scores, -1, keepdims=True))
        probs_low = probs.astype(jnp.bfloat16)
        tan_low = tan_probs.astype(jnp.bfloat16)
        attended = jnp.dot(probs_low, values, preferred_element_type=jnp.float32)
        tan_attended = jnp.dot(tan_low, values, preferred_element_type=jnp.float32) + jnp.dot(
            probs_low, tan_values, preferred_element_type=jnp.float32
        )
        return (attended.astype(jnp.bfloat16), tan_attended.astype(jnp.bfloat16))

    shaped = (
        queries.reshape(rows // block_rows, block_rows, -1),
        tan_queries.reshape(rows // block_rows, block_rows, -1),
    )
    attended, tan_attended = lax.map(one_block, shaped)
    return (attended.reshape(rows, -1), tan_attended.reshape(rows, -1))


def attend_backward(queries, keys, values, grad_attended):
    rows, head_size = queries.shape
    block_rows = min(512, rows)
    scale = 1.0 / math.sqrt(head_size)

    def one_block(carry, inputs):
        grad_keys, grad_values = carry
        query_block, grad_block = inputs
        scores = (
            jnp.einsum("qd,kd->qk", query_block, keys, preferred_element_type=jnp.float32) * scale
        )
        probs = jax.nn.softmax(scores, axis=-1)
        probs_low = probs.astype(jnp.bfloat16)
        attended = jnp.dot(probs_low, values, preferred_element_type=jnp.float32).astype(
            jnp.bfloat16
        )
        grad_values = grad_values + jnp.einsum(
            "qk,qd->kd", probs_low, grad_block, preferred_element_type=jnp.float32
        )
        grad_probs = jnp.einsum("qd,kd->qk", grad_block, values, preferred_element_type=jnp.float32)
        grad_scores = probs * (grad_probs - jnp.sum(probs * grad_probs, -1, keepdims=True)) * scale
        grad_low = grad_scores.astype(jnp.bfloat16)
        grad_queries = jnp.dot(grad_low, keys, preferred_element_type=jnp.float32)
        grad_keys = grad_keys + jnp.einsum(
            "qk,qd->kd", grad_low, query_block, preferred_element_type=jnp.float32
        )
        return ((grad_keys, grad_values), (grad_queries, attended))

    zeros = jnp.zeros((rows, head_size), jnp.float32)
    shaped = (
        queries.reshape(rows // block_rows, block_rows, head_size),
        grad_attended.reshape(rows // block_rows, block_rows, head_size),
    )
    (grad_keys, grad_values), (grad_queries, attended) = lax.scan(one_block, (zeros, zeros), shaped)
    return (
        grad_queries.reshape(rows, head_size),
        grad_keys,
        grad_values,
        attended.reshape(rows, head_size),
    )


def forward_layer(input_rows, tangent_rows, weight_heads, output_flat, gains, scales, moment):
    head_size = weight_heads.shape[1] // 3
    hidden = input_rows.astype(jnp.float32)
    tangent = tangent_rows.astype(jnp.float32)
    inverse = lax.rsqrt(jnp.mean(hidden * hidden, -1, keepdims=True) + EPS)
    normal = hidden * inverse
    tan_inverse = -(inverse**3) * jnp.mean(hidden * tangent, -1, keepdims=True)
    tan_normal = tangent * inverse + hidden * tan_inverse
    modulated = gains + jnp.sin(moment) * scales
    tan_modulated = jnp.cos(moment) * scales
    normed = (normal * modulated).astype(jnp.bfloat16)
    tan_normed = (tan_normal * modulated + normal * tan_modulated).astype(jnp.bfloat16)
    stacked = jnp.stack([normed, tan_normed])
    projected = jnp.einsum(
        "srd,dc->src",
        lax.all_gather(stacked, "seq", axis=1, tiled=True),
        weight_heads,
        preferred_element_type=jnp.float32,
    ).astype(jnp.bfloat16)
    attended, tan_attended = attend_tangent(
        projected[0, :, :head_size],
        projected[0, :, head_size : 2 * head_size],
        projected[0, :, 2 * head_size :],
        projected[1, :, :head_size],
        projected[1, :, head_size : 2 * head_size],
        projected[1, :, 2 * head_size :],
    )
    moved = lax.all_to_all(
        jnp.stack([attended, tan_attended]), "seq", split_axis=1, concat_axis=2, tiled=True
    )
    result = jnp.einsum("sre,ed->srd", moved, output_flat, preferred_element_type=jnp.float32)
    outgoing = jnp.stack(
        [(hidden + result[0]).astype(jnp.bfloat16), (tangent + result[1]).astype(jnp.bfloat16)]
    )
    shifted = passed_along(outgoing, "section", 1)
    return (shifted[0], shifted[1])


def backward_layer(
    cot_rows, normed_all, inv_rows, saved_heads, weight_heads, output_head, gains, scales, moment
):
    head_size = weight_heads.shape[1] // 3
    local_rows = cot_rows.shape[0]
    queries = saved_heads[:, :head_size]
    keys = saved_heads[:, head_size : 2 * head_size]
    values = saved_heads[:, 2 * head_size :]
    cot_all = lax.all_gather(cot_rows, "seq", axis=0, tiled=True)
    grad_out = jnp.einsum(
        "td,hd->th", cot_all, output_head, preferred_element_type=jnp.float32
    ).astype(jnp.bfloat16)
    grad_q, grad_k, grad_v, attended = attend_backward(queries, keys, values, grad_out)
    out_grad = jnp.einsum("th,td->hd", attended, cot_all, preferred_element_type=jnp.float32)
    grad_proj = jnp.concatenate([grad_q, grad_k, grad_v], -1).astype(jnp.bfloat16)
    qkv_grad = jnp.einsum("td,tc->dc", normed_all, grad_proj, preferred_element_type=jnp.float32)
    grad_normed = lax.psum_scatter(
        jnp.einsum("tc,dc->td", grad_proj, weight_heads, preferred_element_type=jnp.float32).astype(
            jnp.bfloat16
        ),
        "seq",
        scatter_dimension=0,
        tiled=True,
    ).astype(jnp.float32)
    own_normed = lax.dynamic_slice_in_dim(
        normed_all, lax.axis_index("seq") * local_rows, local_rows, 0
    )
    modulated = gains + jnp.sin(moment) * scales
    normal = own_normed.astype(jnp.float32) / modulated
    weighted = grad_normed * modulated
    grad_hidden = inv_rows[:, None] * (
        weighted - normal * jnp.mean(normal * weighted, -1, keepdims=True)
    )
    cotangent = (cot_rows.astype(jnp.float32) + grad_hidden).astype(jnp.bfloat16)
    gain_part = jnp.sum(grad_normed * normal, 0)
    norm_part = jnp.stack([gain_part, jnp.sin(moment) * gain_part])
    qkv_total, out_total = (
        lax.psum_scatter(
            qkv_grad.astype(jnp.bfloat16), "dp", scatter_dimension=0, tiled=True
        ).astype(jnp.float32),
        lax.psum_scatter(
            out_grad.astype(jnp.bfloat16), "dp", scatter_dimension=1, tiled=True
        ).astype(jnp.float32),
    )
    norm_total = lax.psum(norm_part, ("seq", "dp"))
    cot_prev = passed_along(cotangent, "section", -1)
    return (cot_prev, qkv_total, out_total, norm_total)


def local(
    layer_input,
    tangent_input,
    cotangent_input,
    saved_normed,
    saved_inv_rms,
    saved_projections,
    time_index,
    input_weight,
    output_weight,
    norm_gain,
    time_scale,
):
    weight_heads = input_weight[0, :, 0, :]
    output_whole = output_weight[0]
    heads, head_size, width = output_whole.shape
    output_flat = output_whole.reshape(heads * head_size, width)
    output_head = lax.dynamic_index_in_dim(output_whole, lax.axis_index("seq"), 0, keepdims=False)
    gains = norm_gain[0]
    scales = time_scale[0]
    moments = timesteps(time_index[0, 0])
    forward_out = forward_layer(
        layer_input[0, 0], tangent_input[0, 0], weight_heads, output_flat, gains, scales, moments[0]
    )
    backward_out = backward_layer(
        cotangent_input[0, 0],
        saved_normed[0, 0],
        saved_inv_rms[0, 0],
        saved_projections[0, 0, :, 0, :],
        weight_heads,
        output_head,
        gains,
        scales,
        moments[1],
    )
    cot_prev, qkv_total, out_total, norm_total = backward_out
    return (
        forward_out[0][None, None],
        forward_out[1][None, None],
        cot_prev[None, None],
        qkv_total[None, :, None, :],
        out_total[None, None],
        norm_total[None],
    )


def solution(mesh):
    placed = (
        P("section", "dp", "seq", None),
        P("section", "dp", "seq", None),
        P("section", "dp", "seq", None),
        P("section", "dp", None, None),
        P("section", "dp", "seq"),
        P("section", "dp", None, "seq", None),
        P("section", "dp", None),
        P("section", None, "seq", None),
        P("section", None, None, None),
        P("section", None),
        P("section", None),
    )
    return jax.shard_map(
        local,
        mesh=mesh,
        in_specs=placed,
        out_specs=(
            P("section", "dp", "seq", None),
            P("section", "dp", "seq", None),
            P("section", "dp", "seq", None),
            P("section", "dp", "seq", None),
            P("section", "seq", None, "dp"),
            P("section", None, None),
        ),
        check_vma=False,
    )
```

profile of v0, /device:TPU:0, one launch (start us, length us, event | category | flops | bytes accessed | tf_op | source)
XLA Modules:
  0.0 192.8 jit_solution(16712994285691690228)
XLA Ops:
  7.2 0.7 all-gather.6.cloned.1.call-update
  8.0 0.7 add_multiply_fusion
  11.4 1.3 fusion.76
  12.7 0.8 fusion.44
  13.5 0.6 multiply_add_fusion
  14.1 20.8 %all-gather.6.cloned.1.call-done = bf16[1,1,512,2048]{3,2,1,0:T(8,128)(2,1)} async-done(((bf16[1,1,128,2048]{3,2,1,0:T(8,128)(2,1)}), bf16[1,1,512,2048]{3,2,1,0:T(8,128)(2,1)}) %all-gather.6.cloned.1.call-update) | async-done | bytes 2097168 | tf_op jit(solution)/shard_map/all_gather | solution.py:144
  34.9 3.4 %convolution_convert_fusion.2 = bf16[128,2048]{1,0:T(8,128)(2,1)} fusion(bf16[1,1,512,2048]{3,2,1,0:T(8,128)(2,1)} %all-gather.6.cloned.1.call-done, bf16[512,384]{1,0:T(8,128)(2,1)S(1)} %bitcast.145, f32[512,512]{0,1:T(8,128)S(1)} %get-tuple-element.94, f32[512]{0:T(512)} %fusion.44, f32[512]{0:T(512)} %copy-done.8), kind=kOutput, calls=%fused_computation.3 | convolution fusion | flops 336658432 | bytes 3805184 | tf_op jit(solution)/shard_map/th,td->hd/dot_general | solution.py:149
  38.4 1.5 fusion.39
  39.9 2.4 %fusion.27 = (bf16[1,128,2048]{2,1,0:T(8,128)(2,1)S(1)}, bf16[1,128,2048]{2,1,0:T(8,128)(2,1)S(1)}) fusion(bf16[1,1,128,2048]{3,2,1,0:T(8,128)(2,1)} %param.11, f32[2048]{0:T(1024)S(1)} %bitcast.154, f32[128]{0:T(128)S(1)} %get-tuple-element.87, f32[2048]{0:T(1024)} %bitcast.155, f32[128]{0:T(128)S(1)} %get-tuple-element.88, bf16[1,1,128,2048]{3,2,1,0:T(8,128)(2,1)} %param.12), kind=kLoop, calls=%fused_computation.41 | loop fusion | flops 3145728 | bytes 2114560 | tf_op jit(solution)/shard_map/convert_element_type | solution.py:108
  42.3 1.1 pad_maximum_fusion
  43.5 2.6 %fusion.22 = bf16[128,512]{1,0:T(8,128)(2,1)S(1)} fusion(bf16[1,1,512,2048]{3,2,1,0:T(8,128)(2,1)} %all-gather.6.cloned.1.call-done, bf16[1,4,128,2048]{3,2,1,0:T(8,128)(2,1)S(1)} %copy-done, s32[]{:T(128)S(6)} %select_n.7), kind=kOutput, calls=%fused_computation.33 | convolution fusion | flops 268500992 | bytes 2752516 | tf_op jit(solution)/shard_map/td,hd->th/dot_general | solution.py:145
  48.0 1.0 copy-done.5
  49.0 2.1 %fusion = bf16[2048,384]{0,1:T(8,128)(2,1)} fusion(bf16[1,1,512,2048]{3,2,1,0:T(8,128)(2,1)S(1)} %copy-done.5, bf16[512,128]{0,1:T(8,128)(2,1)S(1)} %convolution_convert_fusion.4, bf16[512,128]{0,1:T(8,128)(2,1)S(1)} %convolution_convert_fusion.5, bf16[512,128]{0,1:T(8,128)(2,1)S(1)} %convolution_convert_fusion.6), kind=kOutput, calls=%fused_computation.2 | convolution fusion | flops 807272448 | bytes 4063232 | tf_op jit(solution)/shard_map/td,tc->dc/dot_general | solution.py:151
  51.2 4.2 %convolution_convert_fusion = bf16[512,2048]{1,0:T(8,128)(2,1)} fusion(bf16[1,2048,1,384]{3,1,2,0:T(8,128)(2,1)} %param.18, bf16[512,128]{0,1:T(8,128)(2,1)S(1)} %convolution_convert_fusion.4, bf16[512,128]{0,1:T(8,128)(2,1)} %copy-done.6, bf16[512,128]{0,1:T(8,128)(2,1)} %copy-done.7), kind=kOutput, calls=%fused_computation | convolution fusion | flops 807534592 | bytes 4063232 | tf_op jit(solution)/shard_map/tc,dc->td/dot_general | solution.py:153
  55.5 1.8 bitcast_convert_fusion.1
  57.3 31.9 %all-gather.4.cloned.1.call-done = bf16[2,512,2048]{2,1,0:T(8,128)(2,1)} async-done(((bf16[2,128,2048]{2,1,0:T(8,128)(2,1)}), bf16[2,512,2048]{2,1,0:T(8,128)(2,1)}) %all-gather.4.cloned.1.call-update) | async-done | bytes 4194320 | tf_op jit(solution)/shard_map/all_gather | solution.py:113
  89.2 5.0 %fusion.11 = bf16[2,512,384]{2,1,0:T(8,128)(2,1)S(1)} fusion(bf16[2,512,2048]{2,1,0:T(8,128)(2,1)} %all-gather.4.cloned.1.call-done, bf16[1,2048,1,384]{3,1,2,0:T(8,128)(2,1)} %param.18), kind=kOutput, calls=%fused_computation.17 | convolution fusion | flops 1611005952 | bytes 6553600 | tf_op jit(solution)/shard_map/srd,dc->src/dot_general | solution.py:111
  96.7 1.0 copy.19
  97.7 3.6 %all-to-all-start = ((bf16[2,512,128]{2,0,1:T(2,128)(2,1)}), bf16[2,512,128]{2,0,1:T(2,128)(2,1)S(1)}, u32[]{:S(2)}, u32[]{:S(2)}) async-start(bf16[2,512,128]{2,0,1:T(2,128)(2,1)} %copy.19), calls=%async_computation | async-start | bytes 524288 | tf_op jit(solution)/shard_map/all_to_all | solution.py:125
  101.3 16.8 %reduce-scatter.6.cloned.1.call-done = bf16[1024,384]{0,1:T(8,128)(2,1)} async-done(((bf16[2048,384]{0,1:T(8,128)(2,1)}), bf16[1024,384]{0,1:T(8,128)(2,1)}) %reduce-scatter.6.cloned.1.call-update) | async-done | bytes 786448 | tf_op jit(solution)/shard_map/reduce_scatter | solution.py:173
  118.1 2.5 %bitcast_convert_fusion = f32[1,1024,1,384]{1,3,2,0:T(8,128)} fusion(bf16[1024,384]{0,1:T(8,128)(2,1)} %reduce-scatter.6.cloned.1.call-done), kind=kLoop, calls=%fused_computation.68 | loop fusion | flops 393216 | bytes 2359296 | tf_op jit(solution)/shard_map/broadcast_in_dim | solution.py:225
  120.6 4.8 %copy.21 = f32[1,1024,1,384]{3,2,1,0:T(1,128)} copy(f32[1,1024,1,384]{1,3,2,0:T(8,128)} %bitcast_convert_fusion) | data formatting | bytes 3145728
  125.7 0.7 fusion.77
  127.2 1.1 pad_maximum_fusion.1
  128.3 1.5 collective-permute-start
  129.8 22.1 %reduce-scatter.4.cloned.1.call-done = bf16[128,2048]{1,0:T(8,128)(2,1)} async-done(((bf16[512,2048]{1,0:T(8,128)(2,1)}), bf16[128,2048]{1,0:T(8,128)(2,1)}) %reduce-scatter.4.cloned.1.call-update) | async-done | bytes 524304 | tf_op jit(solution)/shard_map/reduce_scatter | solution.py:152
  152.0 1.6 fusion.34
  153.6 1.7 fusion.33
  155.2 3.4 %collective-permute-start.1 = (bf16[128,2048]{1,0:T(8,128)(2,1)S(1)}, bf16[128,2048]{1,0:T(8,128)(2,1)S(1)}, u32[]{:S(2)}, u32[]{:S(2)}) collective-permute-start(bf16[128,2048]{1,0:T(8,128)(2,1)S(1)} %fusion.33), channel_id=1, source_target_pairs={{0,24},{8,0},{16,8},{24,16},{1,25},{9,1},{17,9},{25,17},{2,26},{10... | collective-permute-start | bytes 1572872 | tf_op jit(solution)/shard_map/ppermute | solution.py:17
  158.6 24.5 %psum.7 = f32[1,2,2048]{2,1,0:T(2,128)} all-reduce(f32[1,2,2048]{2,1,0:T(2,128)S(1)} %maximum_bitcast_fusion), channel_id=1, replica_groups=mesh['section'=4,'seq'=4,'dp'=2] {'seq','dp'}, use_global_device_ids=true, to_apply=%region_13.14 | all-reduce | flops 4096 | bytes 32768 | tf_op jit(solution)/shard_map/psum | solution.py:180
  183.2 2.3 %slice_bitcast_fusion = (bf16[1,1,128,2048]{3,2,1,0:T(8,128)(2,1)}, bf16[1,1,128,2048]{3,2,1,0:T(8,128)(2,1)}) fusion(bf16[2,128,2048]{2,1,0:T(8,128)(2,1)} %collective-permute-done), kind=kLoop, calls=%fused_computation.70 | loop fusion | bytes 2097152 | tf_op jit(solution)/shard_map/broadcast_in_dim;squeeze | solution.py:223
  185.5 0.8 copy.25
  (61 shorter events, 6.3 us)
Async XLA Ops:
  7.2 36.3 %copy-start = (bf16[1,4,128,2048]{3,2,1,0:T(8,128)(2,1)S(1)}, bf16[1,4,128,2048]{3,2,1,0:T(8,128)(2,1)}, u32[]{:S(2)}) copy-start(bf16[1,4,128,2048]{3,2,1,0:T(8,128)(2,1)} %param.19) | copy-start | bytes 6291460
  7.2 27.7 %copy-start.4 = (bf16[1,1,512,1,384]{4,2,3,1,0:T(8,128)(2,1)S(1)}, bf16[1,1,512,1,384]{4,2,3,1,0:T(8,128)(2,1)}, u32[]{:S(2)}) copy-start(bf16[1,1,512,1,384]{4,2,3,1,0:T(8,128)(2,1)} %param.16) | copy-start | bytes 1179652
  7.2 27.7 %all-gather.6.cloned.1.call-start = ((), (), s32[]{:S(2)}) async-start(), calls=%async_computation.8 | async-start | bytes 2621440 | tf_op jit(solution)/shard_map/all_gather | solution.py:144
  7.9 47.5 %reduce-scatter.8.cloned.1.call-start = ((), (), s32[]{:S(2)}) async-start(), calls=%async_computation.7 | async-start | bytes 786432 | tf_op jit(solution)/shard_map/reduce_scatter | solution.py:176
  8.0 5.5 %copy-start.10 = (f32[1,2048]{1,0:T(1,128)S(1)}, f32[1,2048]{1,0:T(1,128)}, u32[]{:S(2)}) copy-start(f32[1,2048]{1,0:T(1,128)} %param.20) | copy-start | bytes 24580
  8.0 5.5 %copy-start.11 = (f32[1,2048]{1,0:T(1,128)S(1)}, f32[1,2048]{1,0:T(1,128)}, u32[]{:S(2)}) copy-start(f32[1,2048]{1,0:T(1,128)} %param.21) | copy-start | bytes 24580
  12.7 0.8 copy-start.8
  38.3 50.9 %all-gather.4.cloned.1.call-start = ((), (), s32[]{:S(2)}) async-start(), calls=%async_computation.4 | async-start | bytes 5242880 | tf_op jit(solution)/shard_map/all_gather | solution.py:113
  43.4 2.7 %copy-start.9 = (f32[512]{0:T(512)S(1)}, f32[512]{0:T(512)}, u32[]{:S(2)}) copy-start(f32[512]{0:T(512)} %copy-done.8) | copy-start | bytes 6148
  43.4 2.7 %copy-start.12 = (f32[512]{0:T(512)S(1)}, f32[512]{0:T(512)}, u32[]{:S(2)}) copy-start(f32[512]{0:T(512)} %fusion.44) | copy-start | bytes 6148
  43.4 74.6 %reduce-scatter.6.cloned.1.call-start = ((), (), s32[]{:S(2)}) async-start(), calls=%async_computation.6 | async-start | bytes 2359296 | tf_op jit(solution)/shard_map/reduce_scatter | solution.py:173
  47.1 0.7 copy-start.6
  47.4 0.7 copy-start.7
  47.4 1.6 copy-start.5
  51.2 100.8 %reduce-scatter.4.cloned.1.call-start = ((), (), s32[]{:S(2)}) async-start(), calls=%async_computation.5 | async-start | bytes 2621440 | tf_op jit(solution)/shard_map/reduce_scatter | solution.py:152
  97.7 27.7 %all-to-all-start = ((bf16[2,512,128]{2,0,1:T(2,128)(2,1)}), bf16[2,512,128]{2,0,1:T(2,128)(2,1)S(1)}, u32[]{:S(2)}, u32[]{:S(2)}) async-start(bf16[2,512,128]{2,0,1:T(2,128)(2,1)} %copy.19), calls=%async_computation | async-start | bytes 524288 | tf_op jit(solution)/shard_map/all_to_all | solution.py:125
  125.7 1.1 copy-start.1
  125.7 1.2 copy-start.2
  127.2 26.3 %copy-start.3 = (bf16[1,1,128,2048]{3,2,1,0:T(8,128)(2,1)S(1)}, bf16[1,1,128,2048]{3,2,1,0:T(8,128)(2,1)}, u32[]{:S(2)}) copy-start(bf16[1,1,128,2048]{3,2,1,0:T(8,128)(2,1)} %param.13) | copy-start | bytes 1572868
  127.2 26.3 %copy-start.13 = (f32[1,1,128]{2,1,0:T(1,128)S(1)}, f32[1,1,128]{2,1,0:T(1,128)}, u32[]{:S(2)}) copy-start(f32[1,1,128]{2,1,0:T(1,128)} %param.15) | copy-start | bytes 1540
  128.3 54.9 %collective-permute-start = (bf16[2,128,2048]{2,1,0:T(8,128)(2,1)}, bf16[2,128,2048]{2,1,0:T(8,128)(2,1)}, u32[]{:S(2)}, u32[]{:S(2)}) collective-permute-start(bf16[2,128,2048]{2,1,0:T(8,128)(2,1)} %pad_maximum_fusion.1), channel_id=1, source_target_pairs={{0,8},{8,16},{16,24},{24,0},{1,9},{9,17},{17,25},{25,1},{2,10},{10... | collective-permute-start | bytes 3145736 | tf_op jit(solution)/shard_map/ppermute | solution.py:17
  155.2 30.2 %collective-permute-start.1 = (bf16[128,2048]{1,0:T(8,128)(2,1)S(1)}, bf16[128,2048]{1,0:T(8,128)(2,1)S(1)}, u32[]{:S(2)}, u32[]{:S(2)}) collective-permute-start(bf16[128,2048]{1,0:T(8,128)(2,1)S(1)} %fusion.33), channel_id=1, source_target_pairs={{0,24},{8,0},{16,8},{24,16},{1,25},{9,1},{17,9},{25,17},{2,26},{10... | collective-permute-start | bytes 1572872 | tf_op jit(solution)/shard_map/ppermute | solution.py:17
Sparse Core Ops, SparseCore 0:
  9.6 25.2 all-gather.5
  38.5 14.5 reduce-scatter.7
  54.7 34.4 all-gather.3
  92.0 26.0 reduce-scatter.5
  120.5 31.4 reduce-scatter.3
where the time goes:
time: 194 us; the launch traced here: 193 us
  waiting for transfers between devices  92.5 us (48%)
  blocking collectives  24.5 us (13%)
  matrix products  22.8 us (12%)
  other arithmetic  16.5 us (9%)
  between operations  16.3 us (8%)
  local copies, waits for them, and re-layouts  11.6 us (6%)
  starting transfers between devices  8.7 us (4%)
    all_gather x1, waiting for transfers between devices, forward_layer(): lax.all_gather(stacked, 'seq', axis=1, tiled=True)  31.9 us
    psum x1, blocking collectives, backward_layer(): norm_total = lax.psum(norm_part, ('seq', 'dp'))  24.5 us
    reduce_scatter x1, waiting for transfers between devices, backward_layer(): lax.psum_scatter(jnp.einsum('tc,dc->td', grad_proj, weight_heads, preferr...  22.1 us
    all_gather x1, waiting for transfers between devices, backward_layer(): cot_all = lax.all_gather(cot_rows, 'seq', axis=0, tiled=True)  20.8 us
    reduce_scatter x1, waiting for transfers between devices, backward_layer(): lax.psum_scatter(qkv_grad.astype(jnp.bfloat16), 'dp', scatter_dimension=0...  16.8 us
    unnamed x30, local copies, waits for them, and re-layouts  7.43 us
    dot_general x1, matrix products, forward_layer(): jnp.einsum('srd,dc->src', lax.all_gather(stacked, 'seq', axis=1, tiled=Tr...  4.99 us
    ppermute x2, starting transfers between devices, passed_along(): return lax.ppermute(value, axis, pairs)  4.91 us
  transfers between devices with their start and end apart: 8, of which 4 were waited for; matrix products, arithmetic and copies ran while one was open for 23% of the time, Pallas kernels for 0%

commit v1 on v0

v1 whole, which is shorter than its diff:
```python
import math

import jax
import jax.numpy as jnp
from jax import lax
from jax.sharding import PartitionSpec as P

TSTEPS = 1000


EPS = 1e-06


def passed_along(value, axis, steps):
    count = lax.axis_size(axis)
    pairs = [(source, (source + steps) % count) for source in range(count)]
    return lax.ppermute(value, axis, pairs)


def timesteps(indices):
    return math.pi / 2 * (indices.astype(jnp.float32) + 0.5) / TSTEPS


def attend_tangent(queries, keys, values, tan_queries, tan_keys, tan_values):
    rows = queries.shape[0]
    block_rows = min(512, rows)
    scale = 1.0 / math.sqrt(queries.shape[1])

    def one_block(inputs):
        query_block, tangent_block = inputs
        scores = (
            jnp.einsum("qd,kd->qk", query_block, keys, preferred_element_type=jnp.float32) * scale
        )
        probs = jax.nn.softmax(scores, axis=-1)
        tan_scores = (
            jnp.einsum("qd,kd->qk", tangent_block, keys, preferred_element_type=jnp.float32)
            + jnp.einsum("qd,kd->qk", query_block, tan_keys, preferred_element_type=jnp.float32)
        ) * scale
        tan_probs = probs * (tan_scores - jnp.sum(probs * tan_scores, -1, keepdims=True))
        probs_low = probs.astype(jnp.bfloat16)
        tan_low = tan_probs.astype(jnp.bfloat16)
        attended = jnp.dot(probs_low, values, preferred_element_type=jnp.float32)
        tan_attended = jnp.dot(tan_low, values, preferred_element_type=jnp.float32) + jnp.dot(
            probs_low, tan_values, preferred_element_type=jnp.float32
        )
        return (attended.astype(jnp.bfloat16), tan_attended.astype(jnp.bfloat16))

    shaped = (
        queries.reshape(rows // block_rows, block_rows, -1),
        tan_queries.reshape(rows // block_rows, block_rows, -1),
    )
    attended, tan_attended = lax.map(one_block, shaped)
    return (attended.reshape(rows, -1), tan_attended.reshape(rows, -1))


def attend_backward(queries, keys, values, grad_attended):
    rows, head_size = queries.shape
    block_rows = min(512, rows)
    scale = 1.0 / math.sqrt(head_size)

    def one_block(carry, inputs):
        grad_keys, grad_values = carry
        query_block, grad_block = inputs
        scores = (
            jnp.einsum("qd,kd->qk", query_block, keys, preferred_element_type=jnp.float32) * scale
        )
        probs = jax.nn.softmax(scores, axis=-1)
        probs_low = probs.astype(jnp.bfloat16)
        attended = jnp.dot(probs_low, values, preferred_element_type=jnp.float32).astype(
            jnp.bfloat16
        )
        grad_values = grad_values + jnp.einsum(
            "qk,qd->kd", probs_low, grad_block, preferred_element_type=jnp.float32
        )
        grad_probs = jnp.einsum("qd,kd->qk", grad_block, values, preferred_element_type=jnp.float32)
        grad_scores = probs * (grad_probs - jnp.sum(probs * grad_probs, -1, keepdims=True)) * scale
        grad_low = grad_scores.astype(jnp.bfloat16)
        grad_queries = jnp.dot(grad_low, keys, preferred_element_type=jnp.float32)
        grad_keys = grad_keys + jnp.einsum(
            "qk,qd->kd", grad_low, query_block, preferred_element_type=jnp.float32
        )
        return ((grad_keys, grad_values), (grad_queries, attended))

    zeros = jnp.zeros((rows, head_size), jnp.float32)
    shaped = (
        queries.reshape(rows // block_rows, block_rows, head_size),
        grad_attended.reshape(rows // block_rows, block_rows, head_size),
    )
    (grad_keys, grad_values), (grad_queries, attended) = lax.scan(one_block, (zeros, zeros), shaped)
    return (
        grad_queries.reshape(rows, head_size),
        grad_keys,
        grad_values,
        attended.reshape(rows, head_size),
    )


def swapped(value, axis, mask):
    count = lax.axis_size(axis)
    return lax.ppermute(value, axis, [(source, source ^ mask) for source in range(count)])


def gathered(value):
    count = lax.axis_size("seq")
    pieces = {0: value}
    for mask in range(2, count, 2):
        pieces[mask] = swapped(value, "seq", mask)
    for mask in range(1, count, 2):
        pieces[mask] = swapped(pieces[mask ^ 1], "seq", 1)
    return [pieces[mask] for mask in range(count)]


def summed_to_owner(terms):
    count = len(terms)
    pairs = {}
    for mask in list(range(2, count, 2)) + [0]:
        other = swapped(terms[mask ^ 1], "seq", 1)
        pairs[mask] = terms[mask].astype(jnp.float32) + other.astype(jnp.float32)
    total = pairs[0]
    for mask in range(2, count, 2):
        total = total + swapped(pairs[mask].astype(jnp.bfloat16), "seq", mask).astype(jnp.float32)
    return total


def scattered_over_dp(value, axis):
    count = lax.axis_size("dp")
    me = lax.axis_index("dp")
    length = value.shape[axis] // count
    total = lax.dynamic_slice_in_dim(value, me * length, length, axis)
    for step in range(1, count):
        part = lax.dynamic_slice_in_dim(value, lax.rem(me + step, count) * length, length, axis)
        total = total + passed_along(part.astype(jnp.bfloat16), "dp", step).astype(jnp.float32)
    return total


def summed_everywhere(value):
    for axis in ("seq", "dp"):
        mask = 1
        while mask < lax.axis_size(axis):
            value = value + swapped(value, axis, mask)
            mask *= 2
    return value


def local(
    layer_input,
    tangent_input,
    cotangent_input,
    saved_normed,
    saved_inv_rms,
    saved_projections,
    time_index,
    input_weight,
    output_weight,
    norm_gain,
    time_scale,
):
    count = lax.axis_size("seq")
    me = lax.axis_index("seq")
    weight_heads = input_weight[0, :, 0, :]
    output_whole = output_weight[0]
    heads, head_size, width = output_whole.shape
    output_flat = output_whole.reshape(heads * head_size, width)
    output_head = lax.dynamic_index_in_dim(output_whole, me, 0, keepdims=False)
    gains = norm_gain[0]
    scales = time_scale[0]
    moments = timesteps(time_index[0, 0])
    cot_rows = cotangent_input[0, 0]
    normed_all = saved_normed[0, 0]
    inv_rows = saved_inv_rms[0, 0]
    saved_heads = saved_projections[0, 0, :, 0, :]
    rows = cot_rows.shape[0]
    owners = [jnp.bitwise_xor(me, mask) for mask in range(count)]

    cot_pieces = gathered(cot_rows)
    moment = moments[0]
    hidden = layer_input[0, 0].astype(jnp.float32)
    tangent = tangent_input[0, 0].astype(jnp.float32)
    inverse = lax.rsqrt(jnp.mean(hidden * hidden, -1, keepdims=True) + EPS)
    normal = hidden * inverse
    tan_inverse = -(inverse**3) * jnp.mean(hidden * tangent, -1, keepdims=True)
    tan_normal = tangent * inverse + hidden * tan_inverse
    modulated = gains + jnp.sin(moment) * scales
    tan_modulated = jnp.cos(moment) * scales
    normed = (normal * modulated).astype(jnp.bfloat16)
    tan_normed = (tan_normal * modulated + normal * tan_modulated).astype(jnp.bfloat16)
    normed_pieces = gathered(normed)
    tan_pieces = gathered(tan_normed)

    grad_out = jnp.zeros((rows * count, head_size), jnp.bfloat16)
    for mask in range(count):
        piece = jnp.einsum(
            "td,hd->th", cot_pieces[mask], output_head, preferred_element_type=jnp.float32
        ).astype(jnp.bfloat16)
        grad_out = lax.dynamic_update_slice_in_dim(grad_out, piece, owners[mask] * rows, 0)
    grad_q, grad_k, grad_v, attended_b = attend_backward(
        saved_heads[:, :head_size],
        saved_heads[:, head_size : 2 * head_size],
        saved_heads[:, 2 * head_size :],
        grad_out,
    )
    grad_proj = jnp.concatenate([grad_q, grad_k, grad_v], -1).astype(jnp.bfloat16)
    terms = {}
    for mask in reversed(range(count)):
        piece = lax.dynamic_slice_in_dim(grad_proj, owners[mask] * rows, rows, 0)
        terms[mask] = jnp.einsum(
            "tc,dc->td", piece, weight_heads, preferred_element_type=jnp.float32
        ).astype(jnp.bfloat16)
    grad_normed = summed_to_owner([terms[mask] for mask in range(count)])
    qkv_grad = jnp.einsum("td,tc->dc", normed_all, grad_proj, preferred_element_type=jnp.float32)
    out_grad = jnp.zeros((head_size, width), jnp.float32)
    for mask in range(count):
        piece = lax.dynamic_slice_in_dim(attended_b, owners[mask] * rows, rows, 0)
        out_grad = out_grad + jnp.einsum(
            "th,td->hd", piece, cot_pieces[mask], preferred_element_type=jnp.float32
        )
    qkv_total = scattered_over_dp(qkv_grad, 0)
    out_total = scattered_over_dp(out_grad, 1)

    def projected(pieces):
        return jnp.concatenate(
            [
                jnp.dot(piece, weight_heads, preferred_element_type=jnp.float32).astype(
                    jnp.bfloat16
                )
                for piece in pieces
            ]
        )

    proj = projected(normed_pieces)
    tan_proj = projected(tan_pieces)
    attended, tan_attended = attend_tangent(
        proj[:, :head_size],
        proj[:, head_size : 2 * head_size],
        proj[:, 2 * head_size :],
        tan_proj[:, :head_size],
        tan_proj[:, head_size : 2 * head_size],
        tan_proj[:, 2 * head_size :],
    )
    both = jnp.stack([attended, tan_attended])
    moved = jnp.zeros((2, rows, heads * head_size), jnp.bfloat16)
    for mask in range(count):
        piece = both[:, mask * rows : (mask + 1) * rows]
        if mask:
            piece = swapped(piece, "seq", mask)
        moved = lax.dynamic_update_slice_in_dim(moved, piece, owners[mask] * head_size, 2)
    result = hidden + jnp.dot(moved[0], output_flat, preferred_element_type=jnp.float32)
    next_input = passed_along(result.astype(jnp.bfloat16), "section", 1)
    result = tangent + jnp.dot(moved[1], output_flat, preferred_element_type=jnp.float32)
    next_tangent = passed_along(result.astype(jnp.bfloat16), "section", 1)

    moment = moments[1]
    own_normed = lax.dynamic_slice_in_dim(normed_all, me * rows, rows, 0)
    modulated = gains + jnp.sin(moment) * scales
    normal_b = own_normed.astype(jnp.float32) / modulated
    weighted = grad_normed * modulated
    grad_hidden = inv_rows[:, None] * (
        weighted - normal_b * jnp.mean(normal_b * weighted, -1, keepdims=True)
    )
    cotangent = (cot_rows.astype(jnp.float32) + grad_hidden).astype(jnp.bfloat16)
    cot_prev = passed_along(cotangent, "section", -1)
    gain_part = jnp.sum(grad_normed * normal_b, 0)
    norm_total = summed_everywhere(jnp.stack([gain_part, jnp.sin(moment) * gain_part]))
    return (
        next_input[None, None],
        next_tangent[None, None],
        cot_prev[None, None],
        qkv_total[None, :, None, :],
        out_total[None, None],
        norm_total[None],
    )


def solution(mesh):
    placed = (
        P("section", "dp", "seq", None),
        P("section", "dp", "seq", None),
        P("section", "dp", "seq", None),
        P("section", "dp", None, None),
        P("section", "dp", "seq"),
        P("section", "dp", None, "seq", None),
        P("section", "dp", None),
        P("section", None, "seq", None),
        P("section", None, None, None),
        P("section", None),
        P("section", None),
    )
    return jax.shard_map(
        local,
        mesh=mesh,
        in_specs=placed,
        out_specs=(
            P("section", "dp", "seq", None),
            P("section", "dp", "seq", None),
            P("section", "dp", "seq", None),
            P("section", "dp", "seq", None),
            P("section", "seq", None, "dp"),
            P("section", None, None),
        ),
        check_vma=False,
    )
```

time: 194 us -> 112 us (0.58)
  waiting for transfers between devices: 92.5 us -> 37.6 us
  blocking collectives: 24.5 us -> 0 us
  between operations: 16.3 us -> 3.32 us
  starting transfers between devices: 8.7 us -> 20.9 us
  matrix products: 22.8 us -> 28.2 us
  other arithmetic: 16.5 us -> 11.5 us
    all_gather x2 -> x0, waiting for transfers between devices: 52.7 us -> none  [the longest x1 31.9 us: forward_layer(): lax.all_gather(stacked, 'seq', axis=1, tiled=True)]
    reduce_scatter x3 -> x0, waiting for transfers between devices: 39 us -> none  [the longest x1 22.1 us: backward_layer(): lax.psum_scatter(jnp.einsum('tc,dc->td', grad_proj, weight_heads, preferr...]
    psum x1 -> x0, blocking collectives: 24.5 us -> none  [backward_layer(): norm_total = lax.psum(norm_part, ('seq', 'dp'))]
    ppermute x2 -> x5, waiting for transfers between devices: 0.01 us -> 21.2 us  [passed_along(): return lax.ppermute(value, axis, pairs)]
    ppermute x0 -> x18, waiting for transfers between devices: none -> 16.3 us  [swapped(): lax.ppermute(value, axis, [(source, source ^ mask) for source in range(co...]
    ppermute x0 -> x18, starting transfers between devices: none -> 12.8 us  [swapped(): lax.ppermute(value, axis, [(source, source ^ mask) for source in range(co...]
    dot_general x6 -> x24, matrix products: 18 us -> 24.4 us  [the longest x8 8.68 us: projected(): jnp.dot(piece, weight_heads, preferred_element_type=jnp.float32)]
    all_to_all x1 -> x0, starting transfers between devices: 3.59 us -> none  [forward_layer(): lax.all_to_all(jnp.stack([attended, tan_attended]), 'seq', split_axis=1,...]
  transfers between devices with their start and end apart: 8 -> 23, of which waited for: 4 -> 7; matrix products, arithmetic and copies ran while one was open for 23% -> 38% of each run, Pallas kernels for 0% -> 0%
where the time goes in v1:
time: 112 us
  waiting for transfers between devices  37.6 us (34%)
  matrix products  28.2 us (25%)
  starting transfers between devices  20.9 us (19%)
  other arithmetic  11.5 us (10%)
  local copies, waits for them, and re-layouts  10.1 us (9%)
  between operations  3.32 us (3%)
    ppermute x5, waiting for transfers between devices, passed_along(): return lax.ppermute(value, axis, pairs)  21.2 us
    ppermute x18, waiting for transfers between devices, swapped(): lax.ppermute(value, axis, [(source, source ^ mask) for source in range(co...  16.3 us
    ppermute x18, starting transfers between devices, swapped(): lax.ppermute(value, axis, [(source, source ^ mask) for source in range(co...  12.8 us
    unnamed x34, local copies, waits for them, and re-layouts  9.23 us
    dot_general x8, matrix products, projected(): jnp.dot(piece, weight_heads, preferred_element_type=jnp.float32)  8.68 us
    ppermute x5, starting transfers between devices, passed_along(): return lax.ppermute(value, axis, pairs)  8.11 us
    dot_general x4, matrix products, local(): jnp.einsum('th,td->hd', piece, cot_pieces[mask], preferred_element_type=j...  5.43 us
    dot_general x4, matrix products, local(): jnp.einsum('td,hd->th', cot_pieces[mask], output_head, preferred_element_...  4.57 us
  transfers between devices with their start and end apart: 23, of which 7 were waited for; matrix products, arithmetic and copies ran while one was open for 38% of the time, Pallas kernels for 0%

profile of v1, /device:TPU:0, one launch (start us, length us, event | category | flops | bytes accessed | tf_op | source)
XLA Modules:
  0.0 111.5 jit_solution(17044453285508570009)
XLA Ops:
  0.6 3.0 %collective-permute-start.12 = (bf16[128,2048]{1,0:T(8,128)(2,1)}, bf16[128,2048]{1,0:T(8,128)(2,1)}, u32[]{:S(2)}, u32[]{:S(2)}) collective-permute-start(bf16[128,2048]{1,0:T(8,128)(2,1)} %bitcast.193), channel_id=1, source_target_pairs={{0,4},{2,6},{4,0},{6,2},{1,5},{3,7},{5,1},{7,3},{8,12},{10,14},{12... | collective-permute-start | bytes 1572872 | tf_op jit(solution)/shard_map/ppermute | solution.py:100
  7.1 1.6 %fusion.83 = (f32[128]{0:T(128)S(1)}, f32[128]{0:T(128)S(1)}) fusion(bf16[1,1,128,2048]{3,2,1,0:T(8,128)(2,1)} %param.12, bf16[1,1,128,2048]{3,2,1,0:T(8,128)(2,1)} %param.11), kind=kLoop, calls=%fused_computation.96 | loop fusion | flops 1572608 | bytes 1049600 | tf_op jit(solution)/shard_map/reduce_sum | solution.py:181
  9.5 3.3 %fusion.77 = (bf16[128,2048]{1,0:T(8,128)(2,1)}, bf16[128,2048]{1,0:T(8,128)(2,1)}) fusion(bf16[1,1,128,2048]{3,2,1,0:T(8,128)(2,1)} %param.11, bf16[1,1,128,2048]{3,2,1,0:T(8,128)(2,1)} %param.12, f32[2048]{0:T(1024)S(1)} %bitcast.211, f32[128]{0:T(128)S(1)} %get-tuple-element.81, f32[2048]{0:T(1024)S(1)} %bitcast.208, f32[128]{0:T(128)S(1)} %get-tuple-element.82), kind=kLoop, calls=%fused_computation.90 | loop fusion | flops 3145728 | bytes 2114560 | tf_op jit(solution)/shard_map/convert_element_type | solution.py:186
  13.4 1.7 %collective-permute-start.1 = (bf16[128,2048]{1,0:T(8,128)(2,1)}, bf16[128,2048]{1,0:T(8,128)(2,1)}, u32[]{:S(2)}, u32[]{:S(2)}) collective-permute-start(bf16[128,2048]{1,0:T(8,128)(2,1)} %get-tuple-element.62), channel_id=1, source_target_pairs={{0,4},{2,6},{4,0},{6,2},{1,5},{3,7},{5,1},{7,3},{8,12},{10,14},{12... | collective-permute-start | bytes 1572872 | tf_op jit(solution)/shard_map/ppermute | solution.py:100
  15.1 1.2 %fusion.50 = bf16[128,384]{1,0:T(8,128)(2,1)} fusion(bf16[1,2048,1,384]{3,1,2,0:T(8,128)(2,1)S(1)} %copy-done.1, bf16[1,1,128,2048]{3,2,1,0:T(8,128)(2,1)S(1)} %copy-done.3, bf16[1,1,128,2048]{3,2,1,0:T(8,128)(2,1)S(1)} %copy-done.5, f32[2048]{0:T(1024)S(1)} %bitcast.212, f32[128]{0:T(128)S(1)} %get-tuple-element.81, f32[2048]{0:T(1024)S(1)} %bitcast.209, ...), kind=kOutput, calls=%fused_computation.67 | convolution fusion | flops 203997184 | bytes 2737152 | tf_op jit(solution)/shard_map/dot_general | solution.py:223
  19.0 2.4 %fusion.145 = f32[128,2048]{1,0:T(8,128)} fusion(bf16[512,128]{1,0:T(8,128)(2,1)} %convolution_convert_fusion.4, s32[]{:T(128)S(6)} %select_n.16, bf16[1,1,128,2048]{3,2,1,0:T(8,128)(2,1)} %param.13), kind=kOutput, calls=%fused_computation.178 | convolution fusion | flops 67108864 | bytes 1605636 | tf_op jit(solution)/shard_map/th,td->hd/dot_general | solution.py:214
  21.4 1.5 %fusion.65 = bf16[512,128]{0,1:T(8,128)(2,1)S(1)} fusion(bf16[512,128]{0,1:T(8,128)(2,1)S(1)} %squeeze.46, s32[]{:T(128)S(6)} %select_n.16, bf16[1,4,128,2048]{3,2,1,0:T(8,128)(2,1)S(1)} %copy-done, s32[]{:T(128)S(6)} %select_n.20, bf16[1,1,128,2048]{3,2,1,0:T(8,128)(2,1)} %param.13), kind=kOutput, calls=%fused_computation.78 | convolution fusion | flops 67125248 | bytes 1081352 | tf_op jit(solution)/shard_map/td,hd->th/dot_general | solution.py:192
  22.9 5.0 %collective-permute-done.4 = bf16[128,2048]{1,0:T(8,128)(2,1)} collective-permute-done((bf16[128,2048]{1,0:T(8,128)(2,1)}, bf16[128,2048]{1,0:T(8,128)(2,1)}, u32[]{:S(2)}, u32[]{:S(2)}) %collective-permute-start.4) | collective-permute-done | bytes 524320 | tf_op jit(solution)/shard_map/ppermute | solution.py:100
  27.9 2.0 %fusion.56 = bf16[128,384]{1,0:T(8,128)(2,1)S(1)} fusion(bf16[128,2048]{1,0:T(8,128)(2,1)} %collective-permute-done.4, bf16[1,2048,1,384]{3,1,2,0:T(8,128)(2,1)} %param.18), kind=kOutput, calls=%fused_computation.69 | convolution fusion | flops 201375744 | bytes 2195456 | tf_op jit(solution)/shard_map/dot_general | solution.py:223
  29.9 8.8 %collective-permute-done.1 = bf16[128,2048]{1,0:T(8,128)(2,1)} collective-permute-done((bf16[128,2048]{1,0:T(8,128)(2,1)}, bf16[128,2048]{1,0:T(8,128)(2,1)}, u32[]{:S(2)}, u32[]{:S(2)}) %collective-permute-start.1) | collective-permute-done | bytes 524320 | tf_op jit(solution)/shard_map/ppermute | solution.py:100
  38.7 1.5 %fusion.44 = bf16[128,384]{1,0:T(8,128)(2,1)S(1)} fusion(bf16[128,2048]{1,0:T(8,128)(2,1)} %collective-permute-done.1, bf16[1,2048,1,384]{3,1,2,0:T(8,128)(2,1)S(1)} %copy-done.2), kind=kOutput, calls=%fused_computation.65 | convolution fusion | flops 201375744 | bytes 2195456 | tf_op jit(solution)/shard_map/dot_general | solution.py:223
  40.9 1.5 %fusion.53 = bf16[128,384]{1,0:T(8,128)(2,1)S(1)} fusion(bf16[128,2048]{1,0:T(8,128)(2,1)} %collective-permute-done.3, bf16[1,2048,1,384]{3,1,2,0:T(8,128)(2,1)S(1)} %copy-done.2), kind=kOutput, calls=%fused_computation.68 | convolution fusion | flops 201375744 | bytes 2195456 | tf_op jit(solution)/shard_map/dot_general | solution.py:223
  42.9 1.4 %fusion.67 = bf16[512,128]{0,1:T(8,128)(2,1)S(1)} fusion(bf16[512,128]{0,1:T(8,128)(2,1)S(1)} %fusion.65, s32[]{:T(128)S(6)} %select_n.17, bf16[128,2048]{1,0:T(8,128)(2,1)} %collective-permute-done.11, bf16[1,4,128,2048]{3,2,1,0:T(8,128)(2,1)S(1)} %copy-done, s32[]{:T(128)S(6)} %select_n.20), kind=kOutput, calls=%fused_computation.80 | convolution fusion | flops 67125248 | bytes 1081352 | tf_op jit(solution)/shard_map/td,hd->th/dot_general | solution.py:192
  44.3 1.4 %convolution_add_fusion.2 = f32[128,2048]{1,0:T(8,128)S(1)} fusion(f32[128,2048]{1,0:T(8,128)S(1)} %copy-done.8, bf16[128,2048]{1,0:T(8,128)(2,1)} %collective-permute-done.11, bf16[512,128]{1,0:T(8,128)(2,1)S(1)} %copy-done.11, s32[]{:T(128)S(6)} %select_n.17), kind=kOutput, calls=%fused_computation.2 | convolution fusion | flops 67371008 | bytes 2654212 | tf_op jit(solution)/shard_map/th,td->hd/dot_general | solution.py:214
  45.7 1.4 %fusion.69 = bf16[512,128]{0,1:T(8,128)(2,1)S(1)} fusion(bf16[512,128]{0,1:T(8,128)(2,1)S(1)} %fusion.67, s32[]{:T(128)S(6)} %select_n.18, bf16[128,2048]{1,0:T(8,128)(2,1)} %collective-permute-done.12, bf16[1,4,128,2048]{3,2,1,0:T(8,128)(2,1)S(1)} %copy-done, s32[]{:T(128)S(6)} %select_n.20), kind=kOutput, calls=%fused_computation.82 | convolution fusion | flops 67125248 | bytes 1081352 | tf_op jit(solution)/shard_map/td,hd->th/dot_general | solution.py:192
  47.1 1.4 %convolution_add_fusion.1 = f32[128,2048]{1,0:T(8,128)S(1)} fusion(f32[128,2048]{1,0:T(8,128)S(1)} %convolution_add_fusion.2, bf16[128,2048]{1,0:T(8,128)(2,1)} %collective-permute-done.12, bf16[512,128]{1,0:T(8,128)(2,1)S(1)} %copy-done.11, s32[]{:T(128)S(6)} %select_n.18), kind=kOutput, calls=%fused_computation.1 | convolution fusion | flops 67371008 | bytes 2654212 | tf_op jit(solution)/shard_map/th,td->hd/dot_general | solution.py:214
  56.1 1.5 %collective-permute-start.8 = (bf16[2,128,128]{2,1,0:T(8,128)(2,1)S(1)}, bf16[2,128,128]{2,1,0:T(8,128)(2,1)S(1)}, u32[]{:S(2)}, u32[]{:S(2)}) collective-permute-start(bf16[2,128,128]{2,1,0:T(8,128)(2,1)S(1)} %get-tuple-element.72), channel_id=1, source_target_pairs={{0,6},{2,4},{4,2},{6,0},{1,7},{3,5},{5,3},{7,1},{8,14},{10,12},{12... | collective-permute-start | bytes 196616 | tf_op jit(solution)/shard_map/ppermute | solution.py:100
  59.2 1.6 %collective-permute-start.19 = (bf16[128,1024]{1,0:T(8,128)(2,1)S(1)}, bf16[128,1024]{1,0:T(8,128)(2,1)S(1)}, u32[]{:S(2)}, u32[]{:S(2)}) collective-permute-start(bf16[128,1024]{1,0:T(8,128)(2,1)S(1)} %dynamic-slice_convert_fusion.1), channel_id=1, source_target_pairs={{0,1},{1,0},{2,3},{3,2},{4,5},{5,4},{6,7},{7,6},{8,9},{9,8},{10,11... | collective-permute-start | bytes 786440 | tf_op jit(solution)/shard_map/ppermute | solution.py:17
  60.8 1.3 %collective-permute-done.7 = bf16[2,128,128]{2,1,0:T(8,128)(2,1)S(1)} collective-permute-done((bf16[2,128,128]{2,1,0:T(8,128)(2,1)S(1)}, bf16[2,128,128]{2,1,0:T(8,128)(2,1)S(1)}, u32[]{:S(2)}, u32[]{:S(2)}) %collective-permute-start.7) | collective-permute-done | bytes 65568 | tf_op jit(solution)/shard_map/ppermute | solution.py:100
  62.7 1.6 %collective-permute-start.9 = (bf16[128,2048]{1,0:T(8,128)(2,1)S(1)}, bf16[128,2048]{1,0:T(8,128)(2,1)S(1)}, u32[]{:S(2)}, u32[]{:S(2)}) collective-permute-start(bf16[128,2048]{1,0:T(8,128)(2,1)S(1)} %fusion), channel_id=1, source_target_pairs={{0,8},{8,16},{16,24},{24,0},{1,9},{9,17},{17,25},{25,1},{2,10},{10... | collective-permute-start | bytes 1572872 | tf_op jit(solution)/shard_map/ppermute | solution.py:17
  64.8 1.6 %collective-permute-start.10 = (bf16[128,2048]{1,0:T(8,128)(2,1)S(1)}, bf16[128,2048]{1,0:T(8,128)(2,1)S(1)}, u32[]{:S(2)}, u32[]{:S(2)}) collective-permute-start(bf16[128,2048]{1,0:T(8,128)(2,1)S(1)} %fusion.1), channel_id=1, source_target_pairs={{0,8},{8,16},{16,24},{24,0},{1,9},{9,17},{17,25},{25,1},{2,10},{10... | collective-permute-start | bytes 1572872 | tf_op jit(solution)/shard_map/ppermute | solution.py:17
  67.1 1.3 %collective-permute-start.16 = (bf16[128,2048]{1,0:T(8,128)(2,1)S(1)}, bf16[128,2048]{1,0:T(8,128)(2,1)S(1)}, u32[]{:S(2)}, u32[]{:S(2)}) collective-permute-start(bf16[128,2048]{1,0:T(8,128)(2,1)S(1)} %add_convert_fusion.1), channel_id=1, source_target_pairs={{0,4},{2,6},{4,0},{6,2},{1,5},{3,7},{5,1},{7,3},{8,12},{10,14},{12... | collective-permute-start | bytes 1572872 | tf_op jit(solution)/shard_map/ppermute | solution.py:100
  69.5 1.6 %collective-permute-start.18 = (bf16[1024,384]{0,1:T(8,128)(2,1)S(1)}, bf16[1024,384]{0,1:T(8,128)(2,1)S(1)}, u32[]{:S(2)}, u32[]{:S(2)}) collective-permute-start(bf16[1024,384]{0,1:T(8,128)(2,1)S(1)} %fusion.88), channel_id=1, source_target_pairs={{0,1},{1,0},{2,3},{3,2},{4,5},{5,4},{6,7},{7,6},{8,9},{9,8},{10,11... | collective-permute-start | bytes 2359304 | tf_op jit(solution)/shard_map/ppermute | solution.py:17
  71.9 7.4 %collective-permute-done.9 = bf16[128,2048]{1,0:T(8,128)(2,1)S(1)} collective-permute-done((bf16[128,2048]{1,0:T(8,128)(2,1)S(1)}, bf16[128,2048]{1,0:T(8,128)(2,1)S(1)}, u32[]{:S(2)}, u32[]{:S(2)}) %collective-permute-start.9) | collective-permute-done | bytes 524320 | tf_op jit(solution)/shard_map/ppermute | solution.py:17
  79.4 10.0 %collective-permute-done.10 = bf16[128,2048]{1,0:T(8,128)(2,1)S(1)} collective-permute-done((bf16[128,2048]{1,0:T(8,128)(2,1)S(1)}, bf16[128,2048]{1,0:T(8,128)(2,1)S(1)}, u32[]{:S(2)}, u32[]{:S(2)}) %collective-permute-start.10) | collective-permute-done | bytes 524320 | tf_op jit(solution)/shard_map/ppermute | solution.py:17
  92.7 1.3 %add_convert_fusion = bf16[128,2048]{1,0:T(8,128)(2,1)} fusion(f32[128]{0:T(128)S(1)} %broadcast_multiply_fusion.2, f32[2048]{0:T(1024)S(1)} %bitcast.207, f32[128]{0:T(128)S(1)} %bitcast.213, bf16[1,1,512,2048]{3,2,1,0:T(8,128)(2,1)S(1)} %copy-done.9, s32[]{:T(128)S(6)} %select_n.16, bf16[1,1,128,2048]{3,2,1,0:T(8,128)(2,1)S(1)} %copy-done.7, ...), kind=kLoop, calls=%fused_computation.99 | loop fusion | flops 3407872 | bytes 3679236 | tf_op jit(solution)/shard_map/convert_element_type | solution.py:260
  94.0 1.7 %collective-permute-start.17 = (bf16[128,2048]{1,0:T(8,128)(2,1)}, bf16[128,2048]{1,0:T(8,128)(2,1)}, u32[]{:S(2)}, u32[]{:S(2)}) collective-permute-start(bf16[128,2048]{1,0:T(8,128)(2,1)} %add_convert_fusion), channel_id=1, source_target_pairs={{0,24},{8,0},{16,8},{24,16},{1,25},{9,1},{17,9},{25,17},{2,26},{10... | collective-permute-start | bytes 1572872 | tf_op jit(solution)/shard_map/ppermute | solution.py:17
  95.8 1.6 %collective-permute-start.22 = (f32[2,2048]{1,0:T(2,128)S(1)}, f32[2,2048]{1,0:T(2,128)S(1)}, u32[]{:S(2)}, u32[]{:S(2)}) collective-permute-start(f32[2,2048]{1,0:T(2,128)S(1)} %fusion.190), channel_id=1, source_target_pairs={{0,1},{1,0},{2,3},{3,2},{4,5},{5,4},{6,7},{7,6},{8,9},{9,8},{10,11... | collective-permute-start | bytes 49160 | tf_op jit(solution)/shard_map/ppermute | solution.py:100
  97.3 1.4 %fusion.6 = f32[1,1024,1,384]{1,3,2,0:T(8,128)} fusion(bf16[1024,384]{0,1:T(8,128)(2,1)S(1)} %collective-permute-done.18, f32[384,2048]{1,0:T(8,128)S(1)} %fusion.4, s32[]{:T(128)S(6)} %select_n.21), kind=kLoop, calls=%fused_computation.16 | loop fusion | flops 786432 | bytes 3932164 | tf_op jit(solution)/shard_map/broadcast_in_dim | solution.py:268
  98.8 4.8 %copy.17 = f32[1,1024,1,384]{3,2,1,0:T(1,128)} copy(f32[1,1024,1,384]{1,3,2,0:T(8,128)} %fusion.6) | data formatting | bytes 3145728
  104.2 3.8 %collective-permute-done.17 = bf16[128,2048]{1,0:T(8,128)(2,1)} collective-permute-done((bf16[128,2048]{1,0:T(8,128)(2,1)}, bf16[128,2048]{1,0:T(8,128)(2,1)}, u32[]{:S(2)}, u32[]{:S(2)}) %collective-permute-start.17) | collective-permute-done | bytes 524320 | tf_op jit(solution)/shard_map/ppermute | solution.py:17
  109.6 1.9 %copy.31 = bf16[1,1,128,2048]{3,2,1,0:T(8,128)(2,1)} copy(bf16[1,1,128,2048]{3,2,1,0:T(8,128)(2,1)} %bitcast.27) | data formatting | bytes 1048576
  (112 shorter events, 24.7 us)
Async XLA Ops:
  0.6 20.8 %copy-start = (bf16[1,4,128,2048]{3,2,1,0:T(8,128)(2,1)S(1)}, bf16[1,4,128,2048]{3,2,1,0:T(8,128)(2,1)}, u32[]{:S(2)}) copy-start(bf16[1,4,128,2048]{3,2,1,0:T(8,128)(2,1)} %param.19) | copy-start | bytes 6291460
  0.6 39.6 %collective-permute-start.12 = (bf16[128,2048]{1,0:T(8,128)(2,1)}, bf16[128,2048]{1,0:T(8,128)(2,1)}, u32[]{:S(2)}, u32[]{:S(2)}) collective-permute-start(bf16[128,2048]{1,0:T(8,128)(2,1)} %bitcast.193), channel_id=1, source_target_pairs={{0,4},{2,6},{4,0},{6,2},{1,5},{3,7},{5,1},{7,3},{8,12},{10,14},{12... | collective-permute-start | bytes 1572872 | tf_op jit(solution)/shard_map/ppermute | solution.py:100
  3.7 39.3 %collective-permute-start.11 = (bf16[128,2048]{1,0:T(8,128)(2,1)}, bf16[128,2048]{1,0:T(8,128)(2,1)}, u32[]{:S(2)}, u32[]{:S(2)}) collective-permute-start(bf16[128,2048]{1,0:T(8,128)(2,1)} %bitcast.194), channel_id=1, source_target_pairs={{0,2},{2,0},{4,6},{6,4},{1,3},{3,1},{5,7},{7,5},{8,10},{10,8},{12,... | collective-permute-start | bytes 1572872 | tf_op jit(solution)/shard_map/ppermute | solution.py:100
  7.1 8.0 %copy-start.1 = (bf16[1,2048,1,384]{3,1,2,0:T(8,128)(2,1)S(1)}, bf16[1,2048,1,384]{3,1,2,0:T(8,128)(2,1)}, u32[]{:S(2)}) copy-start(bf16[1,2048,1,384]{3,1,2,0:T(8,128)(2,1)} %param.18) | copy-start | bytes 4718596
  7.1 8.0 %copy-start.3 = (bf16[1,1,128,2048]{3,2,1,0:T(8,128)(2,1)S(1)}, bf16[1,1,128,2048]{3,2,1,0:T(8,128)(2,1)}, u32[]{:S(2)}) copy-start(bf16[1,1,128,2048]{3,2,1,0:T(8,128)(2,1)} %param.11) | copy-start | bytes 1572868
  7.1 8.0 %copy-start.5 = (bf16[1,1,128,2048]{3,2,1,0:T(8,128)(2,1)S(1)}, bf16[1,1,128,2048]{3,2,1,0:T(8,128)(2,1)}, u32[]{:S(2)}) copy-start(bf16[1,1,128,2048]{3,2,1,0:T(8,128)(2,1)} %param.12) | copy-start | bytes 1572868
  12.9 15.0 %collective-permute-start.4 = (bf16[128,2048]{1,0:T(8,128)(2,1)}, bf16[128,2048]{1,0:T(8,128)(2,1)}, u32[]{:S(2)}, u32[]{:S(2)}) collective-permute-start(bf16[128,2048]{1,0:T(8,128)(2,1)} %get-tuple-element.61), channel_id=1, source_target_pairs={{0,4},{2,6},{4,0},{6,2},{1,5},{3,7},{5,1},{7,3},{8,12},{10,14},{12... | collective-permute-start | bytes 1572872 | tf_op jit(solution)/shard_map/ppermute | solution.py:100
  13.1 27.8 %collective-permute-start.3 = (bf16[128,2048]{1,0:T(8,128)(2,1)}, bf16[128,2048]{1,0:T(8,128)(2,1)}, u32[]{:S(2)}, u32[]{:S(2)}) collective-permute-start(bf16[128,2048]{1,0:T(8,128)(2,1)} %get-tuple-element.61), channel_id=1, source_target_pairs={{0,2},{2,0},{4,6},{6,4},{1,3},{3,1},{5,7},{7,5},{8,10},{10,8},{12,... | collective-permute-start | bytes 1572872 | tf_op jit(solution)/shard_map/ppermute | solution.py:100
  13.4 25.4 %collective-permute-start.1 = (bf16[128,2048]{1,0:T(8,128)(2,1)}, bf16[128,2048]{1,0:T(8,128)(2,1)}, u32[]{:S(2)}, u32[]{:S(2)}) collective-permute-start(bf16[128,2048]{1,0:T(8,128)(2,1)} %get-tuple-element.62), channel_id=1, source_target_pairs={{0,4},{2,6},{4,0},{6,2},{1,5},{3,7},{5,1},{7,3},{8,12},{10,14},{12... | collective-permute-start | bytes 1572872 | tf_op jit(solution)/shard_map/ppermute | solution.py:100
  21.4 17.4 %copy-start.2 = (bf16[1,2048,1,384]{3,1,2,0:T(8,128)(2,1)S(1)}, bf16[1,2048,1,384]{3,1,2,0:T(8,128)(2,1)}, u32[]{:S(2)}) copy-start(bf16[1,2048,1,384]{3,1,2,0:T(8,128)(2,1)} %param.18) | copy-start | bytes 4718596
  27.9 14.6 %collective-permute-start = (bf16[128,2048]{1,0:T(8,128)(2,1)}, bf16[128,2048]{1,0:T(8,128)(2,1)S(1)}, u32[]{:S(2)}, u32[]{:S(2)}) collective-permute-start(bf16[128,2048]{1,0:T(8,128)(2,1)} %get-tuple-element.62), channel_id=1, source_target_pairs={{0,2},{2,0},{4,6},{6,4},{1,3},{3,1},{5,7},{7,5},{8,10},{10,8},{12,... | collective-permute-start | bytes 1572872 | tf_op jit(solution)/shard_map/ppermute | solution.py:100
  38.7 14.3 %collective-permute-start.5 = (bf16[128,2048]{1,0:T(8,128)(2,1)}, bf16[128,2048]{1,0:T(8,128)(2,1)S(1)}, u32[]{:S(2)}, u32[]{:S(2)}) collective-permute-start(bf16[128,2048]{1,0:T(8,128)(2,1)} %collective-permute-done.4), channel_id=1, source_target_pairs={{0,2},{2,0},{4,6},{6,4},{1,3},{3,1},{5,7},{7,5},{8,10},{10,8},{12,... | collective-permute-start | bytes 1572872 | tf_op jit(solution)/shard_map/ppermute | solution.py:100
  40.3 10.8 %collective-permute-start.2 = (bf16[128,2048]{1,0:T(8,128)(2,1)}, bf16[128,2048]{1,0:T(8,128)(2,1)S(1)}, u32[]{:S(2)}, u32[]{:S(2)}) collective-permute-start(bf16[128,2048]{1,0:T(8,128)(2,1)} %collective-permute-done.1), channel_id=1, source_target_pairs={{0,2},{2,0},{4,6},{6,4},{1,3},{3,1},{5,7},{7,5},{8,10},{10,8},{12,... | collective-permute-start | bytes 1572872 | tf_op jit(solution)/shard_map/ppermute | solution.py:100
  40.9 7.6 %collective-permute-start.13 = (bf16[128,2048]{1,0:T(8,128)(2,1)}, bf16[128,2048]{1,0:T(8,128)(2,1)S(1)}, u32[]{:S(2)}, u32[]{:S(2)}) collective-permute-start(bf16[128,2048]{1,0:T(8,128)(2,1)} %collective-permute-done.12), channel_id=1, source_target_pairs={{0,2},{2,0},{4,6},{6,4},{1,3},{3,1},{5,7},{7,5},{8,10},{10,8},{12,... | collective-permute-start | bytes 1572872 | tf_op jit(solution)/shard_map/ppermute | solution.py:100
  56.1 6.0 %collective-permute-start.8 = (bf16[2,128,128]{2,1,0:T(8,128)(2,1)S(1)}, bf16[2,128,128]{2,1,0:T(8,128)(2,1)S(1)}, u32[]{:S(2)}, u32[]{:S(2)}) collective-permute-start(bf16[2,128,128]{2,1,0:T(8,128)(2,1)S(1)} %get-tuple-element.72), channel_id=1, source_target_pairs={{0,6},{2,4},{4,2},{6,0},{1,7},{3,5},{5,3},{7,1},{8,14},{10,12},{12... | collective-permute-start | bytes 196616 | tf_op jit(solution)/shard_map/ppermute | solution.py:100
  57.6 1.6 %collective-permute-start.6 = (bf16[2,128,128]{2,1,0:T(8,128)(2,1)S(1)}, bf16[2,128,128]{2,1,0:T(8,128)(2,1)S(1)}, u32[]{:S(2)}, u32[]{:S(2)}) collective-permute-start(bf16[2,128,128]{2,1,0:T(8,128)(2,1)S(1)} %get-tuple-element.74), channel_id=1, source_target_pairs={{0,2},{2,0},{4,6},{6,4},{1,3},{3,1},{5,7},{7,5},{8,10},{10,8},{12,... | collective-permute-start | bytes 196616 | tf_op jit(solution)/shard_map/ppermute | solution.py:100
  57.7 4.5 %copy-start.4 = (bf16[1,1,128,2048]{3,2,1,0:T(8,128)(2,1)S(1)}, bf16[1,1,128,2048]{3,2,1,0:T(8,128)(2,1)}, u32[]{:S(2)}) copy-start(bf16[1,1,128,2048]{3,2,1,0:T(8,128)(2,1)} %param.11) | copy-start | bytes 1572868
  57.7 4.4 %collective-permute-start.7 = (bf16[2,128,128]{2,1,0:T(8,128)(2,1)S(1)}, bf16[2,128,128]{2,1,0:T(8,128)(2,1)S(1)}, u32[]{:S(2)}, u32[]{:S(2)}) collective-permute-start(bf16[2,128,128]{2,1,0:T(8,128)(2,1)S(1)} %get-tuple-element.75), channel_id=1, source_target_pairs={{0,4},{2,6},{4,0},{6,2},{1,5},{3,7},{5,1},{7,3},{8,12},{10,14},{12... | collective-permute-start | bytes 196616 | tf_op jit(solution)/shard_map/ppermute | solution.py:100
  58.3 31.0 %collective-permute-start.14 = (bf16[128,2048]{1,0:T(8,128)(2,1)S(1)}, bf16[128,2048]{1,0:T(8,128)(2,1)S(1)}, u32[]{:S(2)}, u32[]{:S(2)}) collective-permute-start(bf16[128,2048]{1,0:T(8,128)(2,1)S(1)} %convolution_convert_fusion.2), channel_id=1, source_target_pairs={{0,2},{2,0},{4,6},{6,4},{1,3},{3,1},{5,7},{7,5},{8,10},{10,8},{12,... | collective-permute-start | bytes 1572872 | tf_op jit(solution)/shard_map/ppermute | solution.py:100
  58.5 7.9 %collective-permute-start.15 = (bf16[128,2048]{1,0:T(8,128)(2,1)S(1)}, bf16[128,2048]{1,0:T(8,128)(2,1)S(1)}, u32[]{:S(2)}, u32[]{:S(2)}) collective-permute-start(bf16[128,2048]{1,0:T(8,128)(2,1)S(1)} %convolution_convert_fusion), channel_id=1, source_target_pairs={{0,2},{2,0},{4,6},{6,4},{1,3},{3,1},{5,7},{7,5},{8,10},{10,8},{12,... | collective-permute-start | bytes 1572872 | tf_op jit(solution)/shard_map/ppermute | solution.py:100
  59.2 10.3 %collective-permute-start.19 = (bf16[128,1024]{1,0:T(8,128)(2,1)S(1)}, bf16[128,1024]{1,0:T(8,128)(2,1)S(1)}, u32[]{:S(2)}, u32[]{:S(2)}) collective-permute-start(bf16[128,1024]{1,0:T(8,128)(2,1)S(1)} %dynamic-slice_convert_fusion.1), channel_id=1, source_target_pairs={{0,1},{1,0},{2,3},{3,2},{4,5},{5,4},{6,7},{7,6},{8,9},{9,8},{10,11... | collective-permute-start | bytes 786440 | tf_op jit(solution)/shard_map/ppermute | solution.py:17
  62.7 16.7 %collective-permute-start.9 = (bf16[128,2048]{1,0:T(8,128)(2,1)S(1)}, bf16[128,2048]{1,0:T(8,128)(2,1)S(1)}, u32[]{:S(2)}, u32[]{:S(2)}) collective-permute-start(bf16[128,2048]{1,0:T(8,128)(2,1)S(1)} %fusion), channel_id=1, source_target_pairs={{0,8},{8,16},{16,24},{24,0},{1,9},{9,17},{17,25},{25,1},{2,10},{10... | collective-permute-start | bytes 1572872 | tf_op jit(solution)/shard_map/ppermute | solution.py:17
  64.8 3.6 %copy-start.9 = (bf16[1,1,512,2048]{3,2,1,0:T(8,128)(2,1)S(1)}, bf16[1,1,512,2048]{3,2,1,0:T(8,128)(2,1)}, u32[]{:S(2)}) copy-start(bf16[1,1,512,2048]{3,2,1,0:T(8,128)(2,1)} %param.14) | copy-start | bytes 6291460
  64.8 24.5 %collective-permute-start.10 = (bf16[128,2048]{1,0:T(8,128)(2,1)S(1)}, bf16[128,2048]{1,0:T(8,128)(2,1)S(1)}, u32[]{:S(2)}, u32[]{:S(2)}) collective-permute-start(bf16[128,2048]{1,0:T(8,128)(2,1)S(1)} %fusion.1), channel_id=1, source_target_pairs={{0,8},{8,16},{16,24},{24,0},{1,9},{9,17},{17,25},{25,1},{2,10},{10... | collective-permute-start | bytes 1572872 | tf_op jit(solution)/shard_map/ppermute | solution.py:17
  67.1 22.2 %collective-permute-start.16 = (bf16[128,2048]{1,0:T(8,128)(2,1)S(1)}, bf16[128,2048]{1,0:T(8,128)(2,1)S(1)}, u32[]{:S(2)}, u32[]{:S(2)}) collective-permute-start(bf16[128,2048]{1,0:T(8,128)(2,1)S(1)} %add_convert_fusion.1), channel_id=1, source_target_pairs={{0,4},{2,6},{4,0},{6,2},{1,5},{3,7},{5,1},{7,3},{8,12},{10,14},{12... | collective-permute-start | bytes 1572872 | tf_op jit(solution)/shard_map/ppermute | solution.py:100
  69.5 27.8 %collective-permute-start.18 = (bf16[1024,384]{0,1:T(8,128)(2,1)S(1)}, bf16[1024,384]{0,1:T(8,128)(2,1)S(1)}, u32[]{:S(2)}, u32[]{:S(2)}) collective-permute-start(bf16[1024,384]{0,1:T(8,128)(2,1)S(1)} %fusion.88), channel_id=1, source_target_pairs={{0,1},{1,0},{2,3},{3,2},{4,5},{5,4},{6,7},{7,6},{8,9},{9,8},{10,11... | collective-permute-start | bytes 2359304 | tf_op jit(solution)/shard_map/ppermute | solution.py:17
  89.3 3.4 %copy-start.7 = (bf16[1,1,128,2048]{3,2,1,0:T(8,128)(2,1)S(1)}, bf16[1,1,128,2048]{3,2,1,0:T(8,128)(2,1)}, u32[]{:S(2)}) copy-start(bf16[1,1,128,2048]{3,2,1,0:T(8,128)(2,1)} %param.13) | copy-start | bytes 1572868
  89.3 3.4 %copy-start.14 = (f32[1,1,128]{2,1,0:T(1,128)S(1)}, f32[1,1,128]{2,1,0:T(1,128)}, u32[]{:S(2)}) copy-start(f32[1,1,128]{2,1,0:T(1,128)} %param.15) | copy-start | bytes 1540
  90.2 1.2 %collective-permute-start.20 = (f32[2,2048]{1,0:T(2,128)S(1)}, f32[2,2048]{1,0:T(2,128)S(1)}, u32[]{:S(2)}, u32[]{:S(2)}) collective-permute-start(f32[2,2048]{1,0:T(2,128)S(1)} %pad_maximum_fusion.4), channel_id=1, source_target_pairs={{0,2},{2,0},{4,6},{6,4},{1,3},{3,1},{5,7},{7,5},{8,10},{10,8},{12,... | collective-permute-start | bytes 49160 | tf_op jit(solution)/shard_map/ppermute | solution.py:100
  91.5 4.3 %collective-permute-start.21 = (f32[2,2048]{1,0:T(2,128)S(1)}, f32[2,2048]{1,0:T(2,128)S(1)}, u32[]{:S(2)}, u32[]{:S(2)}) collective-permute-start(f32[2,2048]{1,0:T(2,128)S(1)} %fusion.163), channel_id=1, source_target_pairs={{0,4},{2,6},{4,0},{6,2},{1,5},{3,7},{5,1},{7,3},{8,12},{10,14},{12... | collective-permute-start | bytes 49160 | tf_op jit(solution)/shard_map/ppermute | solution.py:100
  94.0 14.0 %collective-permute-start.17 = (bf16[128,2048]{1,0:T(8,128)(2,1)}, bf16[128,2048]{1,0:T(8,128)(2,1)}, u32[]{:S(2)}, u32[]{:S(2)}) collective-permute-start(bf16[128,2048]{1,0:T(8,128)(2,1)} %add_convert_fusion), channel_id=1, source_target_pairs={{0,24},{8,0},{16,8},{24,16},{1,25},{9,1},{17,9},{25,17},{2,26},{10... | collective-permute-start | bytes 1572872 | tf_op jit(solution)/shard_map/ppermute | solution.py:17
  95.8 7.8 %collective-permute-start.22 = (f32[2,2048]{1,0:T(2,128)S(1)}, f32[2,2048]{1,0:T(2,128)S(1)}, u32[]{:S(2)}, u32[]{:S(2)}) collective-permute-start(f32[2,2048]{1,0:T(2,128)S(1)} %fusion.190), channel_id=1, source_target_pairs={{0,1},{1,0},{2,3},{3,2},{4,5},{5,4},{6,7},{7,6},{8,9},{9,8},{10,11... | collective-permute-start | bytes 49160 | tf_op jit(solution)/shard_map/ppermute | solution.py:100
  (6 other events, 8.7 us)

commit v2 on v1

--- a/solution.py
+++ b/solution.py
@@ -100,14 +100,15 @@
     return lax.ppermute(value, axis, [(source, source ^ mask) for source in range(count)])
 
 
-def gathered(value):
-    count = lax.axis_size("seq")
-    pieces = {0: value}
-    for mask in range(2, count, 2):
-        pieces[mask] = swapped(value, "seq", mask)
-    for mask in range(1, count, 2):
-        pieces[mask] = swapped(pieces[mask ^ 1], "seq", 1)
-    return [pieces[mask] for mask in range(count)]
+def from_chips(value):
+    return [swapped(value, "seq", mask) for mask in range(2, lax.axis_size("seq"), 2)]
+
+
+def gathered(value, others):
+    pieces = []
+    for piece in [value] + others:
+        pieces += [piece, swapped(piece, "seq", 1)]
+    return pieces
 
 
 def summed_to_owner(terms):
@@ -172,7 +173,7 @@
     rows = cot_rows.shape[0]
     owners = [jnp.bitwise_xor(me, mask) for mask in range(count)]
 
-    cot_pieces = gathered(cot_rows)
+    cot_far = from_chips(cot_rows)
     moment = moments[0]
     hidden = layer_input[0, 0].astype(jnp.float32)
     tangent = tangent_input[0, 0].astype(jnp.float32)
@@ -184,8 +185,9 @@
     tan_modulated = jnp.cos(moment) * scales
     normed = (normal * modulated).astype(jnp.bfloat16)
     tan_normed = (tan_normal * modulated + normal * tan_modulated).astype(jnp.bfloat16)
-    normed_pieces = gathered(normed)
-    tan_pieces = gathered(tan_normed)
+    normed, tan_normed, cot_far = lax.optimization_barrier((normed, tan_normed, cot_far))
+    cot_pieces = gathered(cot_rows, cot_far)
+    normed_far = from_chips(normed)
 
     grad_out = jnp.zeros((rows * count, head_size), jnp.bfloat16)
     for mask in range(count):
@@ -200,6 +202,11 @@
         grad_out,
     )
     grad_proj = jnp.concatenate([grad_q, grad_k, grad_v], -1).astype(jnp.bfloat16)
+    tan_normed, normed_far, grad_proj, attended_b = lax.optimization_barrier(
+        (tan_normed, normed_far, grad_proj, attended_b)
+    )
+    tan_far = from_chips(tan_normed)
+    normed_pieces = gathered(normed, normed_far)
     terms = {}
     for mask in reversed(range(count)):
         piece = lax.dynamic_slice_in_dim(grad_proj, owners[mask] * rows, rows, 0)
@@ -228,7 +235,7 @@
         )
 
     proj = projected(normed_pieces)
-    tan_proj = projected(tan_pieces)
+    tan_proj = projected(gathered(tan_normed, tan_far))
     attended, tan_attended = attend_tangent(
         proj[:, :head_size],
         proj[:, head_size : 2 * head_size],
@@ -237,17 +244,20 @@
         tan_proj[:, head_size : 2 * head_size],
         tan_proj[:, 2 * head_size :],
     )
-    both = jnp.stack([attended, tan_attended])
-    moved = jnp.zeros((2, rows, heads * head_size), jnp.bfloat16)
-    for mask in range(count):
-        piece = both[:, mask * rows : (mask + 1) * rows]
-        if mask:
-            piece = swapped(piece, "seq", mask)
-        moved = lax.dynamic_update_slice_in_dim(moved, piece, owners[mask] * head_size, 2)
-    result = hidden + jnp.dot(moved[0], output_flat, preferred_element_type=jnp.float32)
-    next_input = passed_along(result.astype(jnp.bfloat16), "section", 1)
-    result = tangent + jnp.dot(moved[1], output_flat, preferred_element_type=jnp.float32)
-    next_tangent = passed_along(result.astype(jnp.bfloat16), "section", 1)
+    def to_rows(value):
+        moved = jnp.zeros((rows, heads * head_size), jnp.bfloat16)
+        for mask in range(count):
+            piece = value[mask * rows : (mask + 1) * rows]
+            if mask:
+                piece = swapped(piece, "seq", mask)
+            moved = lax.dynamic_update_slice_in_dim(moved, piece, owners[mask] * head_size, 1)
+        return jnp.dot(moved, output_flat, preferred_element_type=jnp.float32)
+
+    result = (hidden + to_rows(attended)).astype(jnp.bfloat16)
+    next_input = passed_along(result, "section", 1)
+    tan_result = (tangent + to_rows(tan_attended)).astype(jnp.bfloat16)
+    tan_result, grad_late = lax.optimization_barrier((tan_result, grad_normed))
+    next_tangent = passed_along(tan_result, "section", 1)
 
     moment = moments[1]
     own_normed = lax.dynamic_slice_in_dim(normed_all, me * rows, rows, 0)
@@ -259,7 +269,7 @@
     )
     cotangent = (cot_rows.astype(jnp.float32) + grad_hidden).astype(jnp.bfloat16)
     cot_prev = passed_along(cotangent, "section", -1)
-    gain_part = jnp.sum(grad_normed * normal_b, 0)
+    gain_part = jnp.sum(grad_late * normal_b, 0)
     norm_total = summed_everywhere(jnp.stack([gain_part, jnp.sin(moment) * gain_part]))
     return (
         next_input[None, None],

time: 112 us -> 119 us (1.062)
  local copies, waits for them, and re-layouts: 10.1 us -> 18.8 us
  waiting for transfers between devices: 37.6 us -> 33.2 us
  matrix products: 28.2 us -> 29.9 us
    unnamed x34 -> x36, local copies, waits for them, and re-layouts: 9.23 us -> 12.2 us
    convert_element_type x0 -> x2, local copies, waits for them, and re-layouts: none -> 2.94 us  [local(): piece = jnp.einsum('td,hd->th', cot_pieces[mask], output_head, preferred_...]
    dynamic_update_slice x3 -> x8, local copies, waits for them, and re-layouts: 0.06 us -> 2.83 us  [the longest x2 2.75 us: local(): lax.dynamic_update_slice_in_dim(grad_out, piece, owners[mask] * rows, 0)]
    ppermute x18 -> x21, waiting for transfers between devices: 16.3 us -> 14 us  [swapped(): lax.ppermute(value, axis, [(source, source ^ mask) for source in range(co...]
    ppermute x5, waiting for transfers between devices: 21.2 us -> 19.2 us  [passed_along(): return lax.ppermute(value, axis, pairs)]
    dot_general x4, matrix products: 4.57 us -> 6.2 us  [local(): jnp.einsum('td,hd->th', cot_pieces[mask], output_head, preferred_element_...]
    ppermute x18 -> x21, starting transfers between devices: 12.8 us -> 13.3 us  [swapped(): lax.ppermute(value, axis, [(source, source ^ mask) for source in range(co...]
  transfers between devices with their start and end apart: 23 -> 26, of which waited for: 7 -> 9; matrix products, arithmetic and copies ran while one was open for 38% -> 44% of each run, Pallas kernels for 0% -> 0%
where the time goes in v2:
time: 119 us; the launch traced here: 118 us
  waiting for transfers between devices  33.2 us (28%)
  matrix products  29.9 us (25%)
  starting transfers between devices  21.7 us (18%)
  local copies, waits for them, and re-layouts  18.8 us (16%)
  other arithmetic  11 us (9%)
  between operations  3.45 us (3%)
    ppermute x5, waiting for transfers between devices, passed_along(): return lax.ppermute(value, axis, pairs)  19.2 us
    ppermute x21, waiting for transfers between devices, swapped(): lax.ppermute(value, axis, [(source, source ^ mask) for source in range(co...  14 us
    ppermute x21, starting transfers between devices, swapped(): lax.ppermute(value, axis, [(source, source ^ mask) for source in range(co...  13.3 us
    unnamed x36, local copies, waits for them, and re-layouts  12.2 us
    ppermute x5, starting transfers between devices, passed_along(): return lax.ppermute(value, axis, pairs)  8.42 us
    dot_general x8, matrix products, projected(): jnp.dot(piece, weight_heads, preferred_element_type=jnp.float32)  8.02 us
    dot_general x4, matrix products, local(): jnp.einsum('td,hd->th', cot_pieces[mask], output_head, preferred_element_...  6.2 us
    dot_general x4, matrix products, local(): jnp.einsum('th,td->hd', piece, cot_pieces[mask], preferred_element_type=j...  4.45 us
  transfers between devices with their start and end apart: 26, of which 9 were waited for; matrix products, arithmetic and copies ran while one was open for 44% of the time, Pallas kernels for 0%

profile of v2, /device:TPU:0, one launch (start us, length us, event | category | flops | bytes accessed | tf_op | source)
XLA Modules:
  0.0 118.0 jit_solution(15085026313615546724)
XLA Ops:
  1.2 2.6 %collective-permute-start = (bf16[128,2048]{1,0:T(8,128)(2,1)}, bf16[128,2048]{1,0:T(8,128)(2,1)}, u32[]{:S(2)}, u32[]{:S(2)}) collective-permute-start(bf16[128,2048]{1,0:T(8,128)(2,1)} %bitcast.139), channel_id=1, source_target_pairs={{0,4},{2,6},{4,0},{6,2},{1,5},{3,7},{5,1},{7,3},{8,12},{10,14},{12... | collective-permute-start | bytes 1572872 | tf_op jit(solution)/shard_map/ppermute | solution.py:100
  8.5 1.5 %fusion.70 = (f32[128]{0:T(128)S(1)}, f32[128]{0:T(128)S(1)}) fusion(bf16[1,1,128,2048]{3,2,1,0:T(8,128)(2,1)} %param.12, bf16[1,1,128,2048]{3,2,1,0:T(8,128)(2,1)} %param.11), kind=kLoop, calls=%fused_computation.82 | loop fusion | flops 1572608 | bytes 1049600 | tf_op jit(solution)/shard_map/reduce_sum | solution.py:182
  10.1 3.3 %fusion.66 = (bf16[128,2048]{1,0:T(8,128)(2,1)}, bf16[128,2048]{1,0:T(8,128)(2,1)}) fusion(bf16[1,1,128,2048]{3,2,1,0:T(8,128)(2,1)} %param.12, bf16[1,1,128,2048]{3,2,1,0:T(8,128)(2,1)} %param.11, f32[2048]{0:T(1024)S(1)} %bitcast.152, f32[128]{0:T(128)S(1)} %get-tuple-element.103, f32[2048]{0:T(1024)S(1)} %bitcast.151, f32[128]{0:T(128)S(1)} %get-tuple-element.104), kind=kLoop, calls=%fused_computation.78 | loop fusion | flops 3145728 | bytes 2114560 | tf_op jit(solution)/shard_map/convert_element_type | solution.py:187
  16.6 1.8 %collective-permute-start.2 = (bf16[128,2048]{1,0:T(8,128)(2,1)}, bf16[128,2048]{1,0:T(8,128)(2,1)}, u32[]{:S(2)}, u32[]{:S(2)}) collective-permute-start(bf16[128,2048]{1,0:T(8,128)(2,1)} %get-tuple-element.60), channel_id=1, source_target_pairs={{0,4},{2,6},{4,0},{6,2},{1,5},{3,7},{5,1},{7,3},{8,12},{10,14},{12... | collective-permute-start | bytes 1572872 | tf_op jit(solution)/shard_map/ppermute | solution.py:100
  18.9 2.0 %convolution_convert_fusion.10 = bf16[128,128]{1,0:T(8,128)(2,1)} fusion(bf16[128,2048]{1,0:T(8,128)(2,1)} %collective-permute-done, bf16[1,4,128,2048]{3,2,1,0:T(8,128)(2,1)S(1)} %copy-done, s32[]{:T(128)S(6)} %select_n.16), kind=kOutput, calls=%fused_computation.69 | convolution fusion | flops 67125248 | bytes 1081348 | tf_op jit(solution)/shard_map/td,hd->th/dot_general | solution.py:194
  20.8 1.5 %copy.17 = bf16[128,128]{0,1:T(8,128)(2,1)} copy(bf16[128,128]{1,0:T(8,128)(2,1)} %convolution_convert_fusion.10) | data formatting | bytes 65536 | tf_op jit(solution)/shard_map/convert_element_type | solution.py:196
  22.3 2.0 %fusion.63 = bf16[512,128]{0,1:T(8,128)(2,1)} fusion(bf16[512,128]{0,1:T(8,128)(2,1)} %copy-done.11, s32[]{:T(128)S(6)} %select_n.18, bf16[128,2048]{1,0:T(8,128)(2,1)} %collective-permute-done.3, bf16[1,4,128,2048]{3,2,1,0:T(8,128)(2,1)S(1)} %copy-done, s32[]{:T(128)S(6)} %select_n.16), kind=kOutput, calls=%fused_computation.75 | convolution fusion | flops 67125248 | bytes 1081352 | tf_op jit(solution)/shard_map/td,hd->th/dot_general | solution.py:194
  24.3 1.4 %constant_dynamic-update-slice_fusion.7 = bf16[512,128]{0,1:T(8,128)(2,1)} fusion(bf16[512,128]{0,1:T(8,128)(2,1)} %fusion.63, bf16[128,128]{0,1:T(8,128)(2,1)} %copy.17, s32[]{:T(128)S(6)} %select_n.19), kind=kLoop, calls=%fused_computation.166 | loop fusion | bytes 65540 | tf_op jit(solution)/shard_map/dynamic_update_slice | solution.py:197
  25.7 2.7 %fusion.36 = bf16[128,384]{1,0:T(8,128)(2,1)} fusion(bf16[128,2048]{1,0:T(8,128)(2,1)} %get-tuple-element.60, bf16[1,2048,1,384]{3,1,2,0:T(8,128)(2,1)} %param.18), kind=kOutput, calls=%fused_computation.60 | convolution fusion | flops 201375744 | bytes 2195456 | tf_op jit(solution)/shard_map/dot_general | solution.py:230
  28.3 2.0 %convolution_convert_fusion.9 = bf16[128,128]{1,0:T(8,128)(2,1)} fusion(bf16[128,2048]{1,0:T(8,128)(2,1)} %collective-permute-done.4, bf16[1,4,128,2048]{3,2,1,0:T(8,128)(2,1)S(1)} %copy-done, s32[]{:T(128)S(6)} %select_n.16), kind=kOutput, calls=%fused_computation.68 | convolution fusion | flops 67125248 | bytes 1081348 | tf_op jit(solution)/shard_map/td,hd->th/dot_general | solution.py:194
  30.3 1.5 %copy.18 = bf16[128,128]{0,1:T(8,128)(2,1)} copy(bf16[128,128]{1,0:T(8,128)(2,1)} %convolution_convert_fusion.9) | data formatting | bytes 65536 | tf_op jit(solution)/shard_map/convert_element_type | solution.py:196
  31.7 1.4 %constant_dynamic-update-slice_fusion.6 = bf16[512,128]{0,1:T(8,128)(2,1)} fusion(bf16[512,128]{0,1:T(8,128)(2,1)} %constant_dynamic-update-slice_fusion.7, bf16[128,128]{0,1:T(8,128)(2,1)} %copy.18, s32[]{:T(128)S(6)} %select_n.20), kind=kLoop, calls=%fused_computation.165 | loop fusion | bytes 65540 | tf_op jit(solution)/shard_map/dynamic_update_slice | solution.py:197
  36.7 1.5 %fusion.42 = bf16[128,384]{1,0:T(8,128)(2,1)S(1)} fusion(bf16[128,2048]{1,0:T(8,128)(2,1)} %collective-permute-done.2, bf16[1,2048,1,384]{3,1,2,0:T(8,128)(2,1)S(1)} %copy-done.1), kind=kOutput, calls=%fused_computation.62 | convolution fusion | flops 201375744 | bytes 2195456 | tf_op jit(solution)/shard_map/dot_general | solution.py:230
  42.5 1.4 %fusion = f32[128,2048]{1,0:T(8,128)S(1)} fusion(f32[128,2048]{1,0:T(8,128)S(1)} %fusion.111, f32[128,2048]{1,0:T(8,128)S(1)} %convolution_add_fusion.1, bf16[128,2048]{1,0:T(8,128)(2,1)} %collective-permute-done, bf16[512,128]{1,0:T(8,128)(2,1)S(1)} %copy-done.10, s32[]{:T(128)S(6)} %select_n.19), kind=kOutput, calls=%fused_computation.1 | convolution fusion | flops 67633152 | bytes 3702788 | tf_op jit(solution)/shard_map/th,td->hd/dot_general | solution.py:221
  43.9 1.7 %collective-permute-start.22 = (bf16[128,1024]{1,0:T(8,128)(2,1)S(1)}, bf16[128,1024]{1,0:T(8,128)(2,1)S(1)}, u32[]{:S(2)}, u32[]{:S(2)}) collective-permute-start(bf16[128,1024]{1,0:T(8,128)(2,1)S(1)} %dynamic-slice_convert_fusion.1), channel_id=1, source_target_pairs={{0,1},{1,0},{2,3},{3,2},{4,5},{5,4},{6,7},{7,6},{8,9},{9,8},{10,11... | collective-permute-start | bytes 786440 | tf_op jit(solution)/shard_map/ppermute | solution.py:17
  47.4 1.5 %fusion.39 = bf16[128,384]{1,0:T(8,128)(2,1)S(1)} fusion(bf16[128,2048]{1,0:T(8,128)(2,1)} %collective-permute-done.1, bf16[1,2048,1,384]{3,1,2,0:T(8,128)(2,1)S(1)} %copy-done.1), kind=kOutput, calls=%fused_computation.61 | convolution fusion | flops 201375744 | bytes 2195456 | tf_op jit(solution)/shard_map/dot_general | solution.py:230
  49.7 2.7 %collective-permute-done.22 = bf16[128,1024]{1,0:T(8,128)(2,1)S(1)} collective-permute-done((bf16[128,1024]{1,0:T(8,128)(2,1)S(1)}, bf16[128,1024]{1,0:T(8,128)(2,1)S(1)}, u32[]{:S(2)}, u32[]{:S(2)}) %collective-permute-start.22) | collective-permute-done | bytes 262176 | tf_op jit(solution)/shard_map/ppermute | solution.py:17
  53.3 1.7 %collective-permute-start.21 = (bf16[1024,384]{0,1:T(8,128)(2,1)S(1)}, bf16[1024,384]{0,1:T(8,128)(2,1)S(1)}, u32[]{:S(2)}, u32[]{:S(2)}) collective-permute-start(bf16[1024,384]{0,1:T(8,128)(2,1)S(1)} %fusion.75), channel_id=1, source_target_pairs={{0,1},{1,0},{2,3},{3,2},{4,5},{5,4},{6,7},{7,6},{8,9},{9,8},{10,11... | collective-permute-start | bytes 2359304 | tf_op jit(solution)/shard_map/ppermute | solution.py:17
  55.7 1.6 %collective-permute-start.18 = (bf16[128,2048]{1,0:T(8,128)(2,1)S(1)}, bf16[128,2048]{1,0:T(8,128)(2,1)S(1)}, u32[]{:S(2)}, u32[]{:S(2)}) collective-permute-start(bf16[128,2048]{1,0:T(8,128)(2,1)S(1)} %fusion.5), channel_id=1, source_target_pairs={{0,4},{2,6},{4,0},{6,2},{1,5},{3,7},{5,1},{7,3},{8,12},{10,14},{12... | collective-permute-start | bytes 1572872 | tf_op jit(solution)/shard_map/ppermute | solution.py:100
  60.8 1.5 %collective-permute-start.7 = (bf16[128,128]{1,0:T(8,128)(2,1)S(1)}, bf16[128,128]{1,0:T(8,128)(2,1)S(1)}, u32[]{:S(2)}, u32[]{:S(2)}) collective-permute-start(bf16[128,128]{1,0:T(8,128)(2,1)S(1)} %get-tuple-element.95), channel_id=1, source_target_pairs={{0,4},{2,6},{4,0},{6,2},{1,5},{3,7},{5,1},{7,3},{8,12},{10,14},{12... | collective-permute-start | bytes 98312 | tf_op jit(solution)/shard_map/ppermute | solution.py:100
  62.3 8.9 %collective-permute-done.7 = bf16[128,128]{1,0:T(8,128)(2,1)S(1)} collective-permute-done((bf16[128,128]{1,0:T(8,128)(2,1)S(1)}, bf16[128,128]{1,0:T(8,128)(2,1)S(1)}, u32[]{:S(2)}, u32[]{:S(2)}) %collective-permute-start.7) | collective-permute-done | bytes 32800 | tf_op jit(solution)/shard_map/ppermute | solution.py:100
  71.8 1.6 %collective-permute-start.9 = (bf16[128,2048]{1,0:T(8,128)(2,1)S(1)}, bf16[128,2048]{1,0:T(8,128)(2,1)}, u32[]{:S(2)}, u32[]{:S(2)}) collective-permute-start(bf16[128,2048]{1,0:T(8,128)(2,1)S(1)} %fusion.1), channel_id=1, source_target_pairs={{0,8},{8,16},{16,24},{24,0},{1,9},{9,17},{17,25},{25,1},{2,10},{10... | collective-permute-start | bytes 1572872 | tf_op jit(solution)/shard_map/ppermute | solution.py:17
  75.5 1.4 %collective-permute-start.15 = (bf16[128,128]{1,0:T(8,128)(2,1)S(1)}, bf16[128,128]{1,0:T(8,128)(2,1)S(1)}, u32[]{:S(2)}, u32[]{:S(2)}) collective-permute-start(bf16[128,128]{1,0:T(8,128)(2,1)S(1)} %get-tuple-element.90), channel_id=1, source_target_pairs={{0,6},{2,4},{4,2},{6,0},{1,7},{3,5},{5,3},{7,1},{8,14},{10,12},{12... | collective-permute-start | bytes 98312 | tf_op jit(solution)/shard_map/ppermute | solution.py:100
  78.6 2.2 %collective-permute-done.14 = bf16[128,128]{1,0:T(8,128)(2,1)S(1)} collective-permute-done((bf16[128,128]{1,0:T(8,128)(2,1)S(1)}, bf16[128,128]{1,0:T(8,128)(2,1)S(1)}, u32[]{:S(2)}, u32[]{:S(2)}) %collective-permute-start.14) | collective-permute-done | bytes 32800 | tf_op jit(solution)/shard_map/ppermute | solution.py:100
  85.1 3.3 %collective-permute-start.20 = (bf16[128,2048]{1,0:T(8,128)(2,1)}, bf16[128,2048]{1,0:T(8,128)(2,1)}, u32[]{:S(2)}, u32[]{:S(2)}) collective-permute-start(bf16[128,2048]{1,0:T(8,128)(2,1)} %add_convert_fusion), channel_id=1, source_target_pairs={{0,24},{8,0},{16,8},{24,16},{1,25},{9,1},{17,9},{25,17},{2,26},{10... | collective-permute-start | bytes 1572872 | tf_op jit(solution)/shard_map/ppermute | solution.py:17
  89.1 1.4 %fusion.11 = f32[1,1024,1,384]{1,3,2,0:T(8,128)} fusion(bf16[1024,384]{0,1:T(8,128)(2,1)S(1)} %collective-permute-done.21, f32[384,2048]{1,0:T(8,128)S(1)} %fusion.9, s32[]{:T(128)S(6)} %select_n.21), kind=kLoop, calls=%fused_computation.24 | loop fusion | flops 786432 | bytes 3932164 | tf_op jit(solution)/shard_map/broadcast_in_dim | solution.py:278
  90.5 4.8 %copy.19 = f32[1,1024,1,384]{3,2,1,0:T(1,128)} copy(f32[1,1024,1,384]{1,3,2,0:T(8,128)} %fusion.11) | data formatting | bytes 3145728
  95.9 5.2 %collective-permute-done.20 = bf16[128,2048]{1,0:T(8,128)(2,1)} collective-permute-done((bf16[128,2048]{1,0:T(8,128)(2,1)}, bf16[128,2048]{1,0:T(8,128)(2,1)}, u32[]{:S(2)}, u32[]{:S(2)}) %collective-permute-start.20) | collective-permute-done | bytes 524320 | tf_op jit(solution)/shard_map/ppermute | solution.py:17
  101.0 11.3 %collective-permute-done.19 = bf16[128,2048]{1,0:T(8,128)(2,1)} collective-permute-done((bf16[128,2048]{1,0:T(8,128)(2,1)S(1)}, bf16[128,2048]{1,0:T(8,128)(2,1)}, u32[]{:S(2)}, u32[]{:S(2)}) %collective-permute-start.19) | collective-permute-done | bytes 524320 | tf_op jit(solution)/shard_map/ppermute | solution.py:17
  112.4 1.9 %copy.35 = bf16[1,1,128,2048]{3,2,1,0:T(8,128)(2,1)} copy(bf16[1,1,128,2048]{3,2,1,0:T(8,128)(2,1)} %bitcast.15) | data formatting | bytes 1048576
  114.2 1.9 %copy.36 = bf16[1,1,128,2048]{3,2,1,0:T(8,128)(2,1)} copy(bf16[1,1,128,2048]{3,2,1,0:T(8,128)(2,1)} %bitcast.16) | data formatting | bytes 1048576
  116.1 1.9 %copy.37 = bf16[1,1,128,2048]{3,2,1,0:T(8,128)(2,1)} copy(bf16[1,1,128,2048]{3,2,1,0:T(8,128)(2,1)} %bitcast.21) | data formatting | bytes 1048576
  (130 shorter events, 31.7 us)
Async XLA Ops:
  0.6 12.8 %copy-start = (bf16[1,4,128,2048]{3,2,1,0:T(8,128)(2,1)S(1)}, bf16[1,4,128,2048]{3,2,1,0:T(8,128)(2,1)}, u32[]{:S(2)}) copy-start(bf16[1,4,128,2048]{3,2,1,0:T(8,128)(2,1)} %param.19) | copy-start | bytes 6291460
  0.6 9.4 %copy-start.14 = (f32[1,2048]{1,0:T(1,128)S(1)}, f32[1,2048]{1,0:T(1,128)}, u32[]{:S(2)}) copy-start(f32[1,2048]{1,0:T(1,128)} %param.21) | copy-start | bytes 24580
  0.7 9.4 %copy-start.13 = (f32[1,2048]{1,0:T(1,128)S(1)}, f32[1,2048]{1,0:T(1,128)}, u32[]{:S(2)}) copy-start(f32[1,2048]{1,0:T(1,128)} %param.20) | copy-start | bytes 24580
  0.7 21.6 %collective-permute-start.3 = (bf16[128,2048]{1,0:T(8,128)(2,1)}, bf16[128,2048]{1,0:T(8,128)(2,1)}, u32[]{:S(2)}, u32[]{:S(2)}) collective-permute-start(bf16[128,2048]{1,0:T(8,128)(2,1)} %bitcast.138), channel_id=1, source_target_pairs={{0,2},{2,0},{4,6},{6,4},{1,3},{3,1},{5,7},{7,5},{8,10},{10,8},{12,... | collective-permute-start | bytes 1572872 | tf_op jit(solution)/shard_map/ppermute | solution.py:100
  1.2 15.4 %collective-permute-start = (bf16[128,2048]{1,0:T(8,128)(2,1)}, bf16[128,2048]{1,0:T(8,128)(2,1)}, u32[]{:S(2)}, u32[]{:S(2)}) collective-permute-start(bf16[128,2048]{1,0:T(8,128)(2,1)} %bitcast.139), channel_id=1, source_target_pairs={{0,4},{2,6},{4,0},{6,2},{1,5},{3,7},{5,1},{7,3},{8,12},{10,14},{12... | collective-permute-start | bytes 1572872 | tf_op jit(solution)/shard_map/ppermute | solution.py:100
  8.5 5.0 %copy-start.4 = (bf16[1,1,128,2048]{3,2,1,0:T(8,128)(2,1)S(1)}, bf16[1,1,128,2048]{3,2,1,0:T(8,128)(2,1)}, u32[]{:S(2)}) copy-start(bf16[1,1,128,2048]{3,2,1,0:T(8,128)(2,1)} %param.13) | copy-start | bytes 1572868
  16.6 19.1 %collective-permute-start.2 = (bf16[128,2048]{1,0:T(8,128)(2,1)}, bf16[128,2048]{1,0:T(8,128)(2,1)}, u32[]{:S(2)}, u32[]{:S(2)}) collective-permute-start(bf16[128,2048]{1,0:T(8,128)(2,1)} %get-tuple-element.60), channel_id=1, source_target_pairs={{0,4},{2,6},{4,0},{6,2},{1,5},{3,7},{5,1},{7,3},{8,12},{10,14},{12... | collective-permute-start | bytes 1572872 | tf_op jit(solution)/shard_map/ppermute | solution.py:100
  18.4 28.9 %collective-permute-start.1 = (bf16[128,2048]{1,0:T(8,128)(2,1)}, bf16[128,2048]{1,0:T(8,128)(2,1)}, u32[]{:S(2)}, u32[]{:S(2)}) collective-permute-start(bf16[128,2048]{1,0:T(8,128)(2,1)} %get-tuple-element.60), channel_id=1, source_target_pairs={{0,2},{2,0},{4,6},{6,4},{1,3},{3,1},{5,7},{7,5},{8,10},{10,8},{12,... | collective-permute-start | bytes 1572872 | tf_op jit(solution)/shard_map/ppermute | solution.py:100
  18.4 9.9 %collective-permute-start.4 = (bf16[128,2048]{1,0:T(8,128)(2,1)}, bf16[128,2048]{1,0:T(8,128)(2,1)}, u32[]{:S(2)}, u32[]{:S(2)}) collective-permute-start(bf16[128,2048]{1,0:T(8,128)(2,1)} %collective-permute-done), channel_id=1, source_target_pairs={{0,2},{2,0},{4,6},{6,4},{1,3},{3,1},{5,7},{7,5},{8,10},{10,8},{12,... | collective-permute-start | bytes 1572872 | tf_op jit(solution)/shard_map/ppermute | solution.py:100
  38.2 17.5 %collective-permute-start.5 = (bf16[128,2048]{1,0:T(8,128)(2,1)}, bf16[128,2048]{1,0:T(8,128)(2,1)S(1)}, u32[]{:S(2)}, u32[]{:S(2)}) collective-permute-start(bf16[128,2048]{1,0:T(8,128)(2,1)} %collective-permute-done.2), channel_id=1, source_target_pairs={{0,2},{2,0},{4,6},{6,4},{1,3},{3,1},{5,7},{7,5},{8,10},{10,8},{12,... | collective-permute-start | bytes 1572872 | tf_op jit(solution)/shard_map/ppermute | solution.py:100
  38.7 20.0 %collective-permute-start.11 = (bf16[128,2048]{1,0:T(8,128)(2,1)S(1)}, bf16[128,2048]{1,0:T(8,128)(2,1)S(1)}, u32[]{:S(2)}, u32[]{:S(2)}) collective-permute-start(bf16[128,2048]{1,0:T(8,128)(2,1)S(1)} %copy-done.7), channel_id=1, source_target_pairs={{0,4},{2,6},{4,0},{6,2},{1,5},{3,7},{5,1},{7,3},{8,12},{10,14},{12... | collective-permute-start | bytes 1572872 | tf_op jit(solution)/shard_map/ppermute | solution.py:100
  39.1 20.3 %collective-permute-start.10 = (bf16[128,2048]{1,0:T(8,128)(2,1)S(1)}, bf16[128,2048]{1,0:T(8,128)(2,1)S(1)}, u32[]{:S(2)}, u32[]{:S(2)}) collective-permute-start(bf16[128,2048]{1,0:T(8,128)(2,1)S(1)} %copy-done.7), channel_id=1, source_target_pairs={{0,2},{2,0},{4,6},{6,4},{1,3},{3,1},{5,7},{7,5},{8,10},{10,8},{12,... | collective-permute-start | bytes 1572872 | tf_op jit(solution)/shard_map/ppermute | solution.py:100
  43.9 8.5 %collective-permute-start.22 = (bf16[128,1024]{1,0:T(8,128)(2,1)S(1)}, bf16[128,1024]{1,0:T(8,128)(2,1)S(1)}, u32[]{:S(2)}, u32[]{:S(2)}) collective-permute-start(bf16[128,1024]{1,0:T(8,128)(2,1)S(1)} %dynamic-slice_convert_fusion.1), channel_id=1, source_target_pairs={{0,1},{1,0},{2,3},{3,2},{4,5},{5,4},{6,7},{7,6},{8,9},{9,8},{10,11... | collective-permute-start | bytes 786440 | tf_op jit(solution)/shard_map/ppermute | solution.py:17
  47.3 6.0 %collective-permute-start.17 = (bf16[128,2048]{1,0:T(8,128)(2,1)S(1)}, bf16[128,2048]{1,0:T(8,128)(2,1)S(1)}, u32[]{:S(2)}, u32[]{:S(2)}) collective-permute-start(bf16[128,2048]{1,0:T(8,128)(2,1)S(1)} %convolution_convert_fusion), channel_id=1, source_target_pairs={{0,2},{2,0},{4,6},{6,4},{1,3},{3,1},{5,7},{7,5},{8,10},{10,8},{12,... | collective-permute-start | bytes 1572872 | tf_op jit(solution)/shard_map/ppermute | solution.py:100
  52.4 24.5 %collective-permute-start.16 = (bf16[128,2048]{1,0:T(8,128)(2,1)S(1)}, bf16[128,2048]{1,0:T(8,128)(2,1)S(1)}, u32[]{:S(2)}, u32[]{:S(2)}) collective-permute-start(bf16[128,2048]{1,0:T(8,128)(2,1)S(1)} %convolution_convert_fusion.2), channel_id=1, source_target_pairs={{0,2},{2,0},{4,6},{6,4},{1,3},{3,1},{5,7},{7,5},{8,10},{10,8},{12,... | collective-permute-start | bytes 1572872 | tf_op jit(solution)/shard_map/ppermute | solution.py:100
  53.3 35.8 %collective-permute-start.21 = (bf16[1024,384]{0,1:T(8,128)(2,1)S(1)}, bf16[1024,384]{0,1:T(8,128)(2,1)S(1)}, u32[]{:S(2)}, u32[]{:S(2)}) collective-permute-start(bf16[1024,384]{0,1:T(8,128)(2,1)S(1)} %fusion.75), channel_id=1, source_target_pairs={{0,1},{1,0},{2,3},{3,2},{4,5},{5,4},{6,7},{7,6},{8,9},{9,8},{10,11... | collective-permute-start | bytes 2359304 | tf_op jit(solution)/shard_map/ppermute | solution.py:17
  55.7 21.7 %collective-permute-start.18 = (bf16[128,2048]{1,0:T(8,128)(2,1)S(1)}, bf16[128,2048]{1,0:T(8,128)(2,1)S(1)}, u32[]{:S(2)}, u32[]{:S(2)}) collective-permute-start(bf16[128,2048]{1,0:T(8,128)(2,1)S(1)} %fusion.5), channel_id=1, source_target_pairs={{0,4},{2,6},{4,0},{6,2},{1,5},{3,7},{5,1},{7,3},{8,12},{10,14},{12... | collective-permute-start | bytes 1572872 | tf_op jit(solution)/shard_map/ppermute | solution.py:100
  58.7 12.5 %collective-permute-start.8 = (bf16[128,128]{1,0:T(8,128)(2,1)S(1)}, bf16[128,128]{1,0:T(8,128)(2,1)S(1)}, u32[]{:S(2)}, u32[]{:S(2)}) collective-permute-start(bf16[128,128]{1,0:T(8,128)(2,1)S(1)} %get-tuple-element.94), channel_id=1, source_target_pairs={{0,6},{2,4},{4,2},{6,0},{1,7},{3,5},{5,3},{7,1},{8,14},{10,12},{12... | collective-permute-start | bytes 98312 | tf_op jit(solution)/shard_map/ppermute | solution.py:100
  59.4 11.9 %copy-start.2 = (bf16[1,1,128,2048]{3,2,1,0:T(8,128)(2,1)S(1)}, bf16[1,1,128,2048]{3,2,1,0:T(8,128)(2,1)}, u32[]{:S(2)}) copy-start(bf16[1,1,128,2048]{3,2,1,0:T(8,128)(2,1)} %param.11) | copy-start | bytes 1572868
  59.4 1.4 %collective-permute-start.6 = (bf16[128,128]{1,0:T(8,128)(2,1)S(1)}, bf16[128,128]{1,0:T(8,128)(2,1)S(1)}, u32[]{:S(2)}, u32[]{:S(2)}) collective-permute-start(bf16[128,128]{1,0:T(8,128)(2,1)S(1)} %get-tuple-element.96), channel_id=1, source_target_pairs={{0,2},{2,0},{4,6},{6,4},{1,3},{3,1},{5,7},{7,5},{8,10},{10,8},{12,... | collective-permute-start | bytes 98312 | tf_op jit(solution)/shard_map/ppermute | solution.py:100
  60.8 10.4 %collective-permute-start.7 = (bf16[128,128]{1,0:T(8,128)(2,1)S(1)}, bf16[128,128]{1,0:T(8,128)(2,1)S(1)}, u32[]{:S(2)}, u32[]{:S(2)}) collective-permute-start(bf16[128,128]{1,0:T(8,128)(2,1)S(1)} %get-tuple-element.95), channel_id=1, source_target_pairs={{0,4},{2,6},{4,0},{6,2},{1,5},{3,7},{5,1},{7,3},{8,12},{10,14},{12... | collective-permute-start | bytes 98312 | tf_op jit(solution)/shard_map/ppermute | solution.py:100
  71.2 2.2 %collective-permute-start.12 = (bf16[128,2048]{1,0:T(8,128)(2,1)S(1)}, bf16[128,2048]{1,0:T(8,128)(2,1)S(1)}, u32[]{:S(2)}, u32[]{:S(2)}) collective-permute-start(bf16[128,2048]{1,0:T(8,128)(2,1)S(1)} %collective-permute-done.11), channel_id=1, source_target_pairs={{0,2},{2,0},{4,6},{6,4},{1,3},{3,1},{5,7},{7,5},{8,10},{10,8},{12,... | collective-permute-start | bytes 1572872 | tf_op jit(solution)/shard_map/ppermute | solution.py:100
  71.8 23.5 %collective-permute-start.9 = (bf16[128,2048]{1,0:T(8,128)(2,1)S(1)}, bf16[128,2048]{1,0:T(8,128)(2,1)}, u32[]{:S(2)}, u32[]{:S(2)}) collective-permute-start(bf16[128,2048]{1,0:T(8,128)(2,1)S(1)} %fusion.1), channel_id=1, source_target_pairs={{0,8},{8,16},{16,24},{24,0},{1,9},{9,17},{17,25},{25,1},{2,10},{10... | collective-permute-start | bytes 1572872 | tf_op jit(solution)/shard_map/ppermute | solution.py:17
  75.5 5.4 %collective-permute-start.15 = (bf16[128,128]{1,0:T(8,128)(2,1)S(1)}, bf16[128,128]{1,0:T(8,128)(2,1)S(1)}, u32[]{:S(2)}, u32[]{:S(2)}) collective-permute-start(bf16[128,128]{1,0:T(8,128)(2,1)S(1)} %get-tuple-element.90), channel_id=1, source_target_pairs={{0,6},{2,4},{4,2},{6,0},{1,7},{3,5},{5,3},{7,1},{8,14},{10,12},{12... | collective-permute-start | bytes 98312 | tf_op jit(solution)/shard_map/ppermute | solution.py:100
  76.9 3.9 %collective-permute-start.14 = (bf16[128,128]{1,0:T(8,128)(2,1)S(1)}, bf16[128,128]{1,0:T(8,128)(2,1)S(1)}, u32[]{:S(2)}, u32[]{:S(2)}) collective-permute-start(bf16[128,128]{1,0:T(8,128)(2,1)S(1)} %get-tuple-element.91), channel_id=1, source_target_pairs={{0,4},{2,6},{4,0},{6,2},{1,5},{3,7},{5,1},{7,3},{8,12},{10,14},{12... | collective-permute-start | bytes 98312 | tf_op jit(solution)/shard_map/ppermute | solution.py:100
  77.4 3.5 %copy-start.3 = (bf16[1,1,128,2048]{3,2,1,0:T(8,128)(2,1)S(1)}, bf16[1,1,128,2048]{3,2,1,0:T(8,128)(2,1)}, u32[]{:S(2)}) copy-start(bf16[1,1,128,2048]{3,2,1,0:T(8,128)(2,1)} %param.12) | copy-start | bytes 1572868
  77.4 1.2 %collective-permute-start.13 = (bf16[128,128]{1,0:T(8,128)(2,1)S(1)}, bf16[128,128]{1,0:T(8,128)(2,1)S(1)}, u32[]{:S(2)}, u32[]{:S(2)}) collective-permute-start(bf16[128,128]{1,0:T(8,128)(2,1)S(1)} %get-tuple-element.92), channel_id=1, source_target_pairs={{0,2},{2,0},{4,6},{6,4},{1,3},{3,1},{5,7},{7,5},{8,10},{10,8},{12,... | collective-permute-start | bytes 98312 | tf_op jit(solution)/shard_map/ppermute | solution.py:100
  81.8 1.2 %collective-permute-start.23 = (f32[2,2048]{1,0:T(2,128)S(1)}, f32[2,2048]{1,0:T(2,128)S(1)}, u32[]{:S(2)}, u32[]{:S(2)}) collective-permute-start(f32[2,2048]{1,0:T(2,128)S(1)} %pad_maximum_fusion.3), channel_id=1, source_target_pairs={{0,2},{2,0},{4,6},{6,4},{1,3},{3,1},{5,7},{7,5},{8,10},{10,8},{12,... | collective-permute-start | bytes 49160 | tf_op jit(solution)/shard_map/ppermute | solution.py:100
  83.1 5.3 %collective-permute-start.24 = (f32[2,2048]{1,0:T(2,128)S(1)}, f32[2,2048]{1,0:T(2,128)S(1)}, u32[]{:S(2)}, u32[]{:S(2)}) collective-permute-start(f32[2,2048]{1,0:T(2,128)S(1)} %fusion.133), channel_id=1, source_target_pairs={{0,4},{2,6},{4,0},{6,2},{1,5},{3,7},{5,1},{7,3},{8,12},{10,14},{12... | collective-permute-start | bytes 49160 | tf_op jit(solution)/shard_map/ppermute | solution.py:100
  85.1 16.0 %collective-permute-start.20 = (bf16[128,2048]{1,0:T(8,128)(2,1)}, bf16[128,2048]{1,0:T(8,128)(2,1)}, u32[]{:S(2)}, u32[]{:S(2)}) collective-permute-start(bf16[128,2048]{1,0:T(8,128)(2,1)} %add_convert_fusion), channel_id=1, source_target_pairs={{0,24},{8,0},{16,8},{24,16},{1,25},{9,1},{17,9},{25,17},{2,26},{10... | collective-permute-start | bytes 1572872 | tf_op jit(solution)/shard_map/ppermute | solution.py:17
  88.4 24.0 %collective-permute-start.19 = (bf16[128,2048]{1,0:T(8,128)(2,1)S(1)}, bf16[128,2048]{1,0:T(8,128)(2,1)}, u32[]{:S(2)}, u32[]{:S(2)}) collective-permute-start(bf16[128,2048]{1,0:T(8,128)(2,1)S(1)} %fusion.2), channel_id=1, source_target_pairs={{0,8},{8,16},{16,24},{24,0},{1,9},{9,17},{17,25},{25,1},{2,10},{10... | collective-permute-start | bytes 1572872 | tf_op jit(solution)/shard_map/ppermute | solution.py:17
  88.4 6.8 %collective-permute-start.25 = (f32[2,2048]{1,0:T(2,128)S(1)}, f32[2,2048]{1,0:T(2,128)S(1)}, u32[]{:S(2)}, u32[]{:S(2)}) collective-permute-start(f32[2,2048]{1,0:T(2,128)S(1)} %fusion.167), channel_id=1, source_target_pairs={{0,1},{1,0},{2,3},{3,2},{4,5},{5,4},{6,7},{7,6},{8,9},{9,8},{10,11... | collective-permute-start | bytes 49160 | tf_op jit(solution)/shard_map/ppermute | solution.py:100
  (10 other events, 17.5 us)

commit v3 on v2

--- a/solution.py
+++ b/solution.py
@@ -21,36 +21,53 @@
     return math.pi / 2 * (indices.astype(jnp.float32) + 0.5) / TSTEPS
 
 
-def attend_tangent(queries, keys, values, tan_queries, tan_keys, tan_values):
-    rows = queries.shape[0]
+def attend(queries, keys, values):
+    rows, head_size = queries.shape
     block_rows = min(512, rows)
-    scale = 1.0 / math.sqrt(queries.shape[1])
-
-    def one_block(inputs):
-        query_block, tangent_block = inputs
+    scale = 1.0 / math.sqrt(head_size)
+
+    def one_block(query_block):
         scores = (
             jnp.einsum("qd,kd->qk", query_block, keys, preferred_element_type=jnp.float32) * scale
         )
-        probs = jax.nn.softmax(scores, axis=-1)
+        largest = jnp.max(scores, -1, keepdims=True)
+        raised = jnp.exp(scores - largest)
+        total = jnp.sum(raised, -1, keepdims=True)
+        probs_low = (raised / total).astype(jnp.bfloat16)
+        attended = jnp.dot(probs_low, values, preferred_element_type=jnp.float32)
+        return (attended.astype(jnp.bfloat16), (largest, total))
+
+    attended, kept = lax.map(one_block, queries.reshape(rows // block_rows, block_rows, -1))
+    return (attended.reshape(rows, -1), kept)
+
+
+def attend_tangent(kept, queries, keys, values, tan_queries, tan_keys, tan_values):
+    rows, head_size = queries.shape
+    block_rows = min(512, rows)
+    scale = 1.0 / math.sqrt(head_size)
+
+    def one_block(inputs):
+        (largest, total), query_block, tangent_block = inputs
+        scores = (
+            jnp.einsum("qd,kd->qk", query_block, keys, preferred_element_type=jnp.float32) * scale
+        )
+        probs = jnp.exp(scores - largest) / total
         tan_scores = (
             jnp.einsum("qd,kd->qk", tangent_block, keys, preferred_element_type=jnp.float32)
             + jnp.einsum("qd,kd->qk", query_block, tan_keys, preferred_element_type=jnp.float32)
         ) * scale
         tan_probs = probs * (tan_scores - jnp.sum(probs * tan_scores, -1, keepdims=True))
-        probs_low = probs.astype(jnp.bfloat16)
-        tan_low = tan_probs.astype(jnp.bfloat16)
-        attended = jnp.dot(probs_low, values, preferred_element_type=jnp.float32)
-        tan_attended = jnp.dot(tan_low, values, preferred_element_type=jnp.float32) + jnp.dot(
-            probs_low, tan_values, preferred_element_type=jnp.float32
-        )
-        return (attended.astype(jnp.bfloat16), tan_attended.astype(jnp.bfloat16))
+        tan_attended = jnp.dot(
+            tan_probs.astype(jnp.bfloat16), values, preferred_element_type=jnp.float32
+        ) + jnp.dot(probs.astype(jnp.bfloat16), tan_values, preferred_element_type=jnp.float32)
+        return tan_attended.astype(jnp.bfloat16)
 
     shaped = (
+        kept,
         queries.reshape(rows // block_rows, block_rows, -1),
         tan_queries.reshape(rows // block_rows, block_rows, -1),
     )
-    attended, tan_attended = lax.map(one_block, shaped)
-    return (attended.reshape(rows, -1), tan_attended.reshape(rows, -1))
+    return lax.map(one_block, shaped).reshape(rows, -1)
 
 
 def attend_backward(queries, keys, values, grad_attended):
@@ -111,16 +128,13 @@
     return pieces
 
 
-def summed_to_owner(terms):
-    count = len(terms)
-    pairs = {}
-    for mask in list(range(2, count, 2)) + [0]:
+def summed_on_chip(terms):
+    pairs = []
+    for mask in range(0, len(terms), 2):
         other = swapped(terms[mask ^ 1], "seq", 1)
-        pairs[mask] = terms[mask].astype(jnp.float32) + other.astype(jnp.float32)
-    total = pairs[0]
-    for mask in range(2, count, 2):
-        total = total + swapped(pairs[mask].astype(jnp.bfloat16), "seq", mask).astype(jnp.float32)
-    return total
+        pair = terms[mask].astype(jnp.float32) + other.astype(jnp.float32)
+        pairs.append(pair.astype(jnp.bfloat16) if mask else pair)
+    return pairs
 
 
 def scattered_over_dp(value, axis):
@@ -173,6 +187,12 @@
     rows = cot_rows.shape[0]
     owners = [jnp.bitwise_xor(me, mask) for mask in range(count)]
 
+    def in_pieces(value):
+        return jnp.concatenate(
+            [lax.dynamic_slice_in_dim(value, owner * rows, rows, 0) for owner in owners]
+        )
+
+    saved_heads = in_pieces(saved_heads)
     cot_far = from_chips(cot_rows)
     moment = moments[0]
     hidden = layer_input[0, 0].astype(jnp.float32)
@@ -189,12 +209,14 @@
     cot_pieces = gathered(cot_rows, cot_far)
     normed_far = from_chips(normed)
 
-    grad_out = jnp.zeros((rows * count, head_size), jnp.bfloat16)
-    for mask in range(count):
-        piece = jnp.einsum(
-            "td,hd->th", cot_pieces[mask], output_head, preferred_element_type=jnp.float32
-        ).astype(jnp.bfloat16)
-        grad_out = lax.dynamic_update_slice_in_dim(grad_out, piece, owners[mask] * rows, 0)
+    grad_out = jnp.concatenate(
+        [
+            jnp.einsum(
+                "td,hd->th", piece, output_head, preferred_element_type=jnp.float32
+            ).astype(jnp.bfloat16)
+            for piece in cot_pieces
+        ]
+    )
     grad_q, grad_k, grad_v, attended_b = attend_backward(
         saved_heads[:, :head_size],
         saved_heads[:, head_size : 2 * head_size],
@@ -202,22 +224,26 @@
         grad_out,
     )
     grad_proj = jnp.concatenate([grad_q, grad_k, grad_v], -1).astype(jnp.bfloat16)
-    tan_normed, normed_far, grad_proj, attended_b = lax.optimization_barrier(
-        (tan_normed, normed_far, grad_proj, attended_b)
-    )
-    tan_far = from_chips(tan_normed)
-    normed_pieces = gathered(normed, normed_far)
-    terms = {}
-    for mask in reversed(range(count)):
-        piece = lax.dynamic_slice_in_dim(grad_proj, owners[mask] * rows, rows, 0)
-        terms[mask] = jnp.einsum(
-            "tc,dc->td", piece, weight_heads, preferred_element_type=jnp.float32
+    terms = [
+        jnp.einsum(
+            "tc,dc->td",
+            grad_proj[mask * rows : (mask + 1) * rows],
+            weight_heads,
+            preferred_element_type=jnp.float32,
         ).astype(jnp.bfloat16)
-    grad_normed = summed_to_owner([terms[mask] for mask in range(count)])
+        for mask in range(count)
+    ]
+    pairs, grad_proj, attended_b = lax.optimization_barrier(
+        (summed_on_chip(terms), grad_proj, attended_b)
+    )
+    grad_normed = pairs[0]
+    for mask, pair in zip(range(2, count, 2), pairs[1:]):
+        grad_normed = grad_normed + swapped(pair, "seq", mask).astype(jnp.float32)
+    grad_proj = in_pieces(grad_proj)
     qkv_grad = jnp.einsum("td,tc->dc", normed_all, grad_proj, preferred_element_type=jnp.float32)
     out_grad = jnp.zeros((head_size, width), jnp.float32)
     for mask in range(count):
-        piece = lax.dynamic_slice_in_dim(attended_b, owners[mask] * rows, rows, 0)
+        piece = attended_b[mask * rows : (mask + 1) * rows]
         out_grad = out_grad + jnp.einsum(
             "th,td->hd", piece, cot_pieces[mask], preferred_element_type=jnp.float32
         )
@@ -234,31 +260,41 @@
             ]
         )
 
-    proj = projected(normed_pieces)
-    tan_proj = projected(gathered(tan_normed, tan_far))
-    attended, tan_attended = attend_tangent(
+    proj = projected(gathered(normed, normed_far))
+    queries, keys, values = (
         proj[:, :head_size],
         proj[:, head_size : 2 * head_size],
         proj[:, 2 * head_size :],
+    )
+
+    def returned(value):
+        pieces = [value[mask * rows : (mask + 1) * rows] for mask in range(count)]
+        return pieces[:1] + [swapped(pieces[mask], "seq", mask) for mask in range(1, count)]
+
+    def to_rows(pieces):
+        moved = jnp.zeros((rows, heads * head_size), jnp.bfloat16)
+        for owner, piece in zip(owners, pieces):
+            moved = lax.dynamic_update_slice_in_dim(moved, piece, owner * head_size, 1)
+        return jnp.dot(moved, output_flat, preferred_element_type=jnp.float32)
+
+    attended, kept = attend(queries, keys, values)
+    back = returned(attended)
+    back, tan_normed = lax.optimization_barrier((back, tan_normed))
+    tan_far = from_chips(tan_normed)
+    result = (hidden + to_rows(back)).astype(jnp.bfloat16)
+    next_input = passed_along(result, "section", 1)
+
+    tan_proj = projected(gathered(tan_normed, tan_far))
+    tan_attended = attend_tangent(
+        kept,
+        queries,
+        keys,
+        values,
         tan_proj[:, :head_size],
         tan_proj[:, head_size : 2 * head_size],
         tan_proj[:, 2 * head_size :],
     )
-    def to_rows(value):
-        moved = jnp.zeros((rows, heads * head_size), jnp.bfloat16)
-        for mask in range(count):
-            piece = value[mask * rows : (mask + 1) * rows]
-            if mask:
-                piece = swapped(piece, "seq", mask)
-            moved = lax.dynamic_update_slice_in_dim(moved, piece, owners[mask] * head_size, 1)
-        return jnp.dot(moved, output_flat, preferred_element_type=jnp.float32)
-
-    result = (hidden + to_rows(attended)).astype(jnp.bfloat16)
-    next_input = passed_along(result, "section", 1)
-    tan_result = (tangent + to_rows(tan_attended)).astype(jnp.bfloat16)
-    tan_result, grad_late = lax.optimization_barrier((tan_result, grad_normed))
-    next_tangent = passed_along(tan_result, "section", 1)
-
+    tan_result = (tangent + to_rows(returned(tan_attended))).astype(jnp.bfloat16)
     moment = moments[1]
     own_normed = lax.dynamic_slice_in_dim(normed_all, me * rows, rows, 0)
     modulated = gains + jnp.sin(moment) * scales
@@ -269,7 +305,9 @@
     )
     cotangent = (cot_rows.astype(jnp.float32) + grad_hidden).astype(jnp.bfloat16)
     cot_prev = passed_along(cotangent, "section", -1)
-    gain_part = jnp.sum(grad_late * normal_b, 0)
+    tan_result, cot_prev = lax.optimization_barrier((tan_result, cot_prev))
+    next_tangent = passed_along(tan_result, "section", 1)
+    gain_part = jnp.sum(grad_normed * normal_b, 0)
     norm_total = summed_everywhere(jnp.stack([gain_part, jnp.sin(moment) * gain_part]))
     return (
         next_input[None, None],

time: 119 us -> 103 us (0.87)
  matrix products: 29.9 us -> 19.9 us
  local copies, waits for them, and re-layouts: 18.8 us -> 10.9 us
  waiting for transfers between devices: 33.2 us -> 35.9 us
    dot_general x8, matrix products: 8.02 us -> 3.87 us  [projected(): jnp.dot(piece, weight_heads, preferred_element_type=jnp.float32)]
    unnamed x36 -> x30, local copies, waits for them, and re-layouts: 12.2 us -> 8.78 us
    convert_element_type x2 -> x0, local copies, waits for them, and re-layouts: 2.94 us -> none  [local(): piece = jnp.einsum('td,hd->th', cot_pieces[mask], output_head, preferred_...]
    dynamic_update_slice x8 -> x7, local copies, waits for them, and re-layouts: 2.83 us -> 0.12 us  [to_rows(): moved = lax.dynamic_update_slice_in_dim(moved, piece, owner * head_size, 1)]
    ppermute x21, waiting for transfers between devices: 14 us -> 16.5 us  [swapped(): lax.ppermute(value, axis, [(source, source ^ mask) for source in range(co...]
    dot_general x10, matrix products: 9.61 us -> 7.36 us  [the longest x4 3.92 us: local(): jnp.einsum('td,hd->th', piece, output_head, preferred_element_type=jnp.fl...]
    ppermute x5, starting transfers between devices: 8.42 us -> 6.54 us  [passed_along(): return lax.ppermute(value, axis, pairs)]
    ppermute x21, starting transfers between devices: 13.3 us -> 14.9 us  [swapped(): lax.ppermute(value, axis, [(source, source ^ mask) for source in range(co...]
  transfers between devices with their start and end apart: 26 -> 26, of which waited for: 9 -> 10; matrix products, arithmetic and copies ran while one was open for 44% -> 37% of each run, Pallas kernels for 0% -> 0%
where the time goes in v3:
time: 103 us
  waiting for transfers between devices  35.9 us (35%)
  starting transfers between devices  21.4 us (21%)
  matrix products  19.9 us (19%)
  other arithmetic  11.1 us (11%)
  local copies, waits for them, and re-layouts  10.9 us (11%)
  between operations  3.4 us (3%)
    ppermute x5, waiting for transfers between devices, passed_along(): return lax.ppermute(value, axis, pairs)  19.4 us
    ppermute x21, waiting for transfers between devices, swapped(): lax.ppermute(value, axis, [(source, source ^ mask) for source in range(co...  16.5 us
    ppermute x21, starting transfers between devices, swapped(): lax.ppermute(value, axis, [(source, source ^ mask) for source in range(co...  14.9 us
    unnamed x30, local copies, waits for them, and re-layouts  8.78 us
    ppermute x5, starting transfers between devices, passed_along(): return lax.ppermute(value, axis, pairs)  6.54 us
    dot_general x4, matrix products, local(): jnp.einsum('td,hd->th', piece, output_head, preferred_element_type=jnp.fl...  3.92 us
    dot_general x8, matrix products, projected(): jnp.dot(piece, weight_heads, preferred_element_type=jnp.float32)  3.87 us
    dot_general x4, matrix products, local(): jnp.einsum('th,td->hd', piece, cot_pieces[mask], preferred_element_type=j...  3.5 us
  transfers between devices with their start and end apart: 26, of which 10 were waited for; matrix products, arithmetic and copies ran while one was open for 37% of the time, Pallas kernels for 0%

profile of v3, /device:TPU:0, one launch (start us, length us, event | category | flops | bytes accessed | tf_op | source)
XLA Modules:
  0.0 102.6 jit_solution(12026694038171294236)
XLA Ops:
  1.2 2.6 %collective-permute-start = (bf16[128,2048]{1,0:T(8,128)(2,1)}, bf16[128,2048]{1,0:T(8,128)(2,1)}, u32[]{:S(2)}, u32[]{:S(2)}) collective-permute-start(bf16[128,2048]{1,0:T(8,128)(2,1)} %bitcast.143), channel_id=1, source_target_pairs={{0,4},{2,6},{4,0},{6,2},{1,5},{3,7},{5,1},{7,3},{8,12},{10,14},{12... | collective-permute-start | bytes 1572872 | tf_op jit(solution)/shard_map/ppermute | solution.py:117
  7.2 1.1 %dynamic-slice_bitcast_fusion.3 = (bf16[128,384]{1,0:T(8,128)(2,1)S(1)}, bf16[128,384]{1,0:T(8,128)(2,1)S(1)}, bf16[128,384]{1,0:T(8,128)(2,1)S(1)}, bf16[128,384]{1,0:T(8,128)(2,1)S(1)}) fusion(bf16[1,1,512,1,384]{4,2,3,1,0:T(8,128)(2,1)} %param.16, s32[]{:T(128)S(6)} %select_n.16, s32[]{:T(128)S(6)} %select_n.17, s32[]{:T(128)S(6)} %select_n.19, ...), kind=kLoop, calls=%fused_computation.147 | loop fusion | bytes 786448 | tf_op jit(solution)/shard_map/dynamic_slice | solution.py:192
  8.7 1.5 %fusion.64 = (f32[128]{0:T(128)S(1)}, f32[128]{0:T(128)S(1)}) fusion(bf16[1,1,128,2048]{3,2,1,0:T(8,128)(2,1)} %param.12, bf16[1,1,128,2048]{3,2,1,0:T(8,128)(2,1)} %param.11), kind=kLoop, calls=%fused_computation.76 | loop fusion | flops 1572608 | bytes 1049600 | tf_op jit(solution)/shard_map/reduce_sum | solution.py:202
  11.0 3.3 %fusion.60 = (bf16[128,2048]{1,0:T(8,128)(2,1)}, bf16[128,2048]{1,0:T(8,128)(2,1)}) fusion(bf16[1,1,128,2048]{3,2,1,0:T(8,128)(2,1)} %param.12, bf16[1,1,128,2048]{3,2,1,0:T(8,128)(2,1)} %param.11, f32[2048]{0:T(1024)S(1)} %bitcast.153, f32[128]{0:T(128)S(1)} %get-tuple-element.145, f32[2048]{0:T(1024)S(1)} %bitcast.152, f32[128]{0:T(128)S(1)} %get-tuple-element.146), kind=kLoop, calls=%fused_computation.72 | loop fusion | flops 3145728 | bytes 2114560 | tf_op jit(solution)/shard_map/convert_element_type | solution.py:207
  14.3 0.9 fusion.56
  16.6 1.3 %convolution_convert_fusion.10 = bf16[128,128]{1,0:T(8,128)(2,1)S(1)} fusion(bf16[128,2048]{1,0:T(8,128)(2,1)} %collective-permute-done, bf16[1,4,128,2048]{3,2,1,0:T(8,128)(2,1)S(1)} %copy-done, s32[]{:T(128)S(6)} %select_n.20), kind=kOutput, calls=%fused_computation.65 | convolution fusion | flops 67125248 | bytes 1081348 | tf_op jit(solution)/shard_map/td,hd->th/dot_general | solution.py:214
  18.0 1.8 %collective-permute-start.2 = (bf16[128,2048]{1,0:T(8,128)(2,1)S(1)}, bf16[128,2048]{1,0:T(8,128)(2,1)S(1)}, u32[]{:S(2)}, u32[]{:S(2)}) collective-permute-start(bf16[128,2048]{1,0:T(8,128)(2,1)S(1)} %copy-done.8), channel_id=1, source_target_pairs={{0,4},{2,6},{4,0},{6,2},{1,5},{3,7},{5,1},{7,3},{8,12},{10,14},{12... | collective-permute-start | bytes 1572872 | tf_op jit(solution)/shard_map/ppermute | solution.py:117
  20.0 1.3 %fusion.57 = bf16[128,128]{1,0:T(8,128)(2,1)S(1)} fusion(bf16[128,2048]{1,0:T(8,128)(2,1)} %collective-permute-done.14, bf16[1,4,128,2048]{3,2,1,0:T(8,128)(2,1)S(1)} %copy-done, s32[]{:T(128)S(6)} %select_n.20), kind=kOutput, calls=%fused_computation.69 | convolution fusion | flops 67125248 | bytes 1081348 | tf_op jit(solution)/shard_map/td,hd->th/dot_general | solution.py:214
  25.7 6.7 %collective-permute-done.2 = bf16[128,2048]{1,0:T(8,128)(2,1)S(1)} collective-permute-done((bf16[128,2048]{1,0:T(8,128)(2,1)S(1)}, bf16[128,2048]{1,0:T(8,128)(2,1)S(1)}, u32[]{:S(2)}, u32[]{:S(2)}) %collective-permute-start.2) | collective-permute-done | bytes 524320 | tf_op jit(solution)/shard_map/ppermute | solution.py:117
  33.3 1.0 collective-permute-done.3
  35.7 1.5 %collective-permute-start.6 = (bf16[128,128]{1,0:T(8,128)(2,1)S(1)}, bf16[128,128]{1,0:T(8,128)(2,1)S(1)}, u32[]{:S(2)}, u32[]{:S(2)}) collective-permute-start(bf16[128,128]{1,0:T(8,128)(2,1)S(1)} %get-tuple-element.136), channel_id=1, source_target_pairs={{0,6},{2,4},{4,2},{6,0},{1,7},{3,5},{5,3},{7,1},{8,14},{10,12},{12... | collective-permute-start | bytes 98312 | tf_op jit(solution)/shard_map/ppermute | solution.py:117
  39.1 1.8 %collective-permute-start.18 = (bf16[128,2048]{1,0:T(8,128)(2,1)S(1)}, bf16[128,2048]{1,0:T(8,128)(2,1)S(1)}, u32[]{:S(2)}, u32[]{:S(2)}) collective-permute-start(bf16[128,2048]{1,0:T(8,128)(2,1)S(1)} %add_convert_fusion.1), channel_id=1, source_target_pairs={{0,4},{2,6},{4,0},{6,2},{1,5},{3,7},{5,1},{7,3},{8,12},{10,14},{12... | collective-permute-start | bytes 1572872 | tf_op jit(solution)/shard_map/ppermute | solution.py:117
  41.6 1.4 %convolution_add_fusion.1 = f32[128,2048]{1,0:T(8,128)S(1)} fusion(f32[128,2048]{1,0:T(8,128)S(1)} %fusion.124, bf16[128,2048]{1,0:T(8,128)(2,1)} %collective-permute-done.14, bf16[512,128]{1,0:T(8,128)(2,1)S(1)} %convolution_convert_fusion.4), kind=kOutput, calls=%fused_computation.2 | convolution fusion | flops 67371008 | bytes 2654208 | tf_op jit(solution)/shard_map/th,td->hd/dot_general | solution.py:247
  43.0 1.5 %fusion = f32[128,2048]{1,0:T(8,128)S(1)} fusion(f32[128,2048]{1,0:T(8,128)S(1)} %fusion.120, f32[128,2048]{1,0:T(8,128)S(1)} %convolution_add_fusion.1, bf16[128,2048]{1,0:T(8,128)(2,1)} %collective-permute-done, bf16[512,128]{1,0:T(8,128)(2,1)S(1)} %convolution_convert_fusion.4), kind=kOutput, calls=%fused_computation.1 | convolution fusion | flops 67633152 | bytes 3702784 | tf_op jit(solution)/shard_map/th,td->hd/dot_general | solution.py:247
  44.5 1.5 %collective-permute-start.22 = (bf16[128,1024]{1,0:T(8,128)(2,1)S(1)}, bf16[128,1024]{1,0:T(8,128)(2,1)S(1)}, u32[]{:S(2)}, u32[]{:S(2)}) collective-permute-start(bf16[128,1024]{1,0:T(8,128)(2,1)S(1)} %dynamic-slice_convert_fusion.1), channel_id=1, source_target_pairs={{0,1},{1,0},{2,3},{3,2},{4,5},{5,4},{6,7},{7,6},{8,9},{9,8},{10,11... | collective-permute-start | bytes 786440 | tf_op jit(solution)/shard_map/ppermute | solution.py:17
  46.0 1.0 fusion.5
  49.9 3.9 %collective-permute-done.22 = bf16[128,1024]{1,0:T(8,128)(2,1)S(1)} collective-permute-done((bf16[128,1024]{1,0:T(8,128)(2,1)S(1)}, bf16[128,1024]{1,0:T(8,128)(2,1)S(1)}, u32[]{:S(2)}, u32[]{:S(2)}) %collective-permute-start.22) | collective-permute-done | bytes 262176 | tf_op jit(solution)/shard_map/ppermute | solution.py:17
  53.8 1.5 %collective-permute-start.7 = (bf16[128,2048]{1,0:T(8,128)(2,1)S(1)}, bf16[128,2048]{1,0:T(8,128)(2,1)S(1)}, u32[]{:S(2)}, u32[]{:S(2)}) collective-permute-start(bf16[128,2048]{1,0:T(8,128)(2,1)S(1)} %fusion.1), channel_id=1, source_target_pairs={{0,8},{8,16},{16,24},{24,0},{1,9},{9,17},{17,25},{25,1},{2,10},{10... | collective-permute-start | bytes 1572872 | tf_op jit(solution)/shard_map/ppermute | solution.py:17
  55.3 0.9 add_bitcast_fusion
  57.8 2.3 %collective-permute-start.19 = (bf16[128,2048]{1,0:T(8,128)(2,1)S(1)}, bf16[128,2048]{1,0:T(8,128)(2,1)S(1)}, u32[]{:S(2)}, u32[]{:S(2)}) collective-permute-start(bf16[128,2048]{1,0:T(8,128)(2,1)S(1)} %add_convert_fusion), channel_id=1, source_target_pairs={{0,24},{8,0},{16,8},{24,16},{1,25},{9,1},{17,9},{25,17},{2,26},{10... | collective-permute-start | bytes 1572872 | tf_op jit(solution)/shard_map/ppermute | solution.py:17
  60.2 4.5 %collective-permute-done.9 = bf16[128,2048]{1,0:T(8,128)(2,1)S(1)} collective-permute-done((bf16[128,2048]{1,0:T(8,128)(2,1)S(1)}, bf16[128,2048]{1,0:T(8,128)(2,1)S(1)}, u32[]{:S(2)}, u32[]{:S(2)}) %collective-permute-start.9) | collective-permute-done | bytes 524320 | tf_op jit(solution)/shard_map/ppermute | solution.py:117
  65.2 1.7 %collective-permute-start.24 = (f32[2,2048]{1,0:T(2,128)S(1)}, f32[2,2048]{1,0:T(2,128)S(1)}, u32[]{:S(2)}, u32[]{:S(2)}) collective-permute-start(f32[2,2048]{1,0:T(2,128)S(1)} %fusion.137), channel_id=1, source_target_pairs={{0,4},{2,6},{4,0},{6,2},{1,5},{3,7},{5,1},{7,3},{8,12},{10,14},{12... | collective-permute-start | bytes 49160 | tf_op jit(solution)/shard_map/ppermute | solution.py:117
  70.5 1.4 %collective-permute-start.25 = (f32[2,2048]{1,0:T(2,128)S(1)}, f32[2,2048]{1,0:T(2,128)S(1)}, u32[]{:S(2)}, u32[]{:S(2)}) collective-permute-start(f32[2,2048]{1,0:T(2,128)S(1)} %fusion.168), channel_id=1, source_target_pairs={{0,1},{1,0},{2,3},{3,2},{4,5},{5,4},{6,7},{7,6},{8,9},{9,8},{10,11... | collective-permute-start | bytes 49160 | tf_op jit(solution)/shard_map/ppermute | solution.py:117
  72.0 1.2 %collective-permute-start.12 = (bf16[128,128]{1,0:T(8,128)(2,1)S(1)}, bf16[128,128]{1,0:T(8,128)(2,1)S(1)}, u32[]{:S(2)}, u32[]{:S(2)}) collective-permute-start(bf16[128,128]{1,0:T(8,128)(2,1)S(1)} %get-tuple-element.133), channel_id=1, source_target_pairs={{0,4},{2,6},{4,0},{6,2},{1,5},{3,7},{5,1},{7,3},{8,12},{10,14},{12... | collective-permute-start | bytes 98312 | tf_op jit(solution)/shard_map/ppermute | solution.py:117
  73.1 2.9 %collective-permute-done.12 = bf16[128,128]{1,0:T(8,128)(2,1)S(1)} collective-permute-done((bf16[128,128]{1,0:T(8,128)(2,1)S(1)}, bf16[128,128]{1,0:T(8,128)(2,1)S(1)}, u32[]{:S(2)}, u32[]{:S(2)}) %collective-permute-start.12) | collective-permute-done | bytes 32800 | tf_op jit(solution)/shard_map/ppermute | solution.py:117
  76.6 2.6 %collective-permute-done.19 = bf16[128,2048]{1,0:T(8,128)(2,1)S(1)} collective-permute-done((bf16[128,2048]{1,0:T(8,128)(2,1)S(1)}, bf16[128,2048]{1,0:T(8,128)(2,1)S(1)}, u32[]{:S(2)}, u32[]{:S(2)}) %collective-permute-start.19) | collective-permute-done | bytes 524320 | tf_op jit(solution)/shard_map/ppermute | solution.py:17
  80.6 1.5 %fusion.7 = f32[1,1024,1,384]{1,3,2,0:T(8,128)} fusion(bf16[1024,384]{0,1:T(8,128)(2,1)S(1)} %collective-permute-done.21, f32[384,2048]{1,0:T(8,128)S(1)} %fusion.5, s32[]{:T(128)S(6)} %select_n.21), kind=kLoop, calls=%fused_computation.20 | loop fusion | flops 786432 | bytes 3932164 | tf_op jit(solution)/shard_map/broadcast_in_dim | solution.py:316
  82.0 4.8 %copy.17 = f32[1,1024,1,384]{3,2,1,0:T(1,128)} copy(f32[1,1024,1,384]{1,3,2,0:T(8,128)} %fusion.7) | data formatting | bytes 3145728
  86.9 12.3 %collective-permute-done.20 = bf16[128,2048]{1,0:T(8,128)(2,1)} collective-permute-done((bf16[128,2048]{1,0:T(8,128)(2,1)S(1)}, bf16[128,2048]{1,0:T(8,128)(2,1)}, u32[]{:S(2)}, u32[]{:S(2)}) %collective-permute-start.20) | collective-permute-done | bytes 524320 | tf_op jit(solution)/shard_map/ppermute | solution.py:17
  99.1 0.8 copy.29
  99.9 1.9 %copy.30 = bf16[1,1,128,2048]{3,2,1,0:T(8,128)(2,1)} copy(bf16[1,1,128,2048]{3,2,1,0:T(8,128)(2,1)} %bitcast.23) | data formatting | bytes 1048576
  101.8 0.8 copy.31
  (123 shorter events, 23.9 us)
Async XLA Ops:
  0.6 13.7 %copy-start = (bf16[1,4,128,2048]{3,2,1,0:T(8,128)(2,1)S(1)}, bf16[1,4,128,2048]{3,2,1,0:T(8,128)(2,1)}, u32[]{:S(2)}) copy-start(bf16[1,4,128,2048]{3,2,1,0:T(8,128)(2,1)} %param.19) | copy-start | bytes 6291460
  0.6 19.4 %collective-permute-start.14 = (bf16[128,2048]{1,0:T(8,128)(2,1)}, bf16[128,2048]{1,0:T(8,128)(2,1)}, u32[]{:S(2)}, u32[]{:S(2)}) collective-permute-start(bf16[128,2048]{1,0:T(8,128)(2,1)} %bitcast.142), channel_id=1, source_target_pairs={{0,2},{2,0},{4,6},{6,4},{1,3},{3,1},{5,7},{7,5},{8,10},{10,8},{12,... | collective-permute-start | bytes 1572872 | tf_op jit(solution)/shard_map/ppermute | solution.py:117
  1.2 15.4 %collective-permute-start = (bf16[128,2048]{1,0:T(8,128)(2,1)}, bf16[128,2048]{1,0:T(8,128)(2,1)}, u32[]{:S(2)}, u32[]{:S(2)}) collective-permute-start(bf16[128,2048]{1,0:T(8,128)(2,1)} %bitcast.143), channel_id=1, source_target_pairs={{0,4},{2,6},{4,0},{6,2},{1,5},{3,7},{5,1},{7,3},{8,12},{10,14},{12... | collective-permute-start | bytes 1572872 | tf_op jit(solution)/shard_map/ppermute | solution.py:117
  8.6 5.6 %copy-start.3 = (bf16[1,1,128,2048]{3,2,1,0:T(8,128)(2,1)S(1)}, bf16[1,1,128,2048]{3,2,1,0:T(8,128)(2,1)}, u32[]{:S(2)}) copy-start(bf16[1,1,128,2048]{3,2,1,0:T(8,128)(2,1)} %param.13) | copy-start | bytes 1572868
  15.8 5.6 %copy-start.1 = (bf16[1,2048,1,384]{3,1,2,0:T(8,128)(2,1)S(1)}, bf16[1,2048,1,384]{3,1,2,0:T(8,128)(2,1)}, u32[]{:S(2)}) copy-start(bf16[1,2048,1,384]{3,1,2,0:T(8,128)(2,1)} %param.18) | copy-start | bytes 4718596
  16.6 5.2 %collective-permute-start.15 = (bf16[128,2048]{1,0:T(8,128)(2,1)}, bf16[128,2048]{1,0:T(8,128)(2,1)S(1)}, u32[]{:S(2)}, u32[]{:S(2)}) collective-permute-start(bf16[128,2048]{1,0:T(8,128)(2,1)} %collective-permute-done), channel_id=1, source_target_pairs={{0,2},{2,0},{4,6},{6,4},{1,3},{3,1},{5,7},{7,5},{8,10},{10,8},{12,... | collective-permute-start | bytes 1572872 | tf_op jit(solution)/shard_map/ppermute | solution.py:117
  18.0 14.4 %collective-permute-start.2 = (bf16[128,2048]{1,0:T(8,128)(2,1)S(1)}, bf16[128,2048]{1,0:T(8,128)(2,1)S(1)}, u32[]{:S(2)}, u32[]{:S(2)}) collective-permute-start(bf16[128,2048]{1,0:T(8,128)(2,1)S(1)} %copy-done.8), channel_id=1, source_target_pairs={{0,4},{2,6},{4,0},{6,2},{1,5},{3,7},{5,1},{7,3},{8,12},{10,14},{12... | collective-permute-start | bytes 1572872 | tf_op jit(solution)/shard_map/ppermute | solution.py:117
  19.8 13.0 %collective-permute-start.1 = (bf16[128,2048]{1,0:T(8,128)(2,1)S(1)}, bf16[128,2048]{1,0:T(8,128)(2,1)S(1)}, u32[]{:S(2)}, u32[]{:S(2)}) collective-permute-start(bf16[128,2048]{1,0:T(8,128)(2,1)S(1)} %copy-done.8), channel_id=1, source_target_pairs={{0,2},{2,0},{4,6},{6,4},{1,3},{3,1},{5,7},{7,5},{8,10},{10,8},{12,... | collective-permute-start | bytes 1572872 | tf_op jit(solution)/shard_map/ppermute | solution.py:117
  24.4 13.3 %collective-permute-start.16 = (bf16[128,2048]{1,0:T(8,128)(2,1)S(1)}, bf16[128,2048]{1,0:T(8,128)(2,1)S(1)}, u32[]{:S(2)}, u32[]{:S(2)}) collective-permute-start(bf16[128,2048]{1,0:T(8,128)(2,1)S(1)} %convolution_convert_fusion.2), channel_id=1, source_target_pairs={{0,2},{2,0},{4,6},{6,4},{1,3},{3,1},{5,7},{7,5},{8,10},{10,8},{12,... | collective-permute-start | bytes 1572872 | tf_op jit(solution)/shard_map/ppermute | solution.py:117
  25.4 12.9 %collective-permute-start.17 = (bf16[128,2048]{1,0:T(8,128)(2,1)S(1)}, bf16[128,2048]{1,0:T(8,128)(2,1)S(1)}, u32[]{:S(2)}, u32[]{:S(2)}) collective-permute-start(bf16[128,2048]{1,0:T(8,128)(2,1)S(1)} %convolution_convert_fusion), channel_id=1, source_target_pairs={{0,2},{2,0},{4,6},{6,4},{1,3},{3,1},{5,7},{7,5},{8,10},{10,8},{12,... | collective-permute-start | bytes 1572872 | tf_op jit(solution)/shard_map/ppermute | solution.py:117
  32.4 1.9 %collective-permute-start.3 = (bf16[128,2048]{1,0:T(8,128)(2,1)S(1)}, bf16[128,2048]{1,0:T(8,128)(2,1)S(1)}, u32[]{:S(2)}, u32[]{:S(2)}) collective-permute-start(bf16[128,2048]{1,0:T(8,128)(2,1)S(1)} %collective-permute-done.2), channel_id=1, source_target_pairs={{0,2},{2,0},{4,6},{6,4},{1,3},{3,1},{5,7},{7,5},{8,10},{10,8},{12,... | collective-permute-start | bytes 1572872 | tf_op jit(solution)/shard_map/ppermute | solution.py:117
  35.7 11.5 %collective-permute-start.6 = (bf16[128,128]{1,0:T(8,128)(2,1)S(1)}, bf16[128,128]{1,0:T(8,128)(2,1)S(1)}, u32[]{:S(2)}, u32[]{:S(2)}) collective-permute-start(bf16[128,128]{1,0:T(8,128)(2,1)S(1)} %get-tuple-element.136), channel_id=1, source_target_pairs={{0,6},{2,4},{4,2},{6,0},{1,7},{3,5},{5,3},{7,1},{8,14},{10,12},{12... | collective-permute-start | bytes 98312 | tf_op jit(solution)/shard_map/ppermute | solution.py:117
  37.3 10.6 %collective-permute-start.5 = (bf16[128,128]{1,0:T(8,128)(2,1)S(1)}, bf16[128,128]{1,0:T(8,128)(2,1)S(1)}, u32[]{:S(2)}, u32[]{:S(2)}) collective-permute-start(bf16[128,128]{1,0:T(8,128)(2,1)S(1)} %get-tuple-element.137), channel_id=1, source_target_pairs={{0,4},{2,6},{4,0},{6,2},{1,5},{3,7},{5,1},{7,3},{8,12},{10,14},{12... | collective-permute-start | bytes 98312 | tf_op jit(solution)/shard_map/ppermute | solution.py:117
  37.6 10.3 %collective-permute-start.4 = (bf16[128,128]{1,0:T(8,128)(2,1)S(1)}, bf16[128,128]{1,0:T(8,128)(2,1)S(1)}, u32[]{:S(2)}, u32[]{:S(2)}) collective-permute-start(bf16[128,128]{1,0:T(8,128)(2,1)S(1)} %get-tuple-element.138), channel_id=1, source_target_pairs={{0,2},{2,0},{4,6},{6,4},{1,3},{3,1},{5,7},{7,5},{8,10},{10,8},{12,... | collective-permute-start | bytes 98312 | tf_op jit(solution)/shard_map/ppermute | solution.py:117
  39.1 17.0 %collective-permute-start.18 = (bf16[128,2048]{1,0:T(8,128)(2,1)S(1)}, bf16[128,2048]{1,0:T(8,128)(2,1)S(1)}, u32[]{:S(2)}, u32[]{:S(2)}) collective-permute-start(bf16[128,2048]{1,0:T(8,128)(2,1)S(1)} %add_convert_fusion.1), channel_id=1, source_target_pairs={{0,4},{2,6},{4,0},{6,2},{1,5},{3,7},{5,1},{7,3},{8,12},{10,14},{12... | collective-permute-start | bytes 1572872 | tf_op jit(solution)/shard_map/ppermute | solution.py:117
  44.5 9.2 %collective-permute-start.22 = (bf16[128,1024]{1,0:T(8,128)(2,1)S(1)}, bf16[128,1024]{1,0:T(8,128)(2,1)S(1)}, u32[]{:S(2)}, u32[]{:S(2)}) collective-permute-start(bf16[128,1024]{1,0:T(8,128)(2,1)S(1)} %dynamic-slice_convert_fusion.1), channel_id=1, source_target_pairs={{0,1},{1,0},{2,3},{3,2},{4,5},{5,4},{6,7},{7,6},{8,9},{9,8},{10,11... | collective-permute-start | bytes 786440 | tf_op jit(solution)/shard_map/ppermute | solution.py:17
  47.2 33.4 %collective-permute-start.21 = (bf16[1024,384]{0,1:T(8,128)(2,1)S(1)}, bf16[1024,384]{0,1:T(8,128)(2,1)S(1)}, u32[]{:S(2)}, u32[]{:S(2)}) collective-permute-start(bf16[1024,384]{0,1:T(8,128)(2,1)S(1)} %fusion.69), channel_id=1, source_target_pairs={{0,1},{1,0},{2,3},{3,2},{4,5},{5,4},{6,7},{7,6},{8,9},{9,8},{10,11... | collective-permute-start | bytes 2359304 | tf_op jit(solution)/shard_map/ppermute | solution.py:17
  48.1 16.6 %collective-permute-start.9 = (bf16[128,2048]{1,0:T(8,128)(2,1)S(1)}, bf16[128,2048]{1,0:T(8,128)(2,1)S(1)}, u32[]{:S(2)}, u32[]{:S(2)}) collective-permute-start(bf16[128,2048]{1,0:T(8,128)(2,1)S(1)} %copy-done.7), channel_id=1, source_target_pairs={{0,4},{2,6},{4,0},{6,2},{1,5},{3,7},{5,1},{7,3},{8,12},{10,14},{12... | collective-permute-start | bytes 1572872 | tf_op jit(solution)/shard_map/ppermute | solution.py:117
  48.6 16.6 %collective-permute-start.8 = (bf16[128,2048]{1,0:T(8,128)(2,1)S(1)}, bf16[128,2048]{1,0:T(8,128)(2,1)S(1)}, u32[]{:S(2)}, u32[]{:S(2)}) collective-permute-start(bf16[128,2048]{1,0:T(8,128)(2,1)S(1)} %copy-done.7), channel_id=1, source_target_pairs={{0,2},{2,0},{4,6},{6,4},{1,3},{3,1},{5,7},{7,5},{8,10},{10,8},{12,... | collective-permute-start | bytes 1572872 | tf_op jit(solution)/shard_map/ppermute | solution.py:117
  49.8 6.8 %copy-start.12 = (f32[1,1,128]{2,1,0:T(1,128)S(1)}, f32[1,1,128]{2,1,0:T(1,128)}, u32[]{:S(2)}) copy-start(f32[1,1,128]{2,1,0:T(1,128)} %param.15) | copy-start | bytes 1540
  53.8 16.7 %collective-permute-start.7 = (bf16[128,2048]{1,0:T(8,128)(2,1)S(1)}, bf16[128,2048]{1,0:T(8,128)(2,1)S(1)}, u32[]{:S(2)}, u32[]{:S(2)}) collective-permute-start(bf16[128,2048]{1,0:T(8,128)(2,1)S(1)} %fusion.1), channel_id=1, source_target_pairs={{0,8},{8,16},{16,24},{24,0},{1,9},{9,17},{17,25},{25,1},{2,10},{10... | collective-permute-start | bytes 1572872 | tf_op jit(solution)/shard_map/ppermute | solution.py:17
  56.6 1.2 %collective-permute-start.23 = (f32[2,2048]{1,0:T(2,128)S(1)}, f32[2,2048]{1,0:T(2,128)S(1)}, u32[]{:S(2)}, u32[]{:S(2)}) collective-permute-start(f32[2,2048]{1,0:T(2,128)S(1)} %pad_maximum_fusion.7), channel_id=1, source_target_pairs={{0,2},{2,0},{4,6},{6,4},{1,3},{3,1},{5,7},{7,5},{8,10},{10,8},{12,... | collective-permute-start | bytes 49160 | tf_op jit(solution)/shard_map/ppermute | solution.py:117
  57.8 21.3 %collective-permute-start.19 = (bf16[128,2048]{1,0:T(8,128)(2,1)S(1)}, bf16[128,2048]{1,0:T(8,128)(2,1)S(1)}, u32[]{:S(2)}, u32[]{:S(2)}) collective-permute-start(bf16[128,2048]{1,0:T(8,128)(2,1)S(1)} %add_convert_fusion), channel_id=1, source_target_pairs={{0,24},{8,0},{16,8},{24,16},{1,25},{9,1},{17,9},{25,17},{2,26},{10... | collective-permute-start | bytes 1572872 | tf_op jit(solution)/shard_map/ppermute | solution.py:17
  64.7 2.7 %collective-permute-start.10 = (bf16[128,2048]{1,0:T(8,128)(2,1)S(1)}, bf16[128,2048]{1,0:T(8,128)(2,1)S(1)}, u32[]{:S(2)}, u32[]{:S(2)}) collective-permute-start(bf16[128,2048]{1,0:T(8,128)(2,1)S(1)} %collective-permute-done.9), channel_id=1, source_target_pairs={{0,2},{2,0},{4,6},{6,4},{1,3},{3,1},{5,7},{7,5},{8,10},{10,8},{12,... | collective-permute-start | bytes 1572872 | tf_op jit(solution)/shard_map/ppermute | solution.py:117
  65.2 4.7 %collective-permute-start.24 = (f32[2,2048]{1,0:T(2,128)S(1)}, f32[2,2048]{1,0:T(2,128)S(1)}, u32[]{:S(2)}, u32[]{:S(2)}) collective-permute-start(f32[2,2048]{1,0:T(2,128)S(1)} %fusion.137), channel_id=1, source_target_pairs={{0,4},{2,6},{4,0},{6,2},{1,5},{3,7},{5,1},{7,3},{8,12},{10,14},{12... | collective-permute-start | bytes 49160 | tf_op jit(solution)/shard_map/ppermute | solution.py:117
  69.1 7.0 %copy-start.5 = (bf16[1,1,128,2048]{3,2,1,0:T(8,128)(2,1)S(1)}, bf16[1,1,128,2048]{3,2,1,0:T(8,128)(2,1)}, u32[]{:S(2)}) copy-start(bf16[1,1,128,2048]{3,2,1,0:T(8,128)(2,1)} %param.12) | copy-start | bytes 1572868
  69.5 2.4 %collective-permute-start.11 = (bf16[128,128]{1,0:T(8,128)(2,1)S(1)}, bf16[128,128]{1,0:T(8,128)(2,1)S(1)}, u32[]{:S(2)}, u32[]{:S(2)}) collective-permute-start(bf16[128,128]{1,0:T(8,128)(2,1)S(1)} %get-tuple-element.134), channel_id=1, source_target_pairs={{0,2},{2,0},{4,6},{6,4},{1,3},{3,1},{5,7},{7,5},{8,10},{10,8},{12,... | collective-permute-start | bytes 98312 | tf_op jit(solution)/shard_map/ppermute | solution.py:117
  70.5 9.3 %collective-permute-start.25 = (f32[2,2048]{1,0:T(2,128)S(1)}, f32[2,2048]{1,0:T(2,128)S(1)}, u32[]{:S(2)}, u32[]{:S(2)}) collective-permute-start(f32[2,2048]{1,0:T(2,128)S(1)} %fusion.168), channel_id=1, source_target_pairs={{0,1},{1,0},{2,3},{3,2},{4,5},{5,4},{6,7},{7,6},{8,9},{9,8},{10,11... | collective-permute-start | bytes 49160 | tf_op jit(solution)/shard_map/ppermute | solution.py:117
  71.9 4.2 %collective-permute-start.13 = (bf16[128,128]{1,0:T(8,128)(2,1)S(1)}, bf16[128,128]{1,0:T(8,128)(2,1)S(1)}, u32[]{:S(2)}, u32[]{:S(2)}) collective-permute-start(bf16[128,128]{1,0:T(8,128)(2,1)S(1)} %get-tuple-element.132), channel_id=1, source_target_pairs={{0,6},{2,4},{4,2},{6,0},{1,7},{3,5},{5,3},{7,1},{8,14},{10,12},{12... | collective-permute-start | bytes 98312 | tf_op jit(solution)/shard_map/ppermute | solution.py:117
  72.0 4.1 %collective-permute-start.12 = (bf16[128,128]{1,0:T(8,128)(2,1)S(1)}, bf16[128,128]{1,0:T(8,128)(2,1)S(1)}, u32[]{:S(2)}, u32[]{:S(2)}) collective-permute-start(bf16[128,128]{1,0:T(8,128)(2,1)S(1)} %get-tuple-element.133), channel_id=1, source_target_pairs={{0,4},{2,6},{4,0},{6,2},{1,5},{3,7},{5,1},{7,3},{8,12},{10,14},{12... | collective-permute-start | bytes 98312 | tf_op jit(solution)/shard_map/ppermute | solution.py:117
  79.2 20.0 %collective-permute-start.20 = (bf16[128,2048]{1,0:T(8,128)(2,1)S(1)}, bf16[128,2048]{1,0:T(8,128)(2,1)}, u32[]{:S(2)}, u32[]{:S(2)}) collective-permute-start(bf16[128,2048]{1,0:T(8,128)(2,1)S(1)} %fusion.2), channel_id=1, source_target_pairs={{0,8},{8,16},{16,24},{24,0},{1,9},{9,17},{17,25},{25,1},{2,10},{10... | collective-permute-start | bytes 1572872 | tf_op jit(solution)/shard_map/ppermute | solution.py:17
  86.9 14.9 %copy-start.10 = (bf16[128,2048]{1,0:T(8,128)(2,1)S(1)}, bf16[128,2048]{1,0:T(8,128)(2,1)}, u32[]{:S(2)}) copy-start(bf16[128,2048]{1,0:T(8,128)(2,1)} %copy-done.9) | copy-start | bytes 1572868
  (7 other events, 12.5 us)

commit v4 on v3

--- a/solution.py
+++ b/solution.py
@@ -233,9 +233,8 @@
         ).astype(jnp.bfloat16)
         for mask in range(count)
     ]
-    pairs, grad_proj, attended_b = lax.optimization_barrier(
-        (summed_on_chip(terms), grad_proj, attended_b)
-    )
+    terms, grad_proj, attended_b = lax.optimization_barrier((terms, grad_proj, attended_b))
+    pairs, normed_far = lax.optimization_barrier((summed_on_chip(terms), normed_far))
     grad_normed = pairs[0]
     for mask, pair in zip(range(2, count, 2), pairs[1:]):
         grad_normed = grad_normed + swapped(pair, "seq", mask).astype(jnp.float32)
@@ -279,7 +278,7 @@
 
     attended, kept = attend(queries, keys, values)
     back = returned(attended)
-    back, tan_normed = lax.optimization_barrier((back, tan_normed))
+    back, grad_normed, tan_normed = lax.optimization_barrier((back, grad_normed, tan_normed))
     tan_far = from_chips(tan_normed)
     result = (hidden + to_rows(back)).astype(jnp.bfloat16)
     next_input = passed_along(result, "section", 1)

time: 103 us -> 106 us (1.029)
  waiting for transfers between devices: 35.9 us -> 39.1 us
    ppermute x21, waiting for transfers between devices: 16.5 us -> 26.8 us  [swapped(): lax.ppermute(value, axis, [(source, source ^ mask) for source in range(co...]
    ppermute x5, waiting for transfers between devices: 19.4 us -> 12.3 us  [passed_along(): return lax.ppermute(value, axis, pairs)]
    ppermute x21, starting transfers between devices: 14.9 us -> 12.5 us  [swapped(): lax.ppermute(value, axis, [(source, source ^ mask) for source in range(co...]
    ppermute x5, starting transfers between devices: 6.54 us -> 8.15 us  [passed_along(): return lax.ppermute(value, axis, pairs)]
  transfers between devices with their start and end apart: 26 -> 26, of which waited for: 10 -> 9; matrix products, arithmetic and copies ran while one was open for 37% -> 36% of each run, Pallas kernels for 0% -> 0%
where the time goes in v4:
time: 106 us
  waiting for transfers between devices  39.1 us (37%)
  starting transfers between devices  20.6 us (19%)
  matrix products  19.7 us (19%)
  local copies, waits for them, and re-layouts  11.5 us (11%)
  other arithmetic  11.3 us (11%)
  between operations  3.47 us (3%)
    ppermute x21, waiting for transfers between devices, swapped(): lax.ppermute(value, axis, [(source, source ^ mask) for source in range(co...  26.8 us
    ppermute x21, starting transfers between devices, swapped(): lax.ppermute(value, axis, [(source, source ^ mask) for source in range(co...  12.5 us
    ppermute x5, waiting for transfers between devices, passed_along(): return lax.ppermute(value, axis, pairs)  12.3 us
    unnamed x30, local copies, waits for them, and re-layouts  9.45 us
    ppermute x5, starting transfers between devices, passed_along(): return lax.ppermute(value, axis, pairs)  8.15 us
    dot_general x4, matrix products, local(): jnp.einsum('td,hd->th', piece, output_head, preferred_element_type=jnp.fl...  3.92 us
    dot_general x8, matrix products, projected(): jnp.dot(piece, weight_heads, preferred_element_type=jnp.float32)  3.61 us
    dot_general x4, matrix products, local(): jnp.einsum('th,td->hd', piece, cot_pieces[mask], preferred_element_type=j...  3.53 us
  transfers between devices with their start and end apart: 26, of which 9 were waited for; matrix products, arithmetic and copies ran while one was open for 36% of the time, Pallas kernels for 0%

profile of v4, /device:TPU:0, one launch (start us, length us, event | category | flops | bytes accessed | tf_op | source)
XLA Modules:
  0.0 105.7 jit_solution(3092080374731693477)
XLA Ops:
  1.2 2.6 %collective-permute-start = (bf16[128,2048]{1,0:T(8,128)(2,1)}, bf16[128,2048]{1,0:T(8,128)(2,1)}, u32[]{:S(2)}, u32[]{:S(2)}) collective-permute-start(bf16[128,2048]{1,0:T(8,128)(2,1)} %bitcast.139), channel_id=1, source_target_pairs={{0,4},{2,6},{4,0},{6,2},{1,5},{3,7},{5,1},{7,3},{8,12},{10,14},{12... | collective-permute-start | bytes 1572872 | tf_op jit(solution)/shard_map/ppermute | solution.py:117
  7.2 1.1 %dynamic-slice_bitcast_fusion.3 = (bf16[128,384]{1,0:T(8,128)(2,1)S(1)}, bf16[128,384]{1,0:T(8,128)(2,1)S(1)}, bf16[128,384]{1,0:T(8,128)(2,1)S(1)}, bf16[128,384]{1,0:T(8,128)(2,1)S(1)}) fusion(bf16[1,1,512,1,384]{4,2,3,1,0:T(8,128)(2,1)} %param.16, s32[]{:T(128)S(6)} %select_n.16, s32[]{:T(128)S(6)} %select_n.17, s32[]{:T(128)S(6)} %select_n.19, ...), kind=kLoop, calls=%fused_computation.145 | loop fusion | bytes 786448 | tf_op jit(solution)/shard_map/dynamic_slice | solution.py:192
  8.7 1.5 %fusion.62 = (f32[128]{0:T(128)S(1)}, f32[128]{0:T(128)S(1)}) fusion(bf16[1,1,128,2048]{3,2,1,0:T(8,128)(2,1)} %param.12, bf16[1,1,128,2048]{3,2,1,0:T(8,128)(2,1)} %param.11), kind=kLoop, calls=%fused_computation.74 | loop fusion | flops 1572608 | bytes 1049600 | tf_op jit(solution)/shard_map/reduce_sum | solution.py:202
  10.2 0.7 multiply_add_fusion
  11.0 3.3 %fusion.58 = (bf16[128,2048]{1,0:T(8,128)(2,1)}, bf16[128,2048]{1,0:T(8,128)(2,1)}) fusion(bf16[1,1,128,2048]{3,2,1,0:T(8,128)(2,1)} %param.12, bf16[1,1,128,2048]{3,2,1,0:T(8,128)(2,1)} %param.11, f32[2048]{0:T(1024)S(1)} %bitcast.148, f32[128]{0:T(128)S(1)} %get-tuple-element.157, f32[2048]{0:T(1024)S(1)} %bitcast.147, f32[128]{0:T(128)S(1)} %get-tuple-element.158), kind=kLoop, calls=%fused_computation.70 | loop fusion | flops 3145728 | bytes 2114560 | tf_op jit(solution)/shard_map/convert_element_type | solution.py:207
  14.3 0.9 fusion.54
  15.8 0.8 collective-permute-done
  16.6 1.3 %convolution_convert_fusion.10 = bf16[128,128]{1,0:T(8,128)(2,1)S(1)} fusion(bf16[128,2048]{1,0:T(8,128)(2,1)} %collective-permute-done, bf16[1,4,128,2048]{3,2,1,0:T(8,128)(2,1)S(1)} %copy-done, s32[]{:T(128)S(6)} %select_n.20), kind=kOutput, calls=%fused_computation.63 | convolution fusion | flops 67125248 | bytes 1081348 | tf_op jit(solution)/shard_map/td,hd->th/dot_general | solution.py:214
  18.0 1.8 %collective-permute-start.6 = (bf16[128,2048]{1,0:T(8,128)(2,1)S(1)}, bf16[128,2048]{1,0:T(8,128)(2,1)S(1)}, u32[]{:S(2)}, u32[]{:S(2)}) collective-permute-start(bf16[128,2048]{1,0:T(8,128)(2,1)S(1)} %copy-done.8), channel_id=1, source_target_pairs={{0,4},{2,6},{4,0},{6,2},{1,5},{3,7},{5,1},{7,3},{8,12},{10,14},{12... | collective-permute-start | bytes 1572872 | tf_op jit(solution)/shard_map/ppermute | solution.py:117
  20.0 1.3 %fusion.55 = bf16[128,128]{1,0:T(8,128)(2,1)S(1)} fusion(bf16[128,2048]{1,0:T(8,128)(2,1)} %collective-permute-done.2, bf16[1,4,128,2048]{3,2,1,0:T(8,128)(2,1)S(1)} %copy-done, s32[]{:T(128)S(6)} %select_n.20), kind=kOutput, calls=%fused_computation.67 | convolution fusion | flops 67125248 | bytes 1081348 | tf_op jit(solution)/shard_map/td,hd->th/dot_general | solution.py:214
  27.7 1.4 %convolution_add_fusion.1 = f32[128,2048]{1,0:T(8,128)S(1)} fusion(f32[128,2048]{1,0:T(8,128)S(1)} %fusion.114, bf16[128,2048]{1,0:T(8,128)(2,1)} %collective-permute-done.2, bf16[512,128]{1,0:T(8,128)(2,1)S(1)} %convolution_convert_fusion.5), kind=kOutput, calls=%fused_computation.2 | convolution fusion | flops 67371008 | bytes 2654208 | tf_op jit(solution)/shard_map/th,td->hd/dot_general | solution.py:246
  29.1 1.5 %fusion = f32[128,2048]{1,0:T(8,128)S(1)} fusion(f32[128,2048]{1,0:T(8,128)S(1)} %fusion.110, f32[128,2048]{1,0:T(8,128)S(1)} %convolution_add_fusion.1, bf16[128,2048]{1,0:T(8,128)(2,1)} %collective-permute-done, bf16[512,128]{1,0:T(8,128)(2,1)S(1)} %convolution_convert_fusion.5), kind=kOutput, calls=%fused_computation.1 | convolution fusion | flops 67633152 | bytes 3702784 | tf_op jit(solution)/shard_map/th,td->hd/dot_general | solution.py:246
  30.7 1.6 %collective-permute-start.22 = (bf16[128,1024]{1,0:T(8,128)(2,1)S(1)}, bf16[128,1024]{1,0:T(8,128)(2,1)S(1)}, u32[]{:S(2)}, u32[]{:S(2)}) collective-permute-start(bf16[128,1024]{1,0:T(8,128)(2,1)S(1)} %dynamic-slice_convert_fusion.1), channel_id=1, source_target_pairs={{0,1},{1,0},{2,3},{3,2},{4,5},{5,4},{6,7},{7,6},{8,9},{9,8},{10,11... | collective-permute-start | bytes 786440 | tf_op jit(solution)/shard_map/ppermute | solution.py:17
  32.2 1.0 fusion.3
  34.8 5.1 %collective-permute-done.22 = bf16[128,1024]{1,0:T(8,128)(2,1)S(1)} collective-permute-done((bf16[128,1024]{1,0:T(8,128)(2,1)S(1)}, bf16[128,1024]{1,0:T(8,128)(2,1)S(1)}, u32[]{:S(2)}, u32[]{:S(2)}) %collective-permute-start.22) | collective-permute-done | bytes 262176 | tf_op jit(solution)/shard_map/ppermute | solution.py:17
  39.9 0.9 add_bitcast_fusion
  43.0 1.8 %collective-permute-start.9 = (bf16[128,128]{1,0:T(8,128)(2,1)S(1)}, bf16[128,128]{1,0:T(8,128)(2,1)S(1)}, u32[]{:S(2)}, u32[]{:S(2)}) collective-permute-start(bf16[128,128]{1,0:T(8,128)(2,1)S(1)} %get-tuple-element.149), channel_id=1, source_target_pairs={{0,4},{2,6},{4,0},{6,2},{1,5},{3,7},{5,1},{7,3},{8,12},{10,14},{12... | collective-permute-start | bytes 98312 | tf_op jit(solution)/shard_map/ppermute | solution.py:117
  44.9 9.2 %collective-permute-done.11 = bf16[128,2048]{1,0:T(8,128)(2,1)S(1)} collective-permute-done((bf16[128,2048]{1,0:T(8,128)(2,1)S(1)}, bf16[128,2048]{1,0:T(8,128)(2,1)S(1)}, u32[]{:S(2)}, u32[]{:S(2)}) %collective-permute-start.11) | collective-permute-done | bytes 524320 | tf_op jit(solution)/shard_map/ppermute | solution.py:117
  56.0 1.7 %collective-permute-start.12 = (bf16[128,2048]{1,0:T(8,128)(2,1)S(1)}, bf16[128,2048]{1,0:T(8,128)(2,1)}, u32[]{:S(2)}, u32[]{:S(2)}) collective-permute-start(bf16[128,2048]{1,0:T(8,128)(2,1)S(1)} %fusion.1), channel_id=1, source_target_pairs={{0,8},{8,16},{16,24},{24,0},{1,9},{9,17},{17,25},{25,1},{2,10},{10... | collective-permute-start | bytes 1572872 | tf_op jit(solution)/shard_map/ppermute | solution.py:17
  59.3 2.7 %collective-permute-start.19 = (bf16[128,2048]{1,0:T(8,128)(2,1)S(1)}, bf16[128,2048]{1,0:T(8,128)(2,1)S(1)}, u32[]{:S(2)}, u32[]{:S(2)}) collective-permute-start(bf16[128,2048]{1,0:T(8,128)(2,1)S(1)} %add_convert_fusion), channel_id=1, source_target_pairs={{0,24},{8,0},{16,8},{24,16},{1,25},{9,1},{17,9},{25,17},{2,26},{10... | collective-permute-start | bytes 1572872 | tf_op jit(solution)/shard_map/ppermute | solution.py:17
  62.0 9.7 %collective-permute-done.14 = bf16[128,2048]{1,0:T(8,128)(2,1)S(1)} collective-permute-done((bf16[128,2048]{1,0:T(8,128)(2,1)S(1)}, bf16[128,2048]{1,0:T(8,128)(2,1)S(1)}, u32[]{:S(2)}, u32[]{:S(2)}) %collective-permute-start.14) | collective-permute-done | bytes 524320 | tf_op jit(solution)/shard_map/ppermute | solution.py:117
  76.1 1.6 %collective-permute-start.25 = (f32[2,2048]{1,0:T(2,128)S(1)}, f32[2,2048]{1,0:T(2,128)S(1)}, u32[]{:S(2)}, u32[]{:S(2)}) collective-permute-start(f32[2,2048]{1,0:T(2,128)S(1)} %fusion.158), channel_id=1, source_target_pairs={{0,1},{1,0},{2,3},{3,2},{4,5},{5,4},{6,7},{7,6},{8,9},{9,8},{10,11... | collective-permute-start | bytes 49160 | tf_op jit(solution)/shard_map/ppermute | solution.py:117
  77.6 1.2 %collective-permute-start.17 = (bf16[128,128]{1,0:T(8,128)(2,1)S(1)}, bf16[128,128]{1,0:T(8,128)(2,1)S(1)}, u32[]{:S(2)}, u32[]{:S(2)}) collective-permute-start(bf16[128,128]{1,0:T(8,128)(2,1)S(1)} %get-tuple-element.145), channel_id=1, source_target_pairs={{0,4},{2,6},{4,0},{6,2},{1,5},{3,7},{5,1},{7,3},{8,12},{10,14},{12... | collective-permute-start | bytes 98312 | tf_op jit(solution)/shard_map/ppermute | solution.py:117
  78.9 2.7 %collective-permute-done.17 = bf16[128,128]{1,0:T(8,128)(2,1)S(1)} collective-permute-done((bf16[128,128]{1,0:T(8,128)(2,1)S(1)}, bf16[128,128]{1,0:T(8,128)(2,1)S(1)}, u32[]{:S(2)}, u32[]{:S(2)}) %collective-permute-start.17) | collective-permute-done | bytes 32800 | tf_op jit(solution)/shard_map/ppermute | solution.py:117
  81.6 3.4 %collective-permute-done.18 = bf16[128,128]{1,0:T(8,128)(2,1)S(1)} collective-permute-done((bf16[128,128]{1,0:T(8,128)(2,1)S(1)}, bf16[128,128]{1,0:T(8,128)(2,1)S(1)}, u32[]{:S(2)}, u32[]{:S(2)}) %collective-permute-start.18) | collective-permute-done | bytes 32800 | tf_op jit(solution)/shard_map/ppermute | solution.py:117
  85.5 1.6 %collective-permute-start.20 = (bf16[128,2048]{1,0:T(8,128)(2,1)S(1)}, bf16[128,2048]{1,0:T(8,128)(2,1)}, u32[]{:S(2)}, u32[]{:S(2)}) collective-permute-start(bf16[128,2048]{1,0:T(8,128)(2,1)S(1)} %fusion.2), channel_id=1, source_target_pairs={{0,8},{8,16},{16,24},{24,0},{1,9},{9,17},{17,25},{25,1},{2,10},{10... | collective-permute-start | bytes 1572872 | tf_op jit(solution)/shard_map/ppermute | solution.py:17
  87.1 1.4 %fusion.5 = f32[1,1024,1,384]{1,3,2,0:T(8,128)} fusion(bf16[1024,384]{0,1:T(8,128)(2,1)S(1)} %collective-permute-done.21, f32[384,2048]{1,0:T(8,128)S(1)} %fusion.3, s32[]{:T(128)S(6)} %select_n.21), kind=kLoop, calls=%fused_computation.18 | loop fusion | flops 786432 | bytes 3932164 | tf_op jit(solution)/shard_map/broadcast_in_dim | solution.py:315
  88.5 4.8 %copy.17 = f32[1,1024,1,384]{3,2,1,0:T(1,128)} copy(f32[1,1024,1,384]{1,3,2,0:T(8,128)} %fusion.5) | data formatting | bytes 3145728
  94.0 7.2 %collective-permute-done.20 = bf16[128,2048]{1,0:T(8,128)(2,1)} collective-permute-done((bf16[128,2048]{1,0:T(8,128)(2,1)S(1)}, bf16[128,2048]{1,0:T(8,128)(2,1)}, u32[]{:S(2)}, u32[]{:S(2)}) %collective-permute-start.20) | collective-permute-done | bytes 524320 | tf_op jit(solution)/shard_map/ppermute | solution.py:17
  101.2 1.9 %copy.29 = bf16[1,1,128,2048]{3,2,1,0:T(8,128)(2,1)} copy(bf16[1,1,128,2048]{3,2,1,0:T(8,128)(2,1)} %bitcast.18) | data formatting | bytes 1048576
  103.0 1.9 %copy.30 = bf16[1,1,128,2048]{3,2,1,0:T(8,128)(2,1)} copy(bf16[1,1,128,2048]{3,2,1,0:T(8,128)(2,1)} %bitcast.23) | data formatting | bytes 1048576
  104.9 0.8 copy.31
  (126 shorter events, 21.9 us)
Async XLA Ops:
  0.6 13.7 %copy-start = (bf16[1,4,128,2048]{3,2,1,0:T(8,128)(2,1)S(1)}, bf16[1,4,128,2048]{3,2,1,0:T(8,128)(2,1)}, u32[]{:S(2)}) copy-start(bf16[1,4,128,2048]{3,2,1,0:T(8,128)(2,1)} %param.19) | copy-start | bytes 6291460
  0.6 19.4 %collective-permute-start.2 = (bf16[128,2048]{1,0:T(8,128)(2,1)}, bf16[128,2048]{1,0:T(8,128)(2,1)}, u32[]{:S(2)}, u32[]{:S(2)}) collective-permute-start(bf16[128,2048]{1,0:T(8,128)(2,1)} %bitcast.138), channel_id=1, source_target_pairs={{0,2},{2,0},{4,6},{6,4},{1,3},{3,1},{5,7},{7,5},{8,10},{10,8},{12,... | collective-permute-start | bytes 1572872 | tf_op jit(solution)/shard_map/ppermute | solution.py:117
  1.2 15.4 %collective-permute-start = (bf16[128,2048]{1,0:T(8,128)(2,1)}, bf16[128,2048]{1,0:T(8,128)(2,1)}, u32[]{:S(2)}, u32[]{:S(2)}) collective-permute-start(bf16[128,2048]{1,0:T(8,128)(2,1)} %bitcast.139), channel_id=1, source_target_pairs={{0,4},{2,6},{4,0},{6,2},{1,5},{3,7},{5,1},{7,3},{8,12},{10,14},{12... | collective-permute-start | bytes 1572872 | tf_op jit(solution)/shard_map/ppermute | solution.py:117
  8.6 5.6 %copy-start.4 = (bf16[1,1,128,2048]{3,2,1,0:T(8,128)(2,1)S(1)}, bf16[1,1,128,2048]{3,2,1,0:T(8,128)(2,1)}, u32[]{:S(2)}) copy-start(bf16[1,1,128,2048]{3,2,1,0:T(8,128)(2,1)} %param.13) | copy-start | bytes 1572868
  15.8 5.6 %copy-start.1 = (bf16[1,2048,1,384]{3,1,2,0:T(8,128)(2,1)S(1)}, bf16[1,2048,1,384]{3,1,2,0:T(8,128)(2,1)}, u32[]{:S(2)}) copy-start(bf16[1,2048,1,384]{3,1,2,0:T(8,128)(2,1)} %param.18) | copy-start | bytes 4718596
  16.6 5.2 %collective-permute-start.3 = (bf16[128,2048]{1,0:T(8,128)(2,1)}, bf16[128,2048]{1,0:T(8,128)(2,1)S(1)}, u32[]{:S(2)}, u32[]{:S(2)}) collective-permute-start(bf16[128,2048]{1,0:T(8,128)(2,1)} %collective-permute-done), channel_id=1, source_target_pairs={{0,2},{2,0},{4,6},{6,4},{1,3},{3,1},{5,7},{7,5},{8,10},{10,8},{12,... | collective-permute-start | bytes 1572872 | tf_op jit(solution)/shard_map/ppermute | solution.py:117
  18.0 16.3 %collective-permute-start.6 = (bf16[128,2048]{1,0:T(8,128)(2,1)S(1)}, bf16[128,2048]{1,0:T(8,128)(2,1)S(1)}, u32[]{:S(2)}, u32[]{:S(2)}) collective-permute-start(bf16[128,2048]{1,0:T(8,128)(2,1)S(1)} %copy-done.8), channel_id=1, source_target_pairs={{0,4},{2,6},{4,0},{6,2},{1,5},{3,7},{5,1},{7,3},{8,12},{10,14},{12... | collective-permute-start | bytes 1572872 | tf_op jit(solution)/shard_map/ppermute | solution.py:117
  19.8 14.6 %collective-permute-start.1 = (bf16[128,2048]{1,0:T(8,128)(2,1)S(1)}, bf16[128,2048]{1,0:T(8,128)(2,1)S(1)}, u32[]{:S(2)}, u32[]{:S(2)}) collective-permute-start(bf16[128,2048]{1,0:T(8,128)(2,1)S(1)} %copy-done.8), channel_id=1, source_target_pairs={{0,2},{2,0},{4,6},{6,4},{1,3},{3,1},{5,7},{7,5},{8,10},{10,8},{12,... | collective-permute-start | bytes 1572872 | tf_op jit(solution)/shard_map/ppermute | solution.py:117
  26.5 7.6 %collective-permute-start.4 = (bf16[128,2048]{1,0:T(8,128)(2,1)S(1)}, bf16[128,2048]{1,0:T(8,128)(2,1)S(1)}, u32[]{:S(2)}, u32[]{:S(2)}) collective-permute-start(bf16[128,2048]{1,0:T(8,128)(2,1)S(1)} %convolution_convert_fusion.2), channel_id=1, source_target_pairs={{0,2},{2,0},{4,6},{6,4},{1,3},{3,1},{5,7},{7,5},{8,10},{10,8},{12,... | collective-permute-start | bytes 1572872 | tf_op jit(solution)/shard_map/ppermute | solution.py:117
  26.8 6.5 %collective-permute-start.5 = (bf16[128,2048]{1,0:T(8,128)(2,1)S(1)}, bf16[128,2048]{1,0:T(8,128)(2,1)S(1)}, u32[]{:S(2)}, u32[]{:S(2)}) collective-permute-start(bf16[128,2048]{1,0:T(8,128)(2,1)S(1)} %convolution_convert_fusion), channel_id=1, source_target_pairs={{0,2},{2,0},{4,6},{6,4},{1,3},{3,1},{5,7},{7,5},{8,10},{10,8},{12,... | collective-permute-start | bytes 1572872 | tf_op jit(solution)/shard_map/ppermute | solution.py:117
  29.1 3.1 %copy-start.6 = (bf16[1,1,512,2048]{3,2,1,0:T(8,128)(2,1)S(1)}, bf16[1,1,512,2048]{3,2,1,0:T(8,128)(2,1)}, u32[]{:S(2)}) copy-start(bf16[1,1,512,2048]{3,2,1,0:T(8,128)(2,1)} %param.14) | copy-start | bytes 6291460
  30.7 9.2 %collective-permute-start.22 = (bf16[128,1024]{1,0:T(8,128)(2,1)S(1)}, bf16[128,1024]{1,0:T(8,128)(2,1)S(1)}, u32[]{:S(2)}, u32[]{:S(2)}) collective-permute-start(bf16[128,1024]{1,0:T(8,128)(2,1)S(1)} %dynamic-slice_convert_fusion.1), channel_id=1, source_target_pairs={{0,1},{1,0},{2,3},{3,2},{4,5},{5,4},{6,7},{7,6},{8,9},{9,8},{10,11... | collective-permute-start | bytes 786440 | tf_op jit(solution)/shard_map/ppermute | solution.py:17
  33.4 53.8 %collective-permute-start.21 = (bf16[1024,384]{0,1:T(8,128)(2,1)S(1)}, bf16[1024,384]{0,1:T(8,128)(2,1)S(1)}, u32[]{:S(2)}, u32[]{:S(2)}) collective-permute-start(bf16[1024,384]{0,1:T(8,128)(2,1)S(1)} %fusion.67), channel_id=1, source_target_pairs={{0,1},{1,0},{2,3},{3,2},{4,5},{5,4},{6,7},{7,6},{8,9},{9,8},{10,11... | collective-permute-start | bytes 2359304 | tf_op jit(solution)/shard_map/ppermute | solution.py:17
  34.3 7.3 %collective-permute-start.7 = (bf16[128,2048]{1,0:T(8,128)(2,1)S(1)}, bf16[128,2048]{1,0:T(8,128)(2,1)S(1)}, u32[]{:S(2)}, u32[]{:S(2)}) collective-permute-start(bf16[128,2048]{1,0:T(8,128)(2,1)S(1)} %collective-permute-done.6), channel_id=1, source_target_pairs={{0,2},{2,0},{4,6},{6,4},{1,3},{3,1},{5,7},{7,5},{8,10},{10,8},{12,... | collective-permute-start | bytes 1572872 | tf_op jit(solution)/shard_map/ppermute | solution.py:117
  40.7 13.3 %collective-permute-start.11 = (bf16[128,2048]{1,0:T(8,128)(2,1)S(1)}, bf16[128,2048]{1,0:T(8,128)(2,1)S(1)}, u32[]{:S(2)}, u32[]{:S(2)}) collective-permute-start(bf16[128,2048]{1,0:T(8,128)(2,1)S(1)} %add_convert_fusion.1), channel_id=1, source_target_pairs={{0,4},{2,6},{4,0},{6,2},{1,5},{3,7},{5,1},{7,3},{8,12},{10,14},{12... | collective-permute-start | bytes 1572872 | tf_op jit(solution)/shard_map/ppermute | solution.py:117
  43.0 11.2 %collective-permute-start.10 = (bf16[128,128]{1,0:T(8,128)(2,1)S(1)}, bf16[128,128]{1,0:T(8,128)(2,1)S(1)}, u32[]{:S(2)}, u32[]{:S(2)}) collective-permute-start(bf16[128,128]{1,0:T(8,128)(2,1)S(1)} %get-tuple-element.148), channel_id=1, source_target_pairs={{0,6},{2,4},{4,2},{6,0},{1,7},{3,5},{5,3},{7,1},{8,14},{10,12},{12... | collective-permute-start | bytes 98312 | tf_op jit(solution)/shard_map/ppermute | solution.py:117
  43.0 11.7 %collective-permute-start.9 = (bf16[128,128]{1,0:T(8,128)(2,1)S(1)}, bf16[128,128]{1,0:T(8,128)(2,1)S(1)}, u32[]{:S(2)}, u32[]{:S(2)}) collective-permute-start(bf16[128,128]{1,0:T(8,128)(2,1)S(1)} %get-tuple-element.149), channel_id=1, source_target_pairs={{0,4},{2,6},{4,0},{6,2},{1,5},{3,7},{5,1},{7,3},{8,12},{10,14},{12... | collective-permute-start | bytes 98312 | tf_op jit(solution)/shard_map/ppermute | solution.py:117
  44.8 10.0 %collective-permute-start.8 = (bf16[128,128]{1,0:T(8,128)(2,1)S(1)}, bf16[128,128]{1,0:T(8,128)(2,1)S(1)}, u32[]{:S(2)}, u32[]{:S(2)}) collective-permute-start(bf16[128,128]{1,0:T(8,128)(2,1)S(1)} %get-tuple-element.150), channel_id=1, source_target_pairs={{0,2},{2,0},{4,6},{6,4},{1,3},{3,1},{5,7},{7,5},{8,10},{10,8},{12,... | collective-permute-start | bytes 98312 | tf_op jit(solution)/shard_map/ppermute | solution.py:117
  55.2 4.1 %collective-permute-start.23 = (f32[2,2048]{1,0:T(2,128)S(1)}, f32[2,2048]{1,0:T(2,128)S(1)}, u32[]{:S(2)}, u32[]{:S(2)}) collective-permute-start(f32[2,2048]{1,0:T(2,128)S(1)} %pad_maximum_fusion.7), channel_id=1, source_target_pairs={{0,2},{2,0},{4,6},{6,4},{1,3},{3,1},{5,7},{7,5},{8,10},{10,8},{12,... | collective-permute-start | bytes 49160 | tf_op jit(solution)/shard_map/ppermute | solution.py:117
  56.0 37.9 %collective-permute-start.12 = (bf16[128,2048]{1,0:T(8,128)(2,1)S(1)}, bf16[128,2048]{1,0:T(8,128)(2,1)}, u32[]{:S(2)}, u32[]{:S(2)}) collective-permute-start(bf16[128,2048]{1,0:T(8,128)(2,1)S(1)} %fusion.1), channel_id=1, source_target_pairs={{0,8},{8,16},{16,24},{24,0},{1,9},{9,17},{17,25},{25,1},{2,10},{10... | collective-permute-start | bytes 1572872 | tf_op jit(solution)/shard_map/ppermute | solution.py:17
  57.7 14.0 %collective-permute-start.14 = (bf16[128,2048]{1,0:T(8,128)(2,1)S(1)}, bf16[128,2048]{1,0:T(8,128)(2,1)S(1)}, u32[]{:S(2)}, u32[]{:S(2)}) collective-permute-start(bf16[128,2048]{1,0:T(8,128)(2,1)S(1)} %copy-done.7), channel_id=1, source_target_pairs={{0,4},{2,6},{4,0},{6,2},{1,5},{3,7},{5,1},{7,3},{8,12},{10,14},{12... | collective-permute-start | bytes 1572872 | tf_op jit(solution)/shard_map/ppermute | solution.py:117
  59.2 13.1 %collective-permute-start.13 = (bf16[128,2048]{1,0:T(8,128)(2,1)S(1)}, bf16[128,2048]{1,0:T(8,128)(2,1)S(1)}, u32[]{:S(2)}, u32[]{:S(2)}) collective-permute-start(bf16[128,2048]{1,0:T(8,128)(2,1)S(1)} %copy-done.7), channel_id=1, source_target_pairs={{0,2},{2,0},{4,6},{6,4},{1,3},{3,1},{5,7},{7,5},{8,10},{10,8},{12,... | collective-permute-start | bytes 1572872 | tf_op jit(solution)/shard_map/ppermute | solution.py:117
  59.3 26.2 %collective-permute-start.19 = (bf16[128,2048]{1,0:T(8,128)(2,1)S(1)}, bf16[128,2048]{1,0:T(8,128)(2,1)S(1)}, u32[]{:S(2)}, u32[]{:S(2)}) collective-permute-start(bf16[128,2048]{1,0:T(8,128)(2,1)S(1)} %add_convert_fusion), channel_id=1, source_target_pairs={{0,24},{8,0},{16,8},{24,16},{1,25},{9,1},{17,9},{25,17},{2,26},{10... | collective-permute-start | bytes 1572872 | tf_op jit(solution)/shard_map/ppermute | solution.py:17
  71.8 1.9 %collective-permute-start.15 = (bf16[128,2048]{1,0:T(8,128)(2,1)S(1)}, bf16[128,2048]{1,0:T(8,128)(2,1)S(1)}, u32[]{:S(2)}, u32[]{:S(2)}) collective-permute-start(bf16[128,2048]{1,0:T(8,128)(2,1)S(1)} %collective-permute-done.14), channel_id=1, source_target_pairs={{0,2},{2,0},{4,6},{6,4},{1,3},{3,1},{5,7},{7,5},{8,10},{10,8},{12,... | collective-permute-start | bytes 1572872 | tf_op jit(solution)/shard_map/ppermute | solution.py:117
  72.2 3.8 %collective-permute-start.24 = (f32[2,2048]{1,0:T(2,128)S(1)}, f32[2,2048]{1,0:T(2,128)S(1)}, u32[]{:S(2)}, u32[]{:S(2)}) collective-permute-start(f32[2,2048]{1,0:T(2,128)S(1)} %fusion.127), channel_id=1, source_target_pairs={{0,4},{2,6},{4,0},{6,2},{1,5},{3,7},{5,1},{7,3},{8,12},{10,14},{12... | collective-permute-start | bytes 49160 | tf_op jit(solution)/shard_map/ppermute | solution.py:117
  75.4 9.6 %copy-start.3 = (bf16[1,1,128,2048]{3,2,1,0:T(8,128)(2,1)S(1)}, bf16[1,1,128,2048]{3,2,1,0:T(8,128)(2,1)}, u32[]{:S(2)}) copy-start(bf16[1,1,128,2048]{3,2,1,0:T(8,128)(2,1)} %param.12) | copy-start | bytes 1572868
  75.8 1.8 %collective-permute-start.16 = (bf16[128,128]{1,0:T(8,128)(2,1)S(1)}, bf16[128,128]{1,0:T(8,128)(2,1)S(1)}, u32[]{:S(2)}, u32[]{:S(2)}) collective-permute-start(bf16[128,128]{1,0:T(8,128)(2,1)S(1)} %get-tuple-element.146), channel_id=1, source_target_pairs={{0,2},{2,0},{4,6},{6,4},{1,3},{3,1},{5,7},{7,5},{8,10},{10,8},{12,... | collective-permute-start | bytes 98312 | tf_op jit(solution)/shard_map/ppermute | solution.py:117
  76.1 17.3 %collective-permute-start.25 = (f32[2,2048]{1,0:T(2,128)S(1)}, f32[2,2048]{1,0:T(2,128)S(1)}, u32[]{:S(2)}, u32[]{:S(2)}) collective-permute-start(f32[2,2048]{1,0:T(2,128)S(1)} %fusion.158), channel_id=1, source_target_pairs={{0,1},{1,0},{2,3},{3,2},{4,5},{5,4},{6,7},{7,6},{8,9},{9,8},{10,11... | collective-permute-start | bytes 49160 | tf_op jit(solution)/shard_map/ppermute | solution.py:117
  77.6 3.9 %collective-permute-start.17 = (bf16[128,128]{1,0:T(8,128)(2,1)S(1)}, bf16[128,128]{1,0:T(8,128)(2,1)S(1)}, u32[]{:S(2)}, u32[]{:S(2)}) collective-permute-start(bf16[128,128]{1,0:T(8,128)(2,1)S(1)} %get-tuple-element.145), channel_id=1, source_target_pairs={{0,4},{2,6},{4,0},{6,2},{1,5},{3,7},{5,1},{7,3},{8,12},{10,14},{12... | collective-permute-start | bytes 98312 | tf_op jit(solution)/shard_map/ppermute | solution.py:117
  81.6 3.5 %collective-permute-start.18 = (bf16[128,128]{1,0:T(8,128)(2,1)S(1)}, bf16[128,128]{1,0:T(8,128)(2,1)S(1)}, u32[]{:S(2)}, u32[]{:S(2)}) collective-permute-start(bf16[128,128]{1,0:T(8,128)(2,1)S(1)} %get-tuple-element.144), channel_id=1, source_target_pairs={{0,6},{2,4},{4,2},{6,0},{1,7},{3,5},{5,3},{7,1},{8,14},{10,12},{12... | collective-permute-start | bytes 98312 | tf_op jit(solution)/shard_map/ppermute | solution.py:117
  85.5 15.7 %collective-permute-start.20 = (bf16[128,2048]{1,0:T(8,128)(2,1)S(1)}, bf16[128,2048]{1,0:T(8,128)(2,1)}, u32[]{:S(2)}, u32[]{:S(2)}) collective-permute-start(bf16[128,2048]{1,0:T(8,128)(2,1)S(1)} %fusion.2), channel_id=1, source_target_pairs={{0,8},{8,16},{16,24},{24,0},{1,9},{9,17},{17,25},{25,1},{2,10},{10... | collective-permute-start | bytes 1572872 | tf_op jit(solution)/shard_map/ppermute | solution.py:17
  93.3 11.6 %copy-start.10 = (bf16[128,2048]{1,0:T(8,128)(2,1)S(1)}, bf16[128,2048]{1,0:T(8,128)(2,1)}, u32[]{:S(2)}) copy-start(bf16[128,2048]{1,0:T(8,128)(2,1)} %copy-done.9) | copy-start | bytes 1572868
  (7 other events, 12.4 us)
